TPU v7x, 128 devices: a whole 4x4x4 slice. The times are simulated.
128 devices in a mesh: ctx: 16 (over z, x), fsdp: 8 (over y, core).
Axes of the slice: x: 4, y: 4, z: 4, core: 2. Of those that a mesh axis runs over, the one named last changes fastest.
Arguments:
- tokens: bfloat16 [8, 2048, 768], P('fsdp', 'ctx'), may hold values from -6 to 6
- cotangent: bfloat16 [8, 2048, 768], P('fsdp', 'ctx'), may hold values from -6 to 6
- pair_order: int32 [16], replicated, may hold values from 0 to 15, each once
- first_gain: bfloat16 [768], P('fsdp'), may hold values from 0.5 to 1.5
- first_shift: bfloat16 [768], P('fsdp'), may hold values from -1.5 to 1.5
- qkv_weight: bfloat16 [768, 2304], P('fsdp'), may hold values from -0.3125 to 0.3125
- qv_bias: bfloat16 [1536], P('fsdp'), may hold values from -2.5 to 2.5
- out_weight: bfloat16 [768, 768], P('fsdp'), may hold values from -0.625 to 0.625
- out_bias: bfloat16 [768], P('fsdp'), may hold values from -1.5 to 1.5
- second_gain: bfloat16 [768], P('fsdp'), may hold values from 0.5 to 1.5
- second_shift: bfloat16 [768], P('fsdp'), may hold values from -1.5 to 1.5
- up_weight: bfloat16 [768, 3072], P('fsdp'), may hold values from -0.21875 to 0.21875
- up_bias: bfloat16 [3072], P('fsdp'), may hold values from -2.5 to 2.5
- down_weight: bfloat16 [3072, 768], P('fsdp'), may hold values from -0.15625 to 0.15625
- down_bias: bfloat16 [768], P('fsdp'), may hold values from -1.5 to 1.5
Outputs:
- mixed: bfloat16 [8, 2048, 768], P('fsdp', 'ctx')
- tokens_grad: float32 [8, 2048, 768], P('fsdp', 'ctx')
- first_gain_grad: float32 [768], P('fsdp')
- first_shift_grad: float32 [768], P('fsdp')
- qkv_weight_grad: float32 [768, 2304], P('fsdp')
- qv_bias_grad: float32 [1536], P('fsdp')
- out_weight_grad: float32 [768, 768], P('fsdp')
- out_bias_grad: float32 [768], P('fsdp')
- second_gain_grad: float32 [768], P('fsdp')
- second_shift_grad: float32 [768], P('fsdp')
- up_weight_grad: float32 [768, 3072], P('fsdp')
- up_bias_grad: float32 [3072], P('fsdp')
- down_weight_grad: float32 [3072, 768], P('fsdp')
- down_bias_grad: float32 [768], P('fsdp')
Inputs may be any that keep to these rules, and one draw needn't show every extreme that they name: A permutation of 0 to 15; the blocks at stored block pair i are position blocks pair_order[i] and 31 - pair_order[i].
All inputs are finite; a program needn't handle non-finite values.
Results may differ from a plain program's by a relative error of at most 0.025.
Values may be sent and summed in bfloat16 or wider, within the bound.
No kernel may reach another device: no remote copies, remote signals or barrier semaphores. Data moves between devices by JAX's collectives and lax.ppermute only.
A program may use at most 128 MiB of HBM per device.

v0:
```python
import jax
import jax.numpy as jnp
from jax import lax
from jax.sharding import PartitionSpec as P

HEADS = 12


EPSILON = 1e-05
NEGATIVE = -1e30


def layer_norm(values, scale_row, shift_row):
    center = values - jnp.mean(values, axis=-1, keepdims=True)
    spread = jnp.mean(center * center, axis=-1, keepdims=True)
    return center * lax.rsqrt(spread + EPSILON) * scale_row + shift_row


def gelu_tanh(values):
    return jax.nn.gelu(values, approximate=True)


def positions_of(pair_order, row_count):
    pair_count = pair_order.shape[0]
    half_rows = row_count // 2
    stored = jnp.arange(pair_count * row_count, dtype=jnp.int32)
    device_of = stored // row_count
    inside = stored % row_count
    chosen = jnp.sum(
        jnp.where(
            device_of[:, None] == jnp.arange(pair_count, dtype=jnp.int32)[None, :],
            pair_order[None, :],
            0,
        ),
        axis=1,
    )
    block_of = jnp.where(inside < half_rows, chosen, 2 * pair_count - 1 - chosen)
    return block_of * half_rows + inside % half_rows


def transposed_product(left, right):
    return lax.dot_general(
        left, right, (((0,), (0,)), ((), ())), preferred_element_type=jnp.float32
    )


def times_transposed(left, right):
    return lax.dot_general(
        left, right, (((1,), (1,)), ((), ())), preferred_element_type=jnp.float32
    )


def scores_of(queries, query_places, key_block, key_places):
    scaling = queries.shape[2] ** (-0.5)
    scores = (
        jnp.einsum("qhe,khe->qhk", queries, key_block, preferred_element_type=jnp.float32) * scaling
    )
    allowed = key_places[None, None, :] <= query_places[:, None, None]
    return (scores, allowed)


def probs_of(queries, query_places, key_block, key_places, row_top, row_total):
    scores, allowed = scores_of(queries, query_places, key_block, key_places)
    return jnp.where(allowed, jnp.exp(scores - row_top[:, :, None]) / row_total[:, :, None], 0.0)


def score_grads(
    queries,
    query_places,
    upstream,
    key_block,
    value_block,
    key_places,
    row_top,
    row_total,
    row_delta,
):
    probs = probs_of(queries, query_places, key_block, key_places, row_top, row_total)
    slopes = jnp.einsum("qhe,khe->qhk", upstream, value_block, preferred_element_type=jnp.float32)
    scaling = queries.shape[2] ** (-0.5)
    grad_scores = (scaling * probs * (slopes - row_delta[:, :, None])).astype(jnp.bfloat16)
    return (probs.astype(jnp.bfloat16), grad_scores)


def local(
    tokens,
    cotangent,
    pair_order,
    first_gain,
    first_shift,
    qkv_weight,
    qv_bias,
    out_weight,
    out_bias,
    second_gain,
    second_shift,
    up_weight,
    up_bias,
    down_weight,
    down_bias,
):
    local_params = (
        first_gain,
        first_shift,
        qkv_weight,
        qv_bias,
        out_weight,
        out_bias,
        second_gain,
        second_shift,
        up_weight,
        up_bias,
        down_weight,
        down_bias,
    )
    gathered = (
        lax.all_gather(local_params[0], "fsdp", axis=0, tiled=True),
        lax.all_gather(local_params[1], "fsdp", axis=0, tiled=True),
        lax.all_gather(local_params[2], "fsdp", axis=0, tiled=True),
        lax.all_gather(local_params[3], "fsdp", axis=0, tiled=True),
        lax.all_gather(local_params[4], "fsdp", axis=0, tiled=True),
        lax.all_gather(local_params[5], "fsdp", axis=0, tiled=True),
        lax.all_gather(local_params[6], "fsdp", axis=0, tiled=True),
        lax.all_gather(local_params[7], "fsdp", axis=0, tiled=True),
        lax.all_gather(local_params[8], "fsdp", axis=0, tiled=True),
        lax.all_gather(local_params[9], "fsdp", axis=0, tiled=True),
        lax.all_gather(local_params[10], "fsdp", axis=0, tiled=True),
        lax.all_gather(local_params[11], "fsdp", axis=0, tiled=True),
    )
    (
        gain_one,
        shift_one,
        w_qkv,
        b_qv,
        w_out,
        b_out,
        gain_two,
        shift_two,
        w_up,
        b_up,
        w_down,
        b_down,
    ) = gathered
    gain_one = gain_one.astype(jnp.float32)
    shift_one = shift_one.astype(jnp.float32)
    b_qv = b_qv.astype(jnp.float32)
    b_out = b_out.astype(jnp.float32)
    gain_two = gain_two.astype(jnp.float32)
    shift_two = shift_two.astype(jnp.float32)
    b_up = b_up.astype(jnp.float32)
    b_down = b_down.astype(jnp.float32)
    row_count = tokens.shape[1]
    model_width = tokens.shape[2]
    head_count = HEADS
    head_depth = model_width // head_count
    total_rows = row_count * lax.axis_size("ctx")
    block_size = min(512, total_rows)
    block_count = total_rows // block_size
    key_places = positions_of(pair_order, row_count)
    query_places = lax.dynamic_slice_in_dim(
        key_places, lax.axis_index("ctx") * row_count, row_count
    )
    inputs = tokens[0].astype(jnp.float32)
    normed_one, back_one = jax.vjp(layer_norm, inputs, gain_one, shift_one)
    normed_one = normed_one.astype(jnp.bfloat16)
    projected = jnp.dot(normed_one, w_qkv, preferred_element_type=jnp.float32)
    query_bf = (
        (projected[:, :model_width] + b_qv[:model_width])
        .astype(jnp.bfloat16)
        .reshape(row_count, head_count, head_depth)
    )
    key_bf = (
        projected[:, model_width : 2 * model_width]
        .astype(jnp.bfloat16)
        .reshape(row_count, head_count, head_depth)
    )
    value_bf = (
        (projected[:, 2 * model_width :] + b_qv[model_width:])
        .astype(jnp.bfloat16)
        .reshape(row_count, head_count, head_depth)
    )
    all_keys, all_values = (
        lax.all_gather(key_bf, "ctx", axis=0, tiled=True),
        lax.all_gather(value_bf, "ctx", axis=0, tiled=True),
    )
    key_blocks = all_keys.reshape(block_count, block_size, head_count, head_depth)
    value_blocks = all_values.reshape(block_count, block_size, head_count, head_depth)
    place_blocks = key_places.reshape(block_count, block_size)

    def stat_step(carry, pieces):
        row_top, row_total = carry
        key_block, block_places = pieces
        scores, allowed = scores_of(query_bf, query_places, key_block, block_places)
        masked = jnp.where(allowed, scores, NEGATIVE)
        fresh_top = jnp.maximum(row_top, jnp.max(masked, axis=2))
        raised = jnp.where(allowed, jnp.exp(masked - fresh_top[:, :, None]), 0.0)
        row_total = row_total * jnp.exp(row_top - fresh_top) + jnp.sum(raised, axis=2)
        return ((fresh_top, row_total), None)

    start_stats = (
        jnp.full((row_count, head_count), NEGATIVE, jnp.float32),
        jnp.zeros((row_count, head_count), jnp.float32),
    )
    (row_top, row_total), _ = lax.scan(stat_step, start_stats, (key_blocks, place_blocks))

    def value_step(running, pieces):
        key_block, value_block, block_places = pieces
        probs = probs_of(
            query_bf, query_places, key_block, block_places, row_top, row_total
        ).astype(jnp.bfloat16)
        return (
            running
            + jnp.einsum("qhk,khe->qhe", probs, value_block, preferred_element_type=jnp.float32),
            None,
        )

    attended, _ = lax.scan(
        value_step,
        jnp.zeros((row_count, head_count, head_depth), jnp.float32),
        (key_blocks, value_blocks, place_blocks),
    )
    attended_bf = attended.reshape(row_count, model_width).astype(jnp.bfloat16)
    residual = inputs + jnp.dot(attended_bf, w_out, preferred_element_type=jnp.float32) + b_out
    normed_two, back_two = jax.vjp(layer_norm, residual, gain_two, shift_two)
    normed_two = normed_two.astype(jnp.bfloat16)
    hidden_pre = jnp.dot(normed_two, w_up, preferred_element_type=jnp.float32) + b_up
    active, back_active = jax.vjp(gelu_tanh, hidden_pre)
    active = active.astype(jnp.bfloat16)
    mixed = (
        residual + jnp.dot(active, w_down, preferred_element_type=jnp.float32) + b_down
    ).astype(jnp.bfloat16)
    grad_result = cotangent[0]
    grad_down_bias = jnp.sum(grad_result.astype(jnp.float32), axis=0)
    grad_down = transposed_product(active, grad_result)
    grad_active = times_transposed(grad_result, w_down)
    grad_pre = back_active(grad_active)[0].astype(jnp.bfloat16)
    grad_up_bias = jnp.sum(grad_pre.astype(jnp.float32), axis=0)
    grad_up = transposed_product(normed_two, grad_pre)
    grad_normed_two = times_transposed(grad_pre, w_up)
    residual_part, grad_gain_two, grad_shift_two = back_two(grad_normed_two)
    grad_residual = grad_result.astype(jnp.float32) + residual_part
    grad_branch = grad_residual.astype(jnp.bfloat16)
    grad_out_bias = jnp.sum(grad_branch.astype(jnp.float32), axis=0)
    grad_out_weight = transposed_product(attended_bf, grad_branch)
    grad_attended = (
        times_transposed(grad_branch, w_out)
        .astype(jnp.bfloat16)
        .reshape(row_count, head_count, head_depth)
    )

    def delta_step(running, pieces):
        key_block, value_block, block_places = pieces
        probs = probs_of(query_bf, query_places, key_block, block_places, row_top, row_total)
        slopes = jnp.einsum(
            "qhe,khe->qhk", grad_attended, value_block, preferred_element_type=jnp.float32
        )
        return (running + jnp.sum(probs * slopes, axis=2), None)

    row_delta, _ = lax.scan(
        delta_step,
        jnp.zeros((row_count, head_count), jnp.float32),
        (key_blocks, value_blocks, place_blocks),
    )
    empty_rows = jnp.zeros((row_count, head_count, head_depth), jnp.float32)

    def query_and_key_step(running, pieces):
        key_block, value_block, block_places = pieces
        probs_bf, grad_scores = score_grads(
            query_bf,
            query_places,
            grad_attended,
            key_block,
            value_block,
            block_places,
            row_top,
            row_total,
            row_delta,
        )
        running = running + jnp.einsum(
            "qhk,khe->qhe", grad_scores, key_block, preferred_element_type=jnp.float32
        )
        key_terms = jnp.einsum(
            "qhk,qhe->khe", grad_scores, query_bf, preferred_element_type=jnp.float32
        )
        value_terms = jnp.einsum(
            "qhk,qhe->khe", probs_bf, grad_attended, preferred_element_type=jnp.float32
        )
        return (running, (key_terms, value_terms))

    grad_query, (key_terms, value_terms) = lax.scan(
        query_and_key_step, empty_rows, (key_blocks, value_blocks, place_blocks)
    )
    key_terms = key_terms.reshape(total_rows, head_count, head_depth)
    value_terms = value_terms.reshape(total_rows, head_count, head_depth)
    grad_key, grad_value = (
        lax.psum_scatter(
            key_terms.astype(jnp.bfloat16), "ctx", scatter_dimension=0, tiled=True
        ).astype(jnp.float32),
        lax.psum_scatter(
            value_terms.astype(jnp.bfloat16), "ctx", scatter_dimension=0, tiled=True
        ).astype(jnp.float32),
    )
    grad_query = grad_query.astype(jnp.bfloat16).reshape(row_count, model_width)
    grad_key = grad_key.astype(jnp.bfloat16).reshape(row_count, model_width)
    grad_value = grad_value.astype(jnp.bfloat16).reshape(row_count, model_width)
    grad_qv_bias = jnp.concatenate(
        [
            jnp.sum(grad_query.astype(jnp.float32), axis=0),
            jnp.sum(grad_value.astype(jnp.float32), axis=0),
        ]
    )
    grad_projected = jnp.concatenate([grad_query, grad_key, grad_value], axis=1)
    grad_qkv = transposed_product(normed_one, grad_projected)
    grad_normed_one = times_transposed(grad_projected, w_qkv)
    input_part, grad_gain_one, grad_shift_one = back_one(grad_normed_one)
    tokens_grad = grad_residual + input_part
    full_grads = (
        grad_gain_one,
        grad_shift_one,
        grad_qkv,
        grad_qv_bias,
        grad_out_weight,
        grad_out_bias,
        grad_gain_two,
        grad_shift_two,
        grad_up,
        grad_up_bias,
        grad_down,
        grad_down_bias,
    )
    shards = (
        lax.psum_scatter(
            full_grads[0].astype(jnp.bfloat16), "fsdp", scatter_dimension=0, tiled=True
        ).astype(jnp.float32),
        lax.psum_scatter(
            full_grads[1].astype(jnp.bfloat16), "fsdp", scatter_dimension=0, tiled=True
        ).astype(jnp.float32),
        lax.psum_scatter(
            full_grads[2].astype(jnp.bfloat16), "fsdp", scatter_dimension=0, tiled=True
        ).astype(jnp.float32),
        lax.psum_scatter(
            full_grads[3].astype(jnp.bfloat16), "fsdp", scatter_dimension=0, tiled=True
        ).astype(jnp.float32),
        lax.psum_scatter(
            full_grads[4].astype(jnp.bfloat16), "fsdp", scatter_dimension=0, tiled=True
        ).astype(jnp.float32),
        lax.psum_scatter(
            full_grads[5].astype(jnp.bfloat16), "fsdp", scatter_dimension=0, tiled=True
        ).astype(jnp.float32),
        lax.psum_scatter(
            full_grads[6].astype(jnp.bfloat16), "fsdp", scatter_dimension=0, tiled=True
        ).astype(jnp.float32),
        lax.psum_scatter(
            full_grads[7].astype(jnp.bfloat16), "fsdp", scatter_dimension=0, tiled=True
        ).astype(jnp.float32),
        lax.psum_scatter(
            full_grads[8].astype(jnp.bfloat16), "fsdp", scatter_dimension=0, tiled=True
        ).astype(jnp.float32),
        lax.psum_scatter(
            full_grads[9].astype(jnp.bfloat16), "fsdp", scatter_dimension=0, tiled=True
        ).astype(jnp.float32),
        lax.psum_scatter(
            full_grads[10].astype(jnp.bfloat16), "fsdp", scatter_dimension=0, tiled=True
        ).astype(jnp.float32),
        lax.psum_scatter(
            full_grads[11].astype(jnp.bfloat16), "fsdp", scatter_dimension=0, tiled=True
        ).astype(jnp.float32),
    )
    totals = (
        lax.psum(shards[0].astype(jnp.bfloat16), "ctx").astype(jnp.float32),
        lax.psum(shards[1].astype(jnp.bfloat16), "ctx").astype(jnp.float32),
        lax.psum(shards[2].astype(jnp.bfloat16), "ctx").astype(jnp.float32),
        lax.psum(shards[3].astype(jnp.bfloat16), "ctx").astype(jnp.float32),
        lax.psum(shards[4].astype(jnp.bfloat16), "ctx").astype(jnp.float32),
        lax.psum(shards[5].astype(jnp.bfloat16), "ctx").astype(jnp.float32),
        lax.psum(shards[6].astype(jnp.bfloat16), "ctx").astype(jnp.float32),
        lax.psum(shards[7].astype(jnp.bfloat16), "ctx").astype(jnp.float32),
        lax.psum(shards[8].astype(jnp.bfloat16), "ctx").astype(jnp.float32),
        lax.psum(shards[9].astype(jnp.bfloat16), "ctx").astype(jnp.float32),
        lax.psum(shards[10].astype(jnp.bfloat16), "ctx").astype(jnp.float32),
        lax.psum(shards[11].astype(jnp.bfloat16), "ctx").astype(jnp.float32),
    )
    return (mixed[None], tokens_grad[None]) + tuple(totals)


def solution(mesh):
    in_specs = (
        P("fsdp", "ctx", None),
        P("fsdp", "ctx", None),
        P(),
        P("fsdp"),
        P("fsdp"),
        P("fsdp", None),
        P("fsdp"),
        P("fsdp", None),
        P("fsdp"),
        P("fsdp"),
        P("fsdp"),
        P("fsdp", None),
        P("fsdp"),
        P("fsdp", None),
        P("fsdp"),
    )
    out_specs = (
        P("fsdp", "ctx", None),
        P("fsdp", "ctx", None),
        P("fsdp"),
        P("fsdp"),
        P("fsdp", None),
        P("fsdp"),
        P("fsdp", None),
        P("fsdp"),
        P("fsdp"),
        P("fsdp"),
        P("fsdp", None),
        P("fsdp"),
        P("fsdp", None),
        P("fsdp"),
    )
    return jax.shard_map(local, mesh=mesh, in_specs=in_specs, out_specs=out_specs, check_vma=False)
```

profile of v0, /device:TPU:0, one launch (start us, length us, event | category | flops | bytes accessed | tf_op | source)
XLA Modules:
  0.0 758.4 jit_solution(16182837675105925238)
XLA Ops:
  15.6 26.9 %all-reduce.18 = (bf16[768]{0:T(1024)(128)(2,1)S(1)}, bf16[768]{0:T(1024)(128)(2,1)S(1)}, bf16[1536]{0:T(1024)(128)(2,1)S(1)}, bf16[768]{0:T(1024)(128)(2,1)S(1)...) all-reduce(bf16[768]{0:T(1024)(128)(2,1)S(1)} %dynamic-update-slice, ...), channel_id=1, replica_groups=mesh['ctx'=16,'fsdp'=8] {'fsdp'}, use_global_device_ids=true, to_apply=%add.1 | all-reduce | flops 5376 | bytes 21504
  45.4 2.8 fusion.103
  53.9 11.4 %all-gather = bf16[8,1,384]{2,1,0:T(2,128)(2,1)S(1)} all-gather(bf16[1,1,384]{2,1,0:T(2,128)(2,1)S(1)} %reshape.314), channel_id=1, replica_groups=mesh['ctx'=16,'fsdp'=8] {'fsdp'}, dimensions={0}, use_global_device_ids=true | all-gather | bytes 6912 | tf_op jit(solution)/shard_map/all_gather | solution.py:126
  66.1 35.6 %all-gather.12.cloned.1.call-done = bf16[2048,12,64]{0,2,1:T(8,128)(2,1)} async-done(((bf16[128,12,64]{0,2,1:T(8,128)(2,1)}), bf16[2048,12,64]{0,2,1:T(8,128)(2,1)}) %all-gather.12.cloned.1.call-update) | async-done | bytes 3145744 | tf_op jit(solution)/shard_map/all_gather | solution.py:183
  101.7 2.3 copy.107
  104.0 52.4 %all-gather.10.cloned.1.call-done = bf16[2048,12,64]{0,2,1:T(8,128)(2,1)} async-done(((bf16[128,12,64]{0,2,1:T(8,128)(2,1)}), bf16[2048,12,64]{0,2,1:T(8,128)(2,1)}) %all-gather.10.cloned.1.call-update) | async-done | bytes 3145744 | tf_op jit(solution)/shard_map/all_gather | solution.py:184
  156.4 4.0 copy.108
  160.3 7.0 while.50
  168.0 21.4 %while.51 = (s32[]{:T(128)}, f32[128,12,64]{0,2,1:T(8,128)}, bf16[4,512,12,64]{1,3,2,0:T(8,128)(2,1)}, s32[4,512]{1,0:T(4,128)}, s32[128]{0:T(128)}, /*index=5*/...) while((s32[]{:T(128)}, f32[128,12,64]{0,2,1:T(8,128)}, ...), condition=%wide.region_8.9_spmd.clone, body=%wide.region_7.8_spmd.clone.sunk | while | flops 205520896 | bytes 2711682 | solution.py:217
  168.7 1.4 broadcast_compare_fusion.10
  170.2 3.1 fusion.171
  175.4 3.3 fusion.171
  179.4 1.4 broadcast_compare_fusion.10
  180.8 3.2 fusion.171
  186.2 3.2 fusion.171
  189.4 1.7 convert_element_type.202
  191.1 1.8 fusion.113
  194.4 22.4 %all-gather.16.cloned.1.call-done = bf16[768,3072]{1,0:T(8,128)(2,1)} async-done(((bf16[96,3072]{1,0:T(8,128)(2,1)}), bf16[768,3072]{1,0:T(8,128)(2,1)}) %all-gather.16.cloned.1.call-update) | async-done | bytes 4718608 | tf_op jit(solution)/shard_map/all_gather | solution.py:125
  216.8 4.5 convolution_add_fusion
  221.3 31.4 %all-gather.18.cloned.1.call-done = bf16[3072,768]{1,0:T(8,128)(2,1)} async-done(((bf16[384,768]{1,0:T(8,128)(2,1)}), bf16[3072,768]{1,0:T(8,128)(2,1)}) %all-gather.18.cloned.1.call-update) | async-done | bytes 4718608 | tf_op jit(solution)/shard_map/all_gather | solution.py:127
  252.7 5.5 fusion.114
  258.3 2.3 multiply_reduce_fusion
  264.6 18.6 %while.52 = (s32[]{:T(128)}, f32[128,12]{0,1:T(8,128)S(1)}, s32[4,512]{1,0:T(4,128)}, s32[128]{0:T(128)}, bf16[4,512,12,64]{1,3,2,0:T(8,128)(2,1)S(1)}, /*index=...) while((s32[]{:T(128)}, f32[128,12]{0,1:T(8,128)S(1)}, ...), condition=%wide.region_15.16_spmd.clone, body=%wide.region_13.15_spmd.clone.sunk | while | flops 206112256 | bytes 8456879 | solution.py:259
  266.8 2.4 fusion.177
  271.4 2.4 fusion.177
  276.0 2.4 fusion.177
  280.7 2.4 fusion.177
  283.1 39.8 %while.53 = (s32[]{:T(128)}, f32[128,12,64]{0,2,1:T(8,128)}, bf16[4,512,12,64]{1,3,2,0:T(8,128)(2,1)}, bf16[4,512,12,64]{1,3,2,0:T(8,128)(2,1)}, bf16[4,512,12,6...) while((s32[]{:T(128)}, f32[128,12,64]{0,2,1:T(8,128)}, ...), condition=%wide.region_17.18_spmd.clone, body=%wide.region_16.17_spmd.clone.sunk | while | flops 510656512 | bytes 74869592 | solution.py:290
  284.9 1.7 fusion.188
  286.6 2.1 fusion.189
  291.6 1.6 copy-done.16
  294.8 1.7 fusion.188
  296.5 2.1 fusion.189
  301.5 1.6 copy-done.16
  304.6 1.7 fusion.188
  306.4 2.1 fusion.189
  311.4 1.6 copy-done.16
  314.5 1.7 fusion.188
  316.3 2.1 fusion.189
  321.3 1.6 copy-done.16
  322.9 10.5 %copy.99 = bf16[4,512,12,64]{3,2,1,0:T(8,128)(2,1)} copy(bf16[4,512,12,64]{1,3,2,0:T(8,128)(2,1)} %get-tuple-element.226) | data formatting | bytes 6291456
  333.5 11.2 %reshape.333 = bf16[2048,768]{1,0:T(8,128)(2,1)} reshape(bf16[2048,12,64]{2,1,0:T(8,128)(2,1)} %bitcast.268) | data formatting | bytes 6291456
  344.7 1.8 copy-done.17
  346.5 8.6 %copy.97 = bf16[4,512,12,64]{3,2,1,0:T(8,128)(2,1)} copy(bf16[4,512,12,64]{1,3,2,0:T(8,128)(2,1)S(1)} %copy-done.17) | data formatting | bytes 6291456
  355.1 11.2 %reshape.331 = bf16[2048,768]{1,0:T(8,128)(2,1)} reshape(bf16[2048,12,64]{2,1,0:T(8,128)(2,1)} %bitcast.269) | data formatting | bytes 6291456
  367.3 1.5 convolution_convert_fusion.3
  368.9 3.6 convolution_convert_fusion.1
  374.0 3.7 convolution_convert_fusion
  378.9 41.7 %reduce-scatter.21.cloned.1.call-done = bf16[128,768]{1,0:T(8,128)(2,1)} async-done(((bf16[2048,768]{1,0:T(8,128)(2,1)}), bf16[128,768]{1,0:T(8,128)(2,1)}) %reduce-scatter.21.cloned.1.call-update) | async-done | bytes 196624
  421.8 77.2 %reduce-scatter.19.cloned.1.call-done = bf16[128,768]{1,0:T(8,128)(2,1)} async-done(((bf16[2048,768]{1,0:T(8,128)(2,1)}), bf16[128,768]{1,0:T(8,128)(2,1)}) %reduce-scatter.19.cloned.1.call-update) | async-done | bytes 196624
  500.0 3.0 convolution_convert_fusion.2
  506.3 26.9 %reduce-scatter.13.cloned.1.call-done = bf16[96,768]{1,0:T(8,128)(2,1)} async-done(((bf16[768,768]{1,0:T(8,128)(2,1)}), bf16[96,768]{1,0:T(8,128)(2,1)}) %reduce-scatter.13.cloned.1.call-update) | async-done | bytes 147472 | tf_op jit(solution)/shard_map/reduce_scatter | solution.py:344
  533.1 40.1 %reduce-scatter.15.cloned.1.call-done = bf16[96,3072]{1,0:T(8,128)(2,1)} async-done(((bf16[768,3072]{1,0:T(8,128)(2,1)}), bf16[96,3072]{1,0:T(8,128)(2,1)}) %reduce-scatter.15.cloned.1.call-update) | async-done | bytes 589840 | tf_op jit(solution)/shard_map/reduce_scatter | solution.py:356
  573.2 40.6 %reduce-scatter.17.cloned.1.call-done = bf16[384,768]{1,0:T(8,128)(2,1)} async-done(((bf16[3072,768]{1,0:T(8,128)(2,1)}), bf16[384,768]{1,0:T(8,128)(2,1)}) %reduce-scatter.17.cloned.1.call-update) | async-done | bytes 589840 | tf_op jit(solution)/shard_map/reduce_scatter | solution.py:362
  613.9 38.1 %reduce-scatter.11.cloned.1.call-done = bf16[96,2304]{1,0:T(8,128)(2,1)} async-done(((bf16[768,2304]{1,0:T(8,128)(2,1)}), bf16[96,2304]{1,0:T(8,128)(2,1)}) %reduce-scatter.11.cloned.1.call-update) | async-done | bytes 442384 | tf_op jit(solution)/shard_map/reduce_scatter | solution.py:338
  652.1 4.1 fusion.106
  656.5 24.9 %all-reduce.17 = (bf16[768]{0:T(1024)(128)(2,1)S(1)}, bf16[768]{0:T(1024)(128)(2,1)S(1)}, bf16[768]{0:T(1024)(128)(2,1)S(1)}, bf16[1536]{0:T(1024)(128)(2,1)S(1)...) all-reduce(bf16[768]{0:T(1024)(128)(2,1)} %copy-done.47, ...), channel_id=1, replica_groups=mesh['ctx'=16,'fsdp'=8] {'fsdp'}, use_global_device_ids=true, to_apply=%add.6 | all-reduce | flops 9984 | bytes 39936
  682.0 41.1 %all-reduce.15 = (bf16[96]{0:T(256)(128)(2,1)S(1)}, bf16[96]{0:T(256)(128)(2,1)S(1)}, bf16[192]{0:T(256)(128)(2,1)S(1)}, bf16[96]{0:T(256)(128)(2,1)S(1)}, bf16[...) all-reduce(bf16[96]{0:T(256)(128)(2,1)S(1)} %dynamic-slice.8, ...), channel_id=1, replica_groups=mesh['ctx'=16,'fsdp'=8] {'ctx'}, use_global_device_ids=true, to_apply=%region_24.25 | all-reduce | flops 1152 | bytes 4608 | tf_op jit(solution)/shard_map/psum | solution.py:370
  727.3 1.6 add_bitcast_fusion
  728.9 4.3 fusion.63
  733.2 11.7 %all-reduce.21.cloned.1.call-done = (bf16[96,2304]{1,0:T(8,128)(2,1)}, bf16[96,768]{1,0:T(8,128)(2,1)}, bf16[96,3072]{1,0:T(8,128)(2,1)}, bf16[384,768]{1,0:T(8,128)(2,1)}) async-done(((bf16[96,2304]{1,0:T(8,128)(2,1)}, bf16[96,768]{1,0:T(8,128)(2,1)}, bf16[96,3072]{1,0:T(8,128)(2,1)}, bf16[384,768]{1,0:T(8,128)(2,1)}), (bf16[96,2304]{1,0:T(8,128)(2,1)}, bf16[96,768]{1,0:T(8,128)(2,1)}, ...) | async-done | bytes 1769488 | tf_op jit(solution)/shard_map/psum | solution.py:372
  744.9 1.7 convert_element_type.231
  746.6 2.0 convert_element_type.226
  748.6 2.2 convert_element_type.238
  (331 shorter events, 74.1 us)
Async XLA Ops:
  7.2 37.6 %all-gather.8.cloned.1.call-start = ((), (), s32[]{:S(2)}) async-start(), calls=%async_computation.6 | async-start | bytes 3981312 | tf_op jit(solution)/shard_map/all_gather | solution.py:119
  7.9 93.8 %all-gather.12.cloned.1.call-start = ((), (), s32[]{:S(2)}) async-start(), calls=%async_computation.8 | async-start | bytes 3342336 | tf_op jit(solution)/shard_map/all_gather | solution.py:183
  42.6 2.3 copy-start.36
  42.6 2.3 copy-start.28
  48.2 3.8 copy-start.49
  48.2 5.5 copy-start.54
  49.1 107.3 %all-gather.10.cloned.1.call-start = ((), (), s32[]{:S(2)}) async-start(), calls=%async_computation.7 | async-start | bytes 3342336 | tf_op jit(solution)/shard_map/all_gather | solution.py:184
  50.0 141.1 %all-gather.14.cloned.1.call-start = ((), (), s32[]{:S(2)}) async-start(), calls=%async_computation.9 | async-start | bytes 1327104 | tf_op jit(solution)/shard_map/all_gather | solution.py:121
  50.6 166.2 %all-gather.16.cloned.1.call-start = ((), (), s32[]{:S(2)}) async-start(), calls=%async_computation.10 | async-start | bytes 5308416 | tf_op jit(solution)/shard_map/all_gather | solution.py:125
  51.2 201.5 %all-gather.18.cloned.1.call-start = ((), (), s32[]{:S(2)}) async-start(), calls=%async_computation.11 | async-start | bytes 5308416 | tf_op jit(solution)/shard_map/all_gather | solution.py:127
  51.8 368.9 %reduce-scatter.21.cloned.1.call-start = ((), (), s32[]{:S(2)}) async-start(), calls=%async_computation.17 | async-start | bytes 3342336
  168.0 23.1 %copy-start.8 = (bf16[1,128,768]{2,1,0:T(8,128)(2,1)S(1)}, bf16[1,128,768]{2,1,0:T(8,128)(2,1)}, u32[]{:S(2)}) copy-start(bf16[1,128,768]{2,1,0:T(8,128)(2,1)} %param.23) | copy-start | bytes 589828
  193.0 23.8 %copy-start.38 = (f32[128]{0:T(128)}, f32[128]{0:T(128)S(1)}, u32[]{:S(2)}) copy-start(f32[128]{0:T(128)S(1)} %broadcast_multiply_fusion) | copy-start | bytes 1540
  193.9 22.9 %copy-start.52 = (f32[128]{0:T(128)}, f32[128]{0:T(128)S(1)}, u32[]{:S(2)}) copy-start(f32[128]{0:T(128)S(1)} %multiply_reduce_fusion.2) | copy-start | bytes 1540
  216.8 35.9 %copy-start.20 = (bf16[1,128,768]{2,1,0:T(8,128)(2,1)S(1)}, bf16[1,128,768]{2,1,0:T(8,128)(2,1)}, u32[]{:S(2)}) copy-start(bf16[1,128,768]{2,1,0:T(8,128)(2,1)} %param.24) | copy-start | bytes 589828
  252.7 5.6 copy-start
  252.7 5.6 copy-start.2
  252.7 5.6 copy-start.30
  252.7 5.6 copy-start.39
  252.7 5.6 copy-start.43
  258.2 2.4 copy-start.18
  258.3 2.3 copy-start.53
  258.3 4.0 copy-start.10
  264.6 2.2 copy-start.34
  269.2 2.2 copy-start.34
  273.9 2.2 copy-start.34
  278.5 2.2 copy-start.34
  286.6 2.1 copy-start.13
  288.8 2.1 copy-start.15
  289.7 1.8 copy-start.14
  296.5 2.1 copy-start.13
  298.6 2.1 copy-start.15
  299.6 1.8 copy-start.14
  301.5 1.6 copy-start.16
  306.4 2.1 copy-start.13
  308.5 2.1 copy-start.15
  309.5 1.8 copy-start.14
  316.3 2.1 copy-start.13
  318.4 2.1 copy-start.15
  319.4 1.8 copy-start.14
  344.6 1.9 copy-start.17
  344.6 154.3 %reduce-scatter.19.cloned.1.call-start = ((), (), s32[]{:S(2)}) async-start(), calls=%async_computation.16 | async-start | bytes 3342336
  366.3 2.6 copy-start.3
  366.3 2.6 copy-start.19
  366.3 2.6 copy-start.31
  366.3 2.6 copy-start.35
  366.3 2.6 copy-start.40
  366.3 2.6 copy-start.44
  366.4 166.8 %reduce-scatter.13.cloned.1.call-start = ((), (), s32[]{:S(2)}) async-start(), calls=%async_computation.13 | async-start | bytes 1327104 | tf_op jit(solution)/shard_map/reduce_scatter | solution.py:344
  368.8 204.4 %reduce-scatter.15.cloned.1.call-start = ((), (), s32[]{:S(2)}) async-start(), calls=%async_computation.14 | async-start | bytes 5308416 | tf_op jit(solution)/shard_map/reduce_scatter | solution.py:356
  372.6 241.3 %reduce-scatter.17.cloned.1.call-start = ((), (), s32[]{:S(2)}) async-start(), calls=%async_computation.15 | async-start | bytes 5308416 | tf_op jit(solution)/shard_map/reduce_scatter | solution.py:362
  377.7 122.3 %copy-start.9 = (bf16[1,128,768]{2,1,0:T(8,128)(2,1)S(1)}, bf16[1,128,768]{2,1,0:T(8,128)(2,1)}, u32[]{:S(2)}) copy-start(bf16[1,128,768]{2,1,0:T(8,128)(2,1)} %param.23) | copy-start | bytes 589828
  377.7 122.3 %copy-start.29 = (f32[768]{0:T(1024)S(1)}, f32[768]{0:T(1024)}, u32[]{:S(2)}) copy-start(f32[768]{0:T(1024)} %copy-done.28) | copy-start | bytes 9220
  377.7 122.3 %copy-start.37 = (f32[768]{0:T(1024)S(1)}, f32[768]{0:T(1024)}, u32[]{:S(2)}) copy-start(f32[768]{0:T(1024)} %copy-done.36) | copy-start | bytes 9220
  377.8 122.3 %copy-start.42 = (f32[128]{0:T(128)S(1)}, f32[128]{0:T(128)}, u32[]{:S(2)}) copy-start(f32[128]{0:T(128)} %copy-done.41) | copy-start | bytes 1540
  377.8 122.3 %copy-start.46 = (f32[128]{0:T(128)S(1)}, f32[128]{0:T(128)}, u32[]{:S(2)}) copy-start(f32[128]{0:T(128)} %copy-done.45) | copy-start | bytes 1540
  377.8 274.2 %reduce-scatter.11.cloned.1.call-start = ((), (), s32[]{:S(2)}) async-start(), calls=%async_computation.12 | async-start | bytes 3981312 | tf_op jit(solution)/shard_map/reduce_scatter | solution.py:338
  378.9 124.1 %copy-start.25 = (bf16[128,12,64]{0,2,1:T(8,128)(2,1)}, bf16[128,12,64]{0,2,1:T(8,128)(2,1)S(1)}, u32[]{:S(2)}) copy-start(bf16[128,12,64]{0,2,1:T(8,128)(2,1)S(1)} %get-tuple-element.627) | copy-start | bytes 589828
  503.1 2.7 copy-start.55
  503.1 241.8 %all-reduce.21.cloned.1.call-start = ((), (), s32[]{:S(2)}) async-start(), calls=%async_computation.18 | async-start | bytes 3538944 | tf_op jit(solution)/shard_map/psum | solution.py:372
  505.9 146.1 %copy-start.47 = (bf16[768]{0:T(1024)(128)(2,1)}, bf16[768]{0:T(1024)(128)(2,1)S(1)}, u32[]{:S(2)}) copy-start(bf16[768]{0:T(1024)(128)(2,1)S(1)} %dynamic-update-slice.6) | copy-start | bytes 4612
  652.0 4.2 copy-start.51
  652.0 75.3 %copy-start.12 = (f32[128,768]{1,0:T(8,128)S(1)}, f32[128,768]{1,0:T(8,128)}, u32[]{:S(2)}) copy-start(f32[128,768]{1,0:T(8,128)} %copy-done.11) | copy-start | bytes 1179652
  744.9 5.9 copy-start.26
  (26 other events, 24.7 us)
Sparse Core Ops, SparseCore 0:
  9.7 32.0 all-gather.7
  49.2 52.4 all-gather.11
  104.4 51.9 all-gather.9
  157.9 22.8 all-gather.13
  182.4 34.3 all-gather.15
  218.3 34.2 all-gather.17
  344.8 75.8 reduce-scatter.20
  424.0 74.8 reduce-scatter.18
  501.9 31.2 reduce-scatter.12
  535.4 37.7 reduce-scatter.14
  575.7 38.1 reduce-scatter.16
  616.2 35.8 reduce-scatter.10
  656.2 88.6 all-reduce.20
where the time goes:
time: 761 us; the launch traced here: 758 us
  waiting for transfers between devices  420 us (55%)
  blocking collectives  104 us (14%)
  matrix products  89.6 us (12%)
  local copies, waits for them, and re-layouts  86.8 us (11%)
  other arithmetic  37.8 us (5%)
  between operations  17.8 us (2%)
    unnamed x15, waiting for transfers between devices  121 us
    unnamed x126, local copies, waits for them, and re-layouts  56.3 us
    all_gather x1, waiting for transfers between devices, local(): lax.all_gather(value_bf, 'ctx', axis=0, tiled=True)  52.4 us
    unnamed x2, blocking collectives  51.8 us
    psum x1, blocking collectives, local(): lax.psum(shards[0].astype(jnp.bfloat16), 'ctx').astype(jnp.float32)  41.1 us
    reduce_scatter x1, waiting for transfers between devices, local(): lax.psum_scatter(full_grads[10].astype(jnp.bfloat16), 'fsdp', scatter_dim...  40.6 us
    reduce_scatter x1, waiting for transfers between devices, local(): lax.psum_scatter(full_grads[8].astype(jnp.bfloat16), 'fsdp', scatter_dime...  40.1 us
    reduce_scatter x1, waiting for transfers between devices, local(): lax.psum_scatter(full_grads[2].astype(jnp.bfloat16), 'fsdp', scatter_dime...  38.1 us
  transfers between devices with their start and end apart: 13, of which 11 were waited for; matrix products, arithmetic and copies ran while one was open for 14% of the time, Pallas kernels for 0%

commit v1 on v0

v1 whole, which is shorter than its diff:
```python
import jax
import jax.numpy as jnp
from jax import lax
from jax.experimental import pallas as pl
from jax.experimental.pallas import tpu as pltpu
from jax.sharding import PartitionSpec as P

HEADS = 12
DEPTH = 64
WIDTH = 768
HIDDEN = 3072
ROWS = 128
HALF = 64
CTX = 16
FSDP = 8
SEQ = CTX * ROWS
QT = 256
KT = 512
EPSILON = 1e-05
NEGATIVE = -1e30
VMEM_LIMIT = 56 * 1024 * 1024

BF = jnp.bfloat16
F32 = jnp.float32

VECTORS = (
    ("first_gain", 96),
    ("first_shift", 96),
    ("qv_bias", 192),
    ("out_bias", 96),
    ("second_gain", 96),
    ("second_shift", 96),
    ("up_bias", 384),
    ("down_bias", 96),
)
VECTOR_WIDTH = sum(width for _, width in VECTORS)

OUT_AT, UP_AT, DOWN_AT, PACK_ROWS = 0, 96, 480, 864


def dot(left, right):
    return jnp.dot(left, right, preferred_element_type=F32)


def dot_nt(left, right):
    return lax.dot_general(left, right, (((1,), (1,)), ((), ())), preferred_element_type=F32)


def dot_tn(left, right):
    return lax.dot_general(left, right, (((0,), (0,)), ((), ())), preferred_element_type=F32)


def normalise(values):
    center = values - jnp.mean(values, axis=-1, keepdims=True)
    spread = jnp.mean(center * center, axis=-1, keepdims=True)
    inverse = lax.rsqrt(spread + EPSILON)
    return center * inverse, inverse


def norm_back(upstream, hat, inverse, gain):
    scaled = upstream * gain
    mean_one = jnp.mean(scaled, axis=-1, keepdims=True)
    mean_two = jnp.mean(scaled * hat, axis=-1, keepdims=True)
    return (scaled - mean_one - hat * mean_two) * inverse


def block_at(index):
    return pl.ds(pl.multiple_of(index * HALF, HALF), HALF)


def lanes_at(index, size):
    return pl.ds(pl.multiple_of(index * size, size), size)


def vmem_call(kernel, out_shape, scratch, flops, in_vmem, smem_first=False, transcendentals=0):
    specs = [pl.BlockSpec(memory_space=pltpu.VMEM)] * in_vmem
    if smem_first:
        specs = [pl.BlockSpec(memory_space=pltpu.SMEM)] + specs
    return pl.pallas_call(
        kernel,
        out_shape=out_shape,
        in_specs=specs,
        out_specs=[pl.BlockSpec(memory_space=pltpu.VMEM)] * len(out_shape),
        scratch_shapes=scratch,
        compiler_params=pltpu.CompilerParams(vmem_limit_bytes=VMEM_LIMIT),
        cost_estimate=pl.CostEstimate(
            flops=flops, bytes_accessed=8 * 2**20, transcendentals=transcendentals
        ),
    )


def head_forward_kernel(
    order, tok, weight, bias, gain, shift,
    packed, normed, query, key, value, query_t, key_t, out_t, lse,
    value_t,
):
    def project(c, _):
        hat, _inv = normalise(tok[c].astype(F32))
        low = (hat * gain[...] + shift[...]).astype(BF)
        made = (dot(low, weight[...]) + bias[...]).astype(BF)
        place = order[c]
        for part, block in ((0, place), (1, 2 * CTX - 1 - place)):
            rows = slice(part * HALF, (part + 1) * HALF)
            normed[block_at(block), :] = low[rows]
            query[block_at(block), :] = made[rows, 0:DEPTH]
            key[block_at(block), :] = made[rows, DEPTH : 2 * DEPTH]
            value[block_at(block), :] = made[rows, 2 * DEPTH :]
        return 0

    lax.fori_loop(0, CTX, project, 0)

    def turn(t, _):
        rows = lanes_at(t, QT)
        for source, target in ((query, query_t), (key, key_t), (value, value_t)):
            target[:, rows] = source[rows, :].astype(F32).T.astype(BF)
        return 0

    lax.fori_loop(0, SEQ // QT, turn, 0)

    def attend(i, _):
        lanes = lanes_at(i, QT)
        queries = query_t[:, lanes]

        def step(j, carry, masked):
            top, total, acc = carry
            rows = lanes_at(j, KT)
            scores = dot(key[rows, :], queries) * (DEPTH ** -0.5)
            if masked:
                key_place = j * KT + lax.broadcasted_iota(jnp.int32, (KT, QT), 0)
                query_place = i * QT + lax.broadcasted_iota(jnp.int32, (KT, QT), 1)
                scores = jnp.where(key_place <= query_place, scores, NEGATIVE)
            fresh = jnp.maximum(top, jnp.max(scores, axis=0, keepdims=True))
            raised = jnp.exp(scores - fresh)
            fade = jnp.exp(top - fresh)
            total = total * fade + jnp.sum(raised, axis=0, keepdims=True)
            acc = acc * fade + dot(value_t[:, rows], raised.astype(BF))
            return fresh, total, acc

        start = (
            jnp.full((1, QT), NEGATIVE, F32),
            jnp.zeros((1, QT), F32),
            jnp.zeros((DEPTH, QT), F32),
        )
        full = i // 2
        carry = lax.fori_loop(0, full, lambda j, carry: step(j, carry, False), start)
        top, total, acc = step(full, carry, True)
        result = acc / total
        out_t[:, lanes] = result
        lse[pl.ds(i, 1), :] = top + jnp.log(total)
        return 0

    lax.fori_loop(0, SEQ // QT, attend, 0)


def head_forward(order, tok, weight, bias, gain, shift):
    def kernel(
        order, tok, weight, bias, gain, shift,
        packed, normed, query, key, value, query_t, key_t, out_t, lse,
        value_t, out_rows,
    ):
        head_forward_kernel(
            order, tok, weight, bias, gain, shift,
            packed, normed, query, key, value, query_t, key_t, out_t, lse,
            value_t,
        )

        def turn_back(t, _):
            rows = lanes_at(t, QT)
            out_rows[rows, :] = out_t[:, rows].T
            return 0

        lax.fori_loop(0, SEQ // QT, turn_back, 0)

        def pack(c, _):
            place = order[c]
            packed[c] = jnp.concatenate(
                [out_rows[block_at(place), :], out_rows[block_at(2 * CTX - 1 - place), :]], axis=1
            ).astype(BF)
            return 0

        lax.fori_loop(0, CTX, pack, 0)

    shape = jax.ShapeDtypeStruct
    return vmem_call(
        kernel,
        [
            shape((CTX, HALF, 2 * DEPTH), BF),
            shape((SEQ, WIDTH), BF),
            shape((SEQ, DEPTH), BF),
            shape((SEQ, DEPTH), BF),
            shape((SEQ, DEPTH), BF),
            shape((DEPTH, SEQ), BF),
            shape((DEPTH, SEQ), BF),
            shape((DEPTH, SEQ), F32),
            shape((SEQ // QT, QT), F32),
        ],
        [pltpu.VMEM((DEPTH, SEQ), BF), pltpu.VMEM((SEQ, DEPTH), F32)],
        2 * 10**9,
        5,
        smem_first=True,
        transcendentals=3 * 10**6,
    )(order, tok, weight, bias, gain, shift)


def head_backward(order, upstream, normed, query, key, value, query_t, key_t, out_t, lse):
    def kernel(
        order, upstream, normed, query, key, value, query_t, key_t, out_t, lse,
        packed, weight_grad, bias_grad,
        grad_out, grad_out_t, delta, grad_q_t, grad_k, grad_v, rows_low,
    ):
        def unpack(c, _):
            place = order[c]
            grad_out[block_at(place), :] = upstream[c][:, :DEPTH]
            grad_out[block_at(2 * CTX - 1 - place), :] = upstream[c][:, DEPTH:]
            return 0

        lax.fori_loop(0, CTX, unpack, 0)

        def prepare(t, _):
            rows = lanes_at(t, QT)
            turned = grad_out[rows, :].astype(F32).T
            grad_out_t[:, rows] = turned.astype(BF)
            delta[pl.ds(t, 1), :] = jnp.sum(turned * out_t[:, rows], axis=0, keepdims=True)
            grad_q_t[:, rows] = jnp.zeros((DEPTH, QT), F32)
            grad_k[rows, :] = jnp.zeros((QT, DEPTH), F32)
            grad_v[rows, :] = jnp.zeros((QT, DEPTH), F32)
            return 0

        lax.fori_loop(0, SEQ // QT, prepare, 0)

        def one_query_tile(i, _):
            lanes = lanes_at(i, QT)

            def step(j, masked):
                rows = lanes_at(j, KT)
                scores = dot(key[rows, :], query_t[:, lanes]) * (DEPTH ** -0.5)
                probs = jnp.exp(scores - lse[pl.ds(i, 1), :])
                if masked:
                    key_place = j * KT + lax.broadcasted_iota(jnp.int32, (KT, QT), 0)
                    query_place = i * QT + lax.broadcasted_iota(jnp.int32, (KT, QT), 1)
                    probs = jnp.where(key_place <= query_place, probs, 0.0)
                slopes = dot(value[rows, :], grad_out_t[:, lanes])
                grad_scores = (
                    probs * (slopes - delta[pl.ds(i, 1), :]) * (DEPTH ** -0.5)
                ).astype(BF)
                grad_v[rows, :] += dot(probs.astype(BF), grad_out[lanes, :])
                grad_k[rows, :] += dot(grad_scores, query[lanes, :])
                grad_q_t[:, lanes] += dot(key_t[:, rows], grad_scores)

            full = i // 2

            def body(j, _):
                step(j, False)
                return 0

            lax.fori_loop(0, full, body, 0)
            step(full, True)
            return 0

        lax.fori_loop(0, SEQ // QT, one_query_tile, 0)

        def finish(t, sums):
            rows = lanes_at(t, QT)
            low_q = grad_q_t[:, rows].T.astype(BF)
            low_k = grad_k[rows, :].astype(BF)
            low_v = grad_v[rows, :].astype(BF)
            joined = jnp.concatenate(
                [low_q.astype(F32), low_k.astype(F32), low_v.astype(F32)], axis=1
            )
            rows_low[rows, :] = joined
            return sums + jnp.sum(joined, axis=0, keepdims=True)

        sums = lax.fori_loop(0, SEQ // QT, finish, jnp.zeros((1, 3 * DEPTH), F32))
        bias_grad[...] = sums

        weight_grad[...] = (
            dot_tn(normed[...], rows_low[...].astype(BF))
            .astype(BF)
            .reshape(FSDP, WIDTH // FSDP, 3 * DEPTH)
        )

        def pack(c, _):
            place = order[c]
            upper = rows_low[block_at(place), :]
            lower = rows_low[block_at(2 * CTX - 1 - place), :]
            pieces = []
            for part in range(3):
                lanes = slice(part * DEPTH, (part + 1) * DEPTH)
                pieces += [upper[:, lanes], lower[:, lanes]]
            packed[c] = jnp.concatenate(pieces, axis=1).astype(BF)
            return 0

        lax.fori_loop(0, CTX, pack, 0)

    shape = jax.ShapeDtypeStruct
    return vmem_call(
        kernel,
        [
            shape((CTX, HALF, 6 * DEPTH), BF),
            shape((FSDP, WIDTH // FSDP, 3 * DEPTH), BF),
            shape((1, 3 * DEPTH), F32),
        ],
        [
            pltpu.VMEM((SEQ, DEPTH), BF),
            pltpu.VMEM((DEPTH, SEQ), BF),
            pltpu.VMEM((SEQ // QT, QT), F32),
            pltpu.VMEM((DEPTH, SEQ), F32),
            pltpu.VMEM((SEQ, DEPTH), F32),
            pltpu.VMEM((SEQ, DEPTH), F32),
            pltpu.VMEM((SEQ, 3 * DEPTH), F32),
        ],
        4 * 10**9,
        9,
        smem_first=True,
        transcendentals=3 * 10**6,
    )(order, upstream, normed, query, key, value, query_t, key_t, out_t, lse)


def unpack_heads(ref, lanes):
    upper, lower = [], []
    for head in range(HEADS):
        slot = ref[head][:, lanes : lanes + 2 * DEPTH].astype(F32)
        upper.append(slot[:, :DEPTH])
        lower.append(slot[:, DEPTH:])
    return jnp.concatenate(
        [jnp.concatenate(upper, axis=1), jnp.concatenate(lower, axis=1)], axis=0
    ).astype(BF)


def gelu_parts(values):
    slope = 0.7978845608028654
    cubic = 0.044715
    squared = values * values
    bend = jnp.tanh(slope * (values + cubic * squared * values))
    active = 0.5 * values * (1.0 + bend)
    grad = 0.5 * (1.0 + bend) + 0.5 * values * (1.0 - bend * bend) * slope * (
        1.0 + 3.0 * cubic * squared
    )
    return active, grad


def feed_forward(tokens, heads_out, cotangent, pack, out_bias, gain, shift, up_bias, down_bias):
    def kernel(
        tokens, heads_out, cotangent, pack, out_bias, gain, shift, up_bias, down_bias,
        mixed, attended, normed, active, grad_pre, grad_branch, grad_heads, grad_residual,
        vector_sums, up_sums,
    ):
        inputs = tokens[...].astype(F32)
        result_grad = cotangent[...]
        attended_low = unpack_heads(heads_out, 0)
        attended[...] = attended_low
        w_out = pack[:, OUT_AT:UP_AT, :].reshape(WIDTH, WIDTH)
        residual = inputs + dot(attended_low, w_out) + out_bias[...]
        hat, inverse = normalise(residual)
        low = (hat * gain[...] + shift[...]).astype(BF)
        normed[...] = low
        total = residual + down_bias[...]
        grad_normed = jnp.zeros((ROWS, WIDTH), F32)
        for j in range(HIDDEN // WIDTH):
            lanes = slice(j * WIDTH, (j + 1) * WIDTH)
            w_up = pack[:, UP_AT + 96 * j : UP_AT + 96 * (j + 1), :].reshape(WIDTH, WIDTH)
            w_down = pack[2 * j : 2 * j + 2, DOWN_AT:PACK_ROWS, :].reshape(WIDTH, WIDTH)
            hidden = dot(low, w_up) + up_bias[:, lanes]
            acted, slope = gelu_parts(hidden)
            acted = acted.astype(BF)
            active[:, lanes] = acted
            total = total + dot(acted, w_down)
            pre = (dot_nt(result_grad, w_down) * slope).astype(BF)
            grad_pre[:, lanes] = pre
            up_sums[:, lanes] = jnp.sum(pre.astype(F32), axis=0, keepdims=True)
            grad_normed = grad_normed + dot_nt(pre, w_up)
        mixed[...] = total.astype(BF)
        back = result_grad.astype(F32) + norm_back(grad_normed, hat, inverse, gain[...])
        grad_residual[...] = back
        branch = back.astype(BF)
        grad_branch[...] = branch
        vector_sums[0:1, :] = jnp.sum(branch.astype(F32), axis=0, keepdims=True)
        vector_sums[1:2, :] = jnp.sum(grad_normed * hat, axis=0, keepdims=True)
        vector_sums[2:3, :] = jnp.sum(grad_normed, axis=0, keepdims=True)
        vector_sums[3:4, :] = jnp.sum(result_grad.astype(F32), axis=0, keepdims=True)
        grad_attended = dot_nt(branch, w_out)
        for head in range(HEADS):
            lanes = slice(head * DEPTH, (head + 1) * DEPTH)
            grad_heads[head] = jnp.concatenate(
                [grad_attended[:HALF, lanes], grad_attended[HALF:, lanes]], axis=1
            ).astype(BF)
        for head in range(HEADS, CTX):
            grad_heads[head] = jnp.zeros((HALF, 2 * DEPTH), BF)

    shape = jax.ShapeDtypeStruct
    return vmem_call(
        kernel,
        [
            shape((ROWS, WIDTH), BF),
            shape((ROWS, WIDTH), BF),
            shape((ROWS, WIDTH), BF),
            shape((ROWS, HIDDEN), BF),
            shape((ROWS, HIDDEN), BF),
            shape((ROWS, WIDTH), BF),
            shape((CTX, HALF, 2 * DEPTH), BF),
            shape((ROWS, WIDTH), F32),
            shape((4, WIDTH), F32),
            shape((1, HIDDEN), F32),
        ],
        [],
        4 * 10**9,
        9,
    )(tokens, heads_out, cotangent, pack, out_bias, gain, shift, up_bias, down_bias)


def weight_grads(left, right, blocks):
    def kernel(left, right, out):
        for j in range(blocks):
            made = dot_tn(left[...], right[:, j * WIDTH : (j + 1) * WIDTH])
            out[:, 96 * j : 96 * (j + 1), :] = made.astype(BF).reshape(FSDP, 96, WIDTH)

    return vmem_call(
        kernel,
        [jax.ShapeDtypeStruct((FSDP, 96 * blocks, WIDTH), BF)],
        [],
        2 * ROWS * WIDTH * WIDTH * blocks,
        2,
    )(left, right)[0]


def token_gradient(tokens, heads_grad, weight, gain, grad_residual):
    def kernel(tokens, heads_grad, weight, gain, grad_residual, tokens_grad, sums):
        projected = jnp.concatenate(
            [unpack_heads(heads_grad, 2 * DEPTH * part) for part in range(3)], axis=1
        )
        grad_normed = dot_nt(projected, weight[...])
        hat, inverse = normalise(tokens[...].astype(F32))
        tokens_grad[...] = grad_residual[...] + norm_back(grad_normed, hat, inverse, gain[...])
        sums[0:1, :] = jnp.sum(grad_normed * hat, axis=0, keepdims=True)
        sums[1:2, :] = jnp.sum(grad_normed, axis=0, keepdims=True)

    shape = jax.ShapeDtypeStruct
    return vmem_call(
        kernel,
        [shape((ROWS, WIDTH), F32), shape((2, WIDTH), F32)],
        [],
        2 * ROWS * WIDTH * 3 * WIDTH,
        5,
    )(tokens, heads_grad, weight, gain, grad_residual)


def swap(slots, axes):
    return lax.all_to_all(slots, axes, 0, 0, tiled=True)


def spread(piece, axes, count):
    return swap(jnp.broadcast_to(piece[None], (count,) + piece.shape), axes)


def reduce_over_ctx(shard):
    rows = shard.shape[0] // CTX
    parts = swap(shard.reshape(CTX, rows, WIDTH), "ctx")
    mine = jnp.sum(parts.astype(F32), axis=0).astype(BF)
    return spread(mine, "ctx", CTX).reshape(shard.shape).astype(F32)


def local(
    tokens, cotangent, pair_order, first_gain, first_shift, qkv_weight, qv_bias, out_weight,
    out_bias, second_gain, second_shift, up_weight, up_bias, down_weight, down_bias,
):
    my_tokens, my_cotangent = tokens[0], cotangent[0]
    place = lax.axis_index("ctx")
    head = place % HEADS
    shards = dict(
        first_gain=first_gain, first_shift=first_shift, qv_bias=qv_bias, out_bias=out_bias,
        second_gain=second_gain, second_shift=second_shift, up_bias=up_bias, down_bias=down_bias,
    )

    with jax.named_scope("gather_tokens"):
        all_tokens = spread(my_tokens, "ctx", CTX)
    with jax.named_scope("gather_weights"):
        pack = jnp.concatenate(
            [out_weight]
            + [up_weight[:, j * WIDTH : (j + 1) * WIDTH] for j in range(HIDDEN // WIDTH)]
            + [down_weight],
            axis=0,
        )
        pack = lax.all_gather(pack, "fsdp", axis=0, tiled=False)
        w_qkv = lax.all_gather(qkv_weight, "fsdp", axis=0, tiled=True)
    with jax.named_scope("gather_small"):
        head_columns = jnp.concatenate(
            [
                lax.dynamic_slice_in_dim(qkv_weight, part * WIDTH + head * DEPTH, DEPTH, 1)
                for part in range(3)
            ],
            axis=1,
        )
        vectors = jnp.concatenate([shards[name] for name, _ in VECTORS]).reshape(6, 3 * DEPTH)
        small = jnp.concatenate(
            [head_columns, vectors, jnp.zeros((10, 3 * DEPTH), BF)], axis=0
        )
        small = spread(small, "fsdp", FSDP)
        w_head = small[:, :96].reshape(WIDTH, 3 * DEPTH)
        vectors = small[:, 96:102].reshape(FSDP, VECTOR_WIDTH).astype(F32)
        whole, at = {}, 0
        for name, width in VECTORS:
            whole[name] = vectors[:, at : at + width].reshape(1, FSDP * width)
            at += width
        head_bias = jnp.concatenate(
            [
                lax.dynamic_slice_in_dim(whole["qv_bias"], head * DEPTH, DEPTH, 1),
                jnp.zeros((1, DEPTH), F32),
                lax.dynamic_slice_in_dim(whole["qv_bias"], WIDTH + head * DEPTH, DEPTH, 1),
            ],
            axis=1,
        )

    with jax.named_scope("attention"):
        packed, normed, query, key, value, query_t, key_t, out_t, lse = head_forward(
            pair_order, all_tokens, w_head, head_bias, whole["first_gain"], whole["first_shift"]
        )
        heads_out = swap(packed, "ctx")

    with jax.named_scope("feed_forward"):
        (
            mixed, attended, normed_two, active, grad_pre, grad_branch, grad_heads,
            grad_residual, vector_sums, up_sums,
        ) = feed_forward(
            my_tokens, heads_out, my_cotangent, pack, whole["out_bias"], whole["second_gain"],
            whole["second_shift"], whole["up_bias"], whole["down_bias"],
        )
        heads_up = swap(grad_heads, "ctx")

    with jax.named_scope("feed_forward_weights"):
        grad_down = lax.dot_general(
            active, my_cotangent, (((0,), (0,)), ((), ())), preferred_element_type=F32
        ).astype(BF).reshape(FSDP, 384, WIDTH)
        grad_down = lax.psum_scatter(grad_down, "fsdp", scatter_dimension=0, tiled=False)
        grad_up = weight_grads(normed_two, grad_pre, 4)
        grad_up = lax.psum_scatter(grad_up, "fsdp", scatter_dimension=0, tiled=False)
        grad_out = weight_grads(attended, grad_branch, 1)
        grad_out = lax.psum_scatter(grad_out, "fsdp", scatter_dimension=0, tiled=False)

    with jax.named_scope("attention_back"):
        packed_grad, head_weight_grad, head_bias_grad = head_backward(
            pair_order, heads_up, normed, query, key, value, query_t, key_t, out_t, lse
        )
        heads_grad = swap(packed_grad, "ctx")
    with jax.named_scope("head_weights"):
        parts = swap(head_weight_grad, "fsdp")
        mine = jnp.sum(parts.astype(F32), axis=0).astype(BF)
        head_parts = spread(mine, "ctx", CTX)[:HEADS].astype(F32)
        grad_qkv = (
            head_parts.reshape(HEADS, 96, 3, DEPTH).transpose(1, 2, 0, 3).reshape(96, 3 * WIDTH)
        )

    with jax.named_scope("token_gradient"):
        tokens_grad, first_sums = token_gradient(
            my_tokens, heads_grad, w_qkv, whole["first_gain"], grad_residual
        )

    with jax.named_scope("vector_grads"):
        holds = (jnp.arange(HEADS) == place).astype(F32)[:, None]
        bias_sums = jnp.concatenate(
            [
                (holds * head_bias_grad[:, :DEPTH]).reshape(1, WIDTH),
                (holds * head_bias_grad[:, 2 * DEPTH :]).reshape(1, WIDTH),
            ],
            axis=1,
        )
        sums = dict(
            first_gain=first_sums[0:1], first_shift=first_sums[1:2], qv_bias=bias_sums,
            out_bias=vector_sums[0:1], second_gain=vector_sums[1:2],
            second_shift=vector_sums[2:3], up_bias=up_sums, down_bias=vector_sums[3:4],
        )
        sums = jnp.concatenate(
            [sums[name].reshape(FSDP, width) for name, width in VECTORS], axis=1
        ).astype(BF)
        slots = jnp.broadcast_to(
            sums.reshape(1, FSDP, VECTOR_WIDTH // 128, 128), (CTX, FSDP, VECTOR_WIDTH // 128, 128)
        ).reshape(CTX * FSDP, VECTOR_WIDTH // 128, 128)
        mine = jnp.sum(swap(slots, ("ctx", "fsdp")).astype(F32), axis=0).reshape(VECTOR_WIDTH)
        grads, at = {}, 0
        for name, width in VECTORS:
            grads[name] = mine[at : at + width]
            at += width

    with jax.named_scope("sum_over_ctx"):
        grad_down = reduce_over_ctx(grad_down)
        grad_up = reduce_over_ctx(grad_up)
        grad_up = jnp.concatenate(
            [grad_up[96 * j : 96 * (j + 1)] for j in range(HIDDEN // WIDTH)], axis=1
        )
        grad_out = reduce_over_ctx(
            jnp.concatenate([grad_out, jnp.zeros((32, WIDTH), BF)], axis=0)
        )[:96]

    return (
        mixed[None], tokens_grad[None], grads["first_gain"], grads["first_shift"], grad_qkv,
        grads["qv_bias"], grad_out, grads["out_bias"], grads["second_gain"],
        grads["second_shift"], grad_up, grads["up_bias"], grad_down, grads["down_bias"],
    )


def solution(mesh):
    split, vector = P("fsdp", "ctx", None), P("fsdp")
    matrix = P("fsdp", None)
    in_specs = (
        split, split, P(), vector, vector, matrix, vector, matrix, vector, vector, vector,
        matrix, vector, matrix, vector,
    )
    out_specs = (
        split, split, vector, vector, matrix, vector, matrix, vector, vector, vector, matrix,
        vector, matrix, vector,
    )
    return jax.shard_map(local, mesh=mesh, in_specs=in_specs, out_specs=out_specs, check_vma=False)
```

time: 761 us -> 346 us (0.45)
  waiting for transfers between devices: 420 us -> 116 us
  matrix products: 89.6 us -> 3.53 us
  Pallas kernels: 0 us -> 66.3 us
  blocking collectives: 104 us -> 53.9 us
  local copies, waits for them, and re-layouts: 86.8 us -> 40.9 us
  starting transfers between devices: 0.52 us -> 43.4 us
  other arithmetic: 37.8 us -> 5.65 us
    all_gather x6 -> x2, waiting for transfers between devices: 142 us -> 0.01 us  [the longest x1 0.01 us: local(): pack = lax.all_gather(pack, 'fsdp', axis=0, tiled=False)]
    reduce_scatter x4 -> x3, waiting for transfers between devices: 146 us -> 6.98 us  [the longest x1 6.96 us: local(): lax.psum_scatter(grad_down, 'fsdp', scatter_dimension=0, tiled=False)]
    unnamed x15 -> x5, waiting for transfers between devices: 121 us -> 0.75 us
    all_to_all x0 -> x10, waiting for transfers between devices: none -> 108 us  [swap(): return lax.all_to_all(slots, axes, 0, 0, tiled=True)]
    dot_general x48 -> x1, matrix products: 89.6 us -> 3.53 us  [local(): lax.dot_general(active, my_cotangent, (((0,), (0,)), ((), ())), preferred...]
    pallas_call x0 -> x6, Pallas kernels: none -> 66.3 us  [the longest x1 24.7 us: head_forward(): vmem_call(kernel, [shape((CTX, HALF, 2 * DEPTH), BF), shape((SEQ, WIDTH),...]
    all_to_all x0 -> x4, blocking collectives: none -> 53.9 us  [swap(): return lax.all_to_all(slots, axes, 0, 0, tiled=True)]
    unnamed x2 -> x0, blocking collectives: 51.8 us -> none
  transfers between devices with their start and end apart: 13 -> 15, of which waited for: 11 -> 11; matrix products, arithmetic and copies ran while one was open for 14% -> 11% of each run, Pallas kernels for 0% -> 15%
where the time goes in v1:
time: 346 us; the launch traced here: 344 us
  waiting for transfers between devices  116 us (34%)
  Pallas kernels  66.3 us (19%)
  blocking collectives  53.9 us (16%)
  starting transfers between devices  43.4 us (13%)
  local copies, waits for them, and re-layouts  40.9 us (12%)
  between operations  14.3 us (4%)
  other arithmetic  5.65 us (2%)
  matrix products  3.53 us (1%)
    all_to_all x10, waiting for transfers between devices, swap(): return lax.all_to_all(slots, axes, 0, 0, tiled=True)  108 us
    all_to_all x4, blocking collectives, swap(): return lax.all_to_all(slots, axes, 0, 0, tiled=True)  53.9 us
    all_to_all x10, starting transfers between devices, swap(): return lax.all_to_all(slots, axes, 0, 0, tiled=True)  43.2 us
    pallas_call x1, Pallas kernels, head_forward(): vmem_call(kernel, [shape((CTX, HALF, 2 * DEPTH), BF), shape((SEQ, WIDTH),...  24.7 us
    pallas_call x1, Pallas kernels, head_backward(): vmem_call(kernel, [shape((CTX, HALF, 6 * DEPTH), BF), shape((FSDP, WIDTH...  18.9 us
    unnamed x49, local copies, waits for them, and re-layouts  14.7 us
    pallas_call x1, Pallas kernels, feed_forward(): vmem_call(kernel, [shape((ROWS, WIDTH), BF), shape((ROWS, WIDTH), BF), sh...  10.7 us
    pallas_call x2, Pallas kernels, weight_grads(): vmem_call(kernel, [jax.ShapeDtypeStruct((FSDP, 96 * blocks, WIDTH), BF)],...  7.4 us
  transfers between devices with their start and end apart: 15, of which 11 were waited for; matrix products, arithmetic and copies ran while one was open for 11% of the time, Pallas kernels for 15%

profile of v1, /device:TPU:0, one launch (start us, length us, event | category | flops | bytes accessed | tf_op | source)
XLA Modules:
  0.0 343.5 jit_solution(7103740989155309988)
XLA Ops:
  7.2 1.0 constant_dynamic-update-slice_fusion.1
  8.2 0.9 slice_dynamic-update-slice_fusion.3
  9.1 0.9 slice_dynamic-update-slice_fusion.2
  10.1 0.9 slice_dynamic-update-slice_fusion.1
  11.0 0.9 slice_dynamic-update-slice_fusion
  12.1 1.1 copy-done.3
  13.5 0.9 constant_dynamic-slice_fusion.4
  14.7 13.3 %all_to_all.70 = bf16[8,112,192]{1,2,0:T(8,128)(2,1)S(1)} all-to-all(bf16[8,112,192]{1,2,0:T(8,128)(2,1)S(1)} %broadcast_in_dim.24), channel_id=1, replica_groups=mesh['ctx'=16,'fsdp'=8] {'fsdp'}, dimensions={0} | all-to-all | bytes 688128 | tf_op jit(solution)/shard_map/gather_small/all_to_all | solution.py:448
  28.0 2.0 broadcast_in_dim.22
  30.0 7.9 %all-to-all-start = ((bf16[16,128,768]{2,1,0:T(8,128)(2,1)}), bf16[16,128,768]{2,1,0:T(8,128)(2,1)S(1)}, u32[]{:S(2)}, u32[]{:S(2)}) async-start(bf16[16,128,768]{2,1,0:T(8,128)(2,1)} %broadcast_in_dim.22), calls=%async_computation | async-start | bytes 6291456 | tf_op jit(solution)/shard_map/gather_tokens/all_to_all | solution.py:448
  38.5 0.9 slice.176
  39.4 1.8 copy.63
  41.3 1.4 copy.57
  42.6 1.5 reshape.218
  44.2 0.8 slice.177
  45.6 1.4 fusion.3
  47.1 1.4 reshape.196.gain
  48.4 1.3 reshape.197.shift
  49.8 1.0 copy.55
  50.7 0.7 constant_dynamic-slice_fusion.1
  51.5 1.2 pad_maximum_fusion.1.bias
  52.7 32.1 %all-to-all-done.tok = bf16[16,128,768]{2,1,0:T(8,128)(2,1)S(1)} async-done(((bf16[16,128,768]{2,1,0:T(8,128)(2,1)}), bf16[16,128,768]{2,1,0:T(8,128)(2,1)S(1)}, u32[]{:S(2)}, u32[]{:S(2)}) %all-to-all-start) | async-done | bytes 3145760 | tf_op jit(solution)/shard_map/gather_tokens/all_to_all | solution.py:448
  84.8 1.6 copy-done.1
  86.5 24.7 %attention.1 = (bf16[16,64,128]{2,1,0:T(8,128)(2,1)}, bf16[2048,768]{1,0:T(8,128)(2,1)}, bf16[2048,64]{1,0:T(8,128)(2,1)}, bf16[2048,64]{1,0:T(8,128)(2,1)}, bf1...) custom-call(s32[16]{0:T(128)} %order.3, ...), custom_call_target="tpu_custom_call" | custom-call | flops 2000000000 | bytes 8388608 | tf_op jit(solution)/shard_map/attention/pallas_call | solution.py:184
  111.2 4.1 %all-to-all-start.2 = ((bf16[16,64,128]{2,1,0:T(8,128)(2,1)}), bf16[16,64,128]{2,1,0:T(8,128)(2,1)S(1)}, u32[]{:S(2)}, u32[]{:S(2)}) async-start(bf16[16,64,128]{2,1,0:T(8,128)(2,1)} %get-tuple-element.38), calls=%async_computation.2 | async-start | bytes 524288 | tf_op jit(solution)/shard_map/attention/all_to_all | solution.py:448
  118.0 0.8 slice_bitcast_fusion.1
  119.4 4.6 %all-to-all-done.2.heads_out = bf16[16,64,128]{2,1,0:T(8,128)(2,1)S(1)} async-done(((bf16[16,64,128]{2,1,0:T(8,128)(2,1)}), bf16[16,64,128]{2,1,0:T(8,128)(2,1)S(1)}, u32[]{:S(2)}, u32[]{:S(2)}) %all-to-all-start.2) | async-done | bytes 262176 | tf_op jit(solution)/shard_map/attention/all_to_all | solution.py:448
  124.7 10.7 %feed_forward.1 = (bf16[128,768]{1,0:T(8,128)(2,1)}, bf16[128,768]{1,0:T(8,128)(2,1)}, bf16[128,768]{1,0:T(8,128)(2,1)}, bf16[128,3072]{1,0:T(8,128)(2,1)}, bf16...) custom-call(bf16[128,768]{1,0:T(8,128)(2,1)} %bitcast.53, ...), custom_call_target="tpu_custom_call" | custom-call | flops 4000000000 | bytes 8388608 | tf_op jit(solution)/shard_map/feed_forward/pallas_call | solution.py:391
  135.4 2.5 feed_forward_weights.2
  138.7 4.9 %feed_forward_weights.3 = bf16[8,384,768]{2,1,0:T(8,128)(2,1)} custom-call(bf16[128,768]{1,0:T(8,128)(2,1)} %get-tuple-element.59.left, bf16[128,3072]{1,0:T(8,128)(2,1)} %get-tuple-element.60.right), custom_call_target="tpu_custom_call" | custom-call | flops 603979776 | bytes 8388608 | tf_op jit(solution)/shard_map/feed_forward_weights/pallas_call | solution.py:417
  143.6 1.1 copy-done.2
  144.7 3.5 %convolution_convert_fusion = bf16[3072,768]{1,0:T(8,128)(2,1)} fusion(bf16[128,3072]{1,0:T(8,128)(2,1)S(1)} %copy-done.2, bf16[1,128,768]{2,1,0:T(8,128)(2,1)S(1)} %copy-done.8), kind=kOutput, calls=%fused_computation | convolution fusion | flops 606339072 | bytes 5701632 | tf_op jit(solution)/shard_map/feed_forward_weights/dot_general | solution.py:530
  148.3 0.9 copy-done.6
  149.2 11.9 %all_to_all.71.upstream = bf16[16,64,128]{2,1,0:T(8,128)(2,1)} all-to-all(bf16[16,64,128]{2,1,0:T(8,128)(2,1)S(1)} %copy-done.6), channel_id=1, replica_groups=mesh['ctx'=16,'fsdp'=8] {'ctx'}, dimensions={0} | all-to-all | bytes 524288 | tf_op jit(solution)/shard_map/feed_forward/all_to_all | solution.py:448
  161.2 18.9 %attention_back.1 = (bf16[16,64,384]{2,1,0:T(8,128)(2,1)}, bf16[8,96,192]{2,1,0:T(8,128)(2,1)}, f32[1,192]{1,0:T(1,128)}) custom-call(s32[16]{0:T(128)} %order.3, bf16[16,64,128]{2,1,0:T(8,128)(2,1)} %all_to_all.71.upstream, bf16[2048,768]{1,0:T(8,128)(2,1)} %get-tuple-element.41.normed, bf16[2048,64]{1,0:T(8,128)(2,1)} %get-tuple-element.42.query, ...), custom_call_target="tpu_custom_call" | custom-call | flops 4000000000 | bytes 8388608 | tf_op jit(solution)/shard_map/attention_back/pallas_call | solution.py:296
  180.1 17.0 %all_to_all.72 = bf16[8,96,192]{2,1,0:T(8,128)(2,1)S(1)} all-to-all(bf16[8,96,192]{2,1,0:T(8,128)(2,1)} %get-tuple-element.56), channel_id=1, replica_groups=mesh['ctx'=16,'fsdp'=8] {'fsdp'}, dimensions={0} | all-to-all | bytes 589824 | tf_op jit(solution)/shard_map/head_weights/all_to_all | solution.py:448
  197.1 3.6 %all-to-all-start.4 = ((bf16[16,64,384]{2,1,0:T(8,128)(2,1)}), bf16[16,64,384]{2,1,0:T(8,128)(2,1)S(1)}, u32[]{:S(2)}, u32[]{:S(2)}) async-start(bf16[16,64,384]{2,1,0:T(8,128)(2,1)} %get-tuple-element.49), calls=%async_computation.4 | async-start | bytes 1572864 | tf_op jit(solution)/shard_map/attention_back/all_to_all | solution.py:448
  200.9 13.9 %all-to-all-done.4.heads_grad = bf16[16,64,384]{2,1,0:T(8,128)(2,1)S(1)} async-done(((bf16[16,64,384]{2,1,0:T(8,128)(2,1)}), bf16[16,64,384]{2,1,0:T(8,128)(2,1)S(1)}, u32[]{:S(2)}, u32[]{:S(2)}) %all-to-all-start.4) | async-done | bytes 786464 | tf_op jit(solution)/shard_map/attention_back/all_to_all | solution.py:448
  214.8 1.1 broadcast_in_dim.29
  216.0 3.6 %all-to-all-start.7 = ((bf16[16,96,192]{1,2,0:T(8,128)(2,1)}), bf16[16,96,192]{1,2,0:T(8,128)(2,1)S(1)}, u32[]{:S(2)}, u32[]{:S(2)}) async-start(bf16[16,96,192]{1,2,0:T(8,128)(2,1)} %broadcast_in_dim.29), calls=%async_computation.7 | async-start | bytes 1572864 | tf_op jit(solution)/shard_map/head_weights/all_to_all | solution.py:448
  220.1 1.6 pad_bitcast_fusion
  221.7 11.4 %all-to-all-done.7 = bf16[16,96,192]{1,2,0:T(8,128)(2,1)S(1)} async-done(((bf16[16,96,192]{1,2,0:T(8,128)(2,1)}), bf16[16,96,192]{1,2,0:T(8,128)(2,1)S(1)}, u32[]{:S(2)}, u32[]{:S(2)}) %all-to-all-start.7) | async-done | bytes 589856 | tf_op jit(solution)/shard_map/head_weights/all_to_all | solution.py:448
  233.2 3.5 %all-to-all-start.8 = ((bf16[16,8,768]{2,1,0:T(8,128)(2,1)}), bf16[16,8,768]{2,1,0:T(8,128)(2,1)S(1)}, u32[]{:S(2)}, u32[]{:S(2)}) async-start(bf16[16,8,768]{2,1,0:T(8,128)(2,1)} %pad_bitcast_fusion), calls=%async_computation.9 | async-start | bytes 393216 | tf_op jit(solution)/shard_map/sum_over_ctx/all_to_all | solution.py:448
  237.1 4.6 %token_gradient.1 = (f32[128,768]{1,0:T(8,128)}, f32[2,768]{1,0:T(2,128)}) custom-call(bf16[128,768]{1,0:T(8,128)(2,1)} %bitcast.54, bf16[16,64,384]{2,1,0:T(8,128)(2,1)} %copy-done, bf16[768,2304]{1,0:T(8,128)(2,1)} %all-gather.4.cloned.1.call-done.weight, f32[1,768]{1,0:T(1,128)} %reshape.196.gain, f32[128,768]{1,0:T(8,128)} %get-tuple-element.50.grad_residual), custom_call_target="tpu_custom_call" | custom-call | flops 452984832 | bytes 8388608 | tf_op jit(solution)/shard_map/token_gradient/pallas_call | solution.py:438
  242.7 2.3 all-to-all-done.8
  245.0 0.9 broadcast_in_dim.28
  245.9 6.1 %all-to-all-start.5 = ((bf16[128,9,128]{2,1,0:T(8,128)(2,1)}), bf16[128,9,128]{2,1,0:T(8,128)(2,1)S(1)}, u32[]{:S(2)}, u32[]{:S(2)}) async-start(bf16[128,9,128]{2,1,0:T(8,128)(2,1)} %bitcast.9), calls=%async_computation.5 | async-start | bytes 1048576 | tf_op jit(solution)/shard_map/vector_grads/all_to_all | solution.py:448
  252.0 13.5 %all-to-all-done.5 = bf16[128,9,128]{2,1,0:T(8,128)(2,1)S(1)} async-done(((bf16[128,9,128]{2,1,0:T(8,128)(2,1)}), bf16[128,9,128]{2,1,0:T(8,128)(2,1)S(1)}, u32[]{:S(2)}, u32[]{:S(2)}) %all-to-all-start.5) | async-done | bytes 294944 | tf_op jit(solution)/shard_map/vector_grads/all_to_all | solution.py:448
  265.5 11.7 %all_to_all.73 = bf16[16,8,768]{2,1,0:T(8,128)(2,1)S(1)} all-to-all(bf16[16,8,768]{2,1,0:T(8,128)(2,1)S(1)} %broadcast_in_dim.30), channel_id=1, replica_groups=mesh['ctx'=16,'fsdp'=8] {'ctx'}, dimensions={0} | all-to-all | bytes 393216 | tf_op jit(solution)/shard_map/sum_over_ctx/all_to_all | solution.py:448
  277.2 3.6 %all-to-all-start.10 = ((bf16[16,24,768]{2,1,0:T(8,128)(2,1)}), bf16[16,24,768]{2,1,0:T(8,128)(2,1)S(1)}, u32[]{:S(2)}, u32[]{:S(2)}) async-start(bf16[16,24,768]{2,1,0:T(8,128)(2,1)} %bitcast.57), calls=%async_computation.12 | async-start | bytes 1179648 | tf_op jit(solution)/shard_map/sum_over_ctx/all_to_all | solution.py:448
  280.8 7.0 %reduce-scatter.8.cloned.1.call-done = bf16[1,384,768]{2,1,0:T(8,128)(2,1)} async-done(((bf16[8,384,768]{2,1,0:T(8,128)(2,1)}), bf16[1,384,768]{2,1,0:T(8,128)(2,1)}) %reduce-scatter.8.cloned.1.call-update) | async-done | bytes 589840 | tf_op jit(solution)/shard_map/feed_forward_weights/reduce_scatter | solution.py:533
  287.7 4.3 %all-to-all-done.10 = bf16[16,24,768]{2,1,0:T(8,128)(2,1)S(1)} async-done(((bf16[16,24,768]{2,1,0:T(8,128)(2,1)}), bf16[16,24,768]{2,1,0:T(8,128)(2,1)S(1)}, u32[]{:S(2)}, u32[]{:S(2)}) %all-to-all-start.10) | async-done | bytes 589856 | tf_op jit(solution)/shard_map/sum_over_ctx/all_to_all | solution.py:448
  292.0 3.6 %all-to-all-start.12 = ((bf16[16,24,768]{2,1,0:T(8,128)(2,1)}), bf16[16,24,768]{2,1,0:T(8,128)(2,1)S(1)}, u32[]{:S(2)}, u32[]{:S(2)}) async-start(bf16[16,24,768]{2,1,0:T(8,128)(2,1)} %bitcast.56), calls=%async_computation.15 | async-start | bytes 1179648 | tf_op jit(solution)/shard_map/sum_over_ctx/all_to_all | solution.py:448
  295.9 1.3 copy.62
  297.2 8.8 %all-to-all-done.12 = bf16[16,24,768]{2,1,0:T(8,128)(2,1)S(1)} async-done(((bf16[16,24,768]{2,1,0:T(8,128)(2,1)}), bf16[16,24,768]{2,1,0:T(8,128)(2,1)S(1)}, u32[]{:S(2)}, u32[]{:S(2)}) %all-to-all-start.12) | async-done | bytes 589856 | tf_op jit(solution)/shard_map/sum_over_ctx/all_to_all | solution.py:448
  306.1 0.9 broadcast_in_dim.31
  306.9 3.6 %all-to-all-start.11 = ((bf16[16,24,768]{2,1,0:T(8,128)(2,1)}), bf16[16,24,768]{2,1,0:T(8,128)(2,1)S(1)}, u32[]{:S(2)}, u32[]{:S(2)}) async-start(bf16[16,24,768]{2,1,0:T(8,128)(2,1)} %broadcast_in_dim.31), calls=%async_computation.13 | async-start | bytes 1179648 | tf_op jit(solution)/shard_map/sum_over_ctx/all_to_all | solution.py:448
  312.5 0.7 fusion
  313.3 7.7 %all-to-all-done.11 = bf16[16,24,768]{2,1,0:T(8,128)(2,1)S(1)} async-done(((bf16[16,24,768]{2,1,0:T(8,128)(2,1)}), bf16[16,24,768]{2,1,0:T(8,128)(2,1)S(1)}, u32[]{:S(2)}, u32[]{:S(2)}) %all-to-all-start.11) | async-done | bytes 589856 | tf_op jit(solution)/shard_map/sum_over_ctx/all_to_all | solution.py:448
  321.0 0.9 broadcast_in_dim.64
  321.8 3.6 %all-to-all-start.13 = ((bf16[16,24,768]{2,1,0:T(8,128)(2,1)}), bf16[16,24,768]{2,1,0:T(8,128)(2,1)S(1)}, u32[]{:S(2)}, u32[]{:S(2)}) async-start(bf16[16,24,768]{2,1,0:T(8,128)(2,1)} %broadcast_in_dim.64), calls=%async_computation.16 | async-start | bytes 1179648 | tf_op jit(solution)/shard_map/sum_over_ctx/all_to_all | solution.py:448
  325.5 1.1 pad_maximum_fusion
  326.7 9.2 %all-to-all-done.13 = bf16[16,24,768]{2,1,0:T(8,128)(2,1)S(1)} async-done(((bf16[16,24,768]{2,1,0:T(8,128)(2,1)}), bf16[16,24,768]{2,1,0:T(8,128)(2,1)S(1)}, u32[]{:S(2)}, u32[]{:S(2)}) %all-to-all-start.13) | async-done | bytes 589856 | tf_op jit(solution)/shard_map/sum_over_ctx/all_to_all | solution.py:448
  335.9 1.1 bitcast_convert_fusion
  (101 shorter events, 11.4 us)
Async XLA Ops:
  7.2 4.7 %copy-start.5 = (bf16[384,768]{1,0:T(8,128)(2,1)S(1)}, bf16[384,768]{1,0:T(8,128)(2,1)}, u32[]{:S(2)}) copy-start(bf16[384,768]{1,0:T(8,128)(2,1)} %param.28) | copy-start | bytes 1769476
  7.2 116.8 %all-gather.6.cloned.1.call-start = ((), (), s32[]{:S(2)}) async-start(), calls=%async_computation.21 | async-start | bytes 11943936 | tf_op jit(solution)/shard_map/gather_weights/all_gather | solution.py:483
  11.9 1.3 copy-start.11
  11.9 1.3 copy-start.13
  12.0 1.3 copy-start.14
  12.0 1.3 copy-start.15
  12.0 1.3 copy-start.16
  12.0 1.3 copy-start.17
  12.0 1.3 copy-start.18
  12.0 1.3 copy-start.19
  12.1 1.1 copy-start.3
  12.1 15.9 %copy-start.4 = (bf16[1,128,768]{2,1,0:T(8,128)(2,1)S(1)}, bf16[1,128,768]{2,1,0:T(8,128)(2,1)}, u32[]{:S(2)}) copy-start(bf16[1,128,768]{2,1,0:T(8,128)(2,1)} %param.15) | copy-start | bytes 589828
  30.0 54.9 %all-to-all-start = ((bf16[16,128,768]{2,1,0:T(8,128)(2,1)}), bf16[16,128,768]{2,1,0:T(8,128)(2,1)S(1)}, u32[]{:S(2)}, u32[]{:S(2)}) async-start(bf16[16,128,768]{2,1,0:T(8,128)(2,1)} %broadcast_in_dim.22), calls=%async_computation | async-start | bytes 6291456 | tf_op jit(solution)/shard_map/gather_tokens/all_to_all | solution.py:448
  84.8 1.6 copy-start.1
  111.2 12.8 %all-to-all-start.2 = ((bf16[16,64,128]{2,1,0:T(8,128)(2,1)}), bf16[16,64,128]{2,1,0:T(8,128)(2,1)S(1)}, u32[]{:S(2)}, u32[]{:S(2)}) async-start(bf16[16,64,128]{2,1,0:T(8,128)(2,1)} %get-tuple-element.38), calls=%async_computation.2 | async-start | bytes 524288 | tf_op jit(solution)/shard_map/attention/all_to_all | solution.py:448
  115.3 104.8 %reduce-scatter.4.cloned.1.call-start = ((), (), s32[]{:S(2)}) async-start(), calls=%async_computation.18 | async-start | bytes 1327104 | tf_op jit(solution)/shard_map/feed_forward_weights/reduce_scatter | solution.py:537
  124.0 0.7 copy-start.7
  137.9 99.2 %all-gather.4.cloned.1.call-start = ((), (), s32[]{:S(2)}) async-start(), calls=%async_computation.17 | async-start | bytes 3981312 | tf_op jit(solution)/shard_map/gather_weights/all_gather | solution.py:484
  138.7 138.5 %reduce-scatter.6.cloned.1.call-start = ((), (), s32[]{:S(2)}) async-start(), calls=%async_computation.19 | async-start | bytes 5308416 | tf_op jit(solution)/shard_map/feed_forward_weights/reduce_scatter | solution.py:535
  143.6 1.1 copy-start.2
  143.6 1.2 copy-start.8
  143.6 144.1 %reduce-scatter.8.cloned.1.call-start = ((), (), s32[]{:S(2)}) async-start(), calls=%async_computation.20 | async-start | bytes 5308416 | tf_op jit(solution)/shard_map/feed_forward_weights/reduce_scatter | solution.py:533
  148.3 1.0 copy-start.6
  180.1 20.6 %copy-start.10 = (f32[4,768]{1,0:T(4,128)S(1)}, f32[4,768]{1,0:T(4,128)}, u32[]{:S(2)}) copy-start(f32[4,768]{1,0:T(4,128)} %get-tuple-element.54) | copy-start | bytes 36868
  197.1 17.8 %all-to-all-start.4 = ((bf16[16,64,384]{2,1,0:T(8,128)(2,1)}), bf16[16,64,384]{2,1,0:T(8,128)(2,1)S(1)}, u32[]{:S(2)}, u32[]{:S(2)}) async-start(bf16[16,64,384]{2,1,0:T(8,128)(2,1)} %get-tuple-element.49), calls=%async_computation.4 | async-start | bytes 1572864 | tf_op jit(solution)/shard_map/attention_back/all_to_all | solution.py:448
  200.8 19.2 %copy-start.9 = (f32[1,3072]{1,0:T(1,128)S(1)}, f32[1,3072]{1,0:T(1,128)}, u32[]{:S(2)}) copy-start(f32[1,3072]{1,0:T(1,128)} %get-tuple-element.55) | copy-start | bytes 36868
  200.8 19.2 %copy-start.12 = (f32[1,192]{1,0:T(1,128)S(1)}, f32[1,192]{1,0:T(1,128)}, u32[]{:S(2)}) copy-start(f32[1,192]{1,0:T(1,128)} %get-tuple-element.53) | copy-start | bytes 2308
  214.8 6.9 %copy-start = (bf16[16,64,384]{2,1,0:T(8,128)(2,1)}, bf16[16,64,384]{2,1,0:T(8,128)(2,1)S(1)}, u32[]{:S(2)}) copy-start(bf16[16,64,384]{2,1,0:T(8,128)(2,1)S(1)} %all-to-all-done.4.heads_grad) | copy-start | bytes 2359300
  216.0 17.2 %all-to-all-start.7 = ((bf16[16,96,192]{1,2,0:T(8,128)(2,1)}), bf16[16,96,192]{1,2,0:T(8,128)(2,1)S(1)}, u32[]{:S(2)}, u32[]{:S(2)}) async-start(bf16[16,96,192]{1,2,0:T(8,128)(2,1)} %broadcast_in_dim.29), calls=%async_computation.7 | async-start | bytes 1572864 | tf_op jit(solution)/shard_map/head_weights/all_to_all | solution.py:448
  233.2 11.8 %all-to-all-start.8 = ((bf16[16,8,768]{2,1,0:T(8,128)(2,1)}), bf16[16,8,768]{2,1,0:T(8,128)(2,1)S(1)}, u32[]{:S(2)}, u32[]{:S(2)}) async-start(bf16[16,8,768]{2,1,0:T(8,128)(2,1)} %pad_bitcast_fusion), calls=%async_computation.9 | async-start | bytes 393216 | tf_op jit(solution)/shard_map/sum_over_ctx/all_to_all | solution.py:448
  245.9 19.6 %all-to-all-start.5 = ((bf16[128,9,128]{2,1,0:T(8,128)(2,1)}), bf16[128,9,128]{2,1,0:T(8,128)(2,1)S(1)}, u32[]{:S(2)}, u32[]{:S(2)}) async-start(bf16[128,9,128]{2,1,0:T(8,128)(2,1)} %bitcast.9), calls=%async_computation.5 | async-start | bytes 1048576 | tf_op jit(solution)/shard_map/vector_grads/all_to_all | solution.py:448
  277.2 14.8 %all-to-all-start.10 = ((bf16[16,24,768]{2,1,0:T(8,128)(2,1)}), bf16[16,24,768]{2,1,0:T(8,128)(2,1)S(1)}, u32[]{:S(2)}, u32[]{:S(2)}) async-start(bf16[16,24,768]{2,1,0:T(8,128)(2,1)} %bitcast.57), calls=%async_computation.12 | async-start | bytes 1179648 | tf_op jit(solution)/shard_map/sum_over_ctx/all_to_all | solution.py:448
  292.0 14.1 %all-to-all-start.12 = ((bf16[16,24,768]{2,1,0:T(8,128)(2,1)}), bf16[16,24,768]{2,1,0:T(8,128)(2,1)S(1)}, u32[]{:S(2)}, u32[]{:S(2)}) async-start(bf16[16,24,768]{2,1,0:T(8,128)(2,1)} %bitcast.56), calls=%async_computation.15 | async-start | bytes 1179648 | tf_op jit(solution)/shard_map/sum_over_ctx/all_to_all | solution.py:448
  306.9 14.0 %all-to-all-start.11 = ((bf16[16,24,768]{2,1,0:T(8,128)(2,1)}), bf16[16,24,768]{2,1,0:T(8,128)(2,1)S(1)}, u32[]{:S(2)}, u32[]{:S(2)}) async-start(bf16[16,24,768]{2,1,0:T(8,128)(2,1)} %broadcast_in_dim.31), calls=%async_computation.13 | async-start | bytes 1179648 | tf_op jit(solution)/shard_map/sum_over_ctx/all_to_all | solution.py:448
  321.8 14.0 %all-to-all-start.13 = ((bf16[16,24,768]{2,1,0:T(8,128)(2,1)}), bf16[16,24,768]{2,1,0:T(8,128)(2,1)S(1)}, u32[]{:S(2)}, u32[]{:S(2)}) async-start(bf16[16,24,768]{2,1,0:T(8,128)(2,1)} %broadcast_in_dim.64), calls=%async_computation.16 | async-start | bytes 1179648 | tf_op jit(solution)/shard_map/sum_over_ctx/all_to_all | solution.py:448
Sparse Core Ops, SparseCore 0:
  13.3 61.5 all-gather.5
  138.0 28.4 reduce-scatter.3
  168.3 32.7 all-gather.3
  203.3 39.0 reduce-scatter.5
  244.6 43.0 reduce-scatter.7

commit v2 on v1

--- a/solution.py
+++ b/solution.py
@@ -13,8 +13,9 @@
 HALF = 64
 CTX = 16
 FSDP = 8
+SIDE = 4
 SEQ = CTX * ROWS
-QT = 256
+QT = 512
 KT = 512
 EPSILON = 1e-05
 NEGATIVE = -1e30
@@ -36,6 +37,8 @@
 VECTOR_WIDTH = sum(width for _, width in VECTORS)
 
 OUT_AT, UP_AT, DOWN_AT, PACK_ROWS = 0, 96, 480, 864
+CTX_ROWS = PACK_ROWS // CTX
+LAST_ROWS = CTX_ROWS + 26
 
 
 def dot(left, right):
@@ -64,18 +67,30 @@
     return (scaled - mean_one - hat * mean_two) * inverse
 
 
+UNROLL = True
+
+
+def loop(count, body):
+    if UNROLL:
+        for step in range(count):
+            body(step, 0)
+    else:
+        lax.fori_loop(0, count, body, 0)
+
+
 def block_at(index):
     return pl.ds(pl.multiple_of(index * HALF, HALF), HALF)
 
 
 def lanes_at(index, size):
+    if isinstance(index, int):
+        return pl.ds(index * size, size)
     return pl.ds(pl.multiple_of(index * size, size), size)
 
 
-def vmem_call(kernel, out_shape, scratch, flops, in_vmem, smem_first=False, transcendentals=0):
+def vmem_call(kernel, out_shape, scratch, flops, in_vmem, smem=0, transcendentals=0):
     specs = [pl.BlockSpec(memory_space=pltpu.VMEM)] * in_vmem
-    if smem_first:
-        specs = [pl.BlockSpec(memory_space=pltpu.SMEM)] + specs
+    specs = [pl.BlockSpec(memory_space=pltpu.SMEM)] * smem + specs
     return pl.pallas_call(
         kernel,
         out_shape=out_shape,
@@ -89,25 +104,35 @@
     )
 
 
+def normalised_rows(tokens):
+    def kernel(tokens, hat):
+        hat[...] = normalise(tokens[...].astype(F32))[0].astype(BF)
+
+    return vmem_call(
+        kernel, [jax.ShapeDtypeStruct((ROWS, WIDTH), BF)], [], 10**6, 1
+    )(tokens)[0]
+
+
 def head_forward_kernel(
-    order, tok, weight, bias, gain, shift,
+    order, where, blocks, weight, bias, gain, shift,
     packed, normed, query, key, value, query_t, key_t, out_t, lse,
     value_t,
 ):
-    def project(c, _):
-        hat, _inv = normalise(tok[c].astype(F32))
+    at_z, at_x = where[0] // SIDE, lax.rem(where[0], SIDE)
+
+    for half, offsets, block in blocks:
+        count = len(offsets)
+        hat = block[...].reshape(count * HALF, WIDTH).astype(F32)
         low = (hat * gain[...] + shift[...]).astype(BF)
         made = (dot(low, weight[...]) + bias[...]).astype(BF)
-        place = order[c]
-        for part, block in ((0, place), (1, 2 * CTX - 1 - place)):
-            rows = slice(part * HALF, (part + 1) * HALF)
-            normed[block_at(block), :] = low[rows]
-            query[block_at(block), :] = made[rows, 0:DEPTH]
-            key[block_at(block), :] = made[rows, DEPTH : 2 * DEPTH]
-            value[block_at(block), :] = made[rows, 2 * DEPTH :]
-        return 0
-
-    lax.fori_loop(0, CTX, project, 0)
+        for n, (dz, dx) in enumerate(offsets):
+            place = order[lax.rem(at_z + dz, SIDE) * SIDE + lax.rem(at_x + dx, SIDE)]
+            to = block_at(place if half == 0 else 2 * CTX - 1 - place)
+            rows = slice(n * HALF, (n + 1) * HALF)
+            normed[to, :] = low[rows]
+            query[to, :] = made[rows, 0:DEPTH]
+            key[to, :] = made[rows, DEPTH : 2 * DEPTH]
+            value[to, :] = made[rows, 2 * DEPTH :]
 
     def turn(t, _):
         rows = lanes_at(t, QT)
@@ -141,25 +166,38 @@
             jnp.zeros((1, QT), F32),
             jnp.zeros((DEPTH, QT), F32),
         )
-        full = i // 2
-        carry = lax.fori_loop(0, full, lambda j, carry: step(j, carry, False), start)
-        top, total, acc = step(full, carry, True)
+        full = i * QT // KT
+        if isinstance(i, int):
+            carry = start
+            for j in range(full):
+                carry = step(j, carry, False)
+        else:
+            carry = lax.fori_loop(0, full, lambda j, carry: step(j, carry, False), start)
+        for extra in range(max(1, QT // KT)):
+            carry = step(full + extra, carry, True)
+        top, total, acc = carry
         result = acc / total
         out_t[:, lanes] = result
         lse[pl.ds(i, 1), :] = top + jnp.log(total)
         return 0
 
-    lax.fori_loop(0, SEQ // QT, attend, 0)
-
-
-def head_forward(order, tok, weight, bias, gain, shift):
-    def kernel(
-        order, tok, weight, bias, gain, shift,
-        packed, normed, query, key, value, query_t, key_t, out_t, lse,
-        value_t, out_rows,
-    ):
+    loop(SEQ // QT, attend)
+
+
+def head_forward(order, where, blocks, weight, bias, gain, shift):
+    layout = [(half, offsets) for half, offsets, _ in blocks]
+
+    def kernel(order, where, *refs):
+        block_refs, refs = refs[: len(layout)], refs[len(layout) :]
+        (
+            weight, bias, gain, shift,
+            packed, normed, query, key, value, query_t, key_t, out_t, lse,
+            value_t, out_rows,
+        ) = refs
         head_forward_kernel(
-            order, tok, weight, bias, gain, shift,
+            order, where,
+            [(half, offsets, ref) for (half, offsets), ref in zip(layout, block_refs)],
+            weight, bias, gain, shift,
             packed, normed, query, key, value, query_t, key_t, out_t, lse,
             value_t,
         )
@@ -196,16 +234,16 @@
         ],
         [pltpu.VMEM((DEPTH, SEQ), BF), pltpu.VMEM((SEQ, DEPTH), F32)],
         2 * 10**9,
-        5,
-        smem_first=True,
+        len(blocks) + 4,
+        smem=2,
         transcendentals=3 * 10**6,
-    )(order, tok, weight, bias, gain, shift)
-
-
-def head_backward(order, upstream, normed, query, key, value, query_t, key_t, out_t, lse):
+    )(order, where, *[block for _, _, block in blocks], weight, bias, gain, shift)
+
+
+def head_backward(order, upstream, query, key, value, query_t, key_t, out_t, lse):
     def kernel(
-        order, upstream, normed, query, key, value, query_t, key_t, out_t, lse,
-        packed, weight_grad, bias_grad,
+        order, upstream, query, key, value, query_t, key_t, out_t, lse,
+        packed, low_rows, bias_grad,
         grad_out, grad_out_t, delta, grad_q_t, grad_k, grad_v, rows_low,
     ):
         def unpack(c, _):
@@ -247,17 +285,18 @@
                 grad_k[rows, :] += dot(grad_scores, query[lanes, :])
                 grad_q_t[:, lanes] += dot(key_t[:, rows], grad_scores)
 
-            full = i // 2
+            full = i * QT // KT
 
             def body(j, _):
                 step(j, False)
                 return 0
 
-            lax.fori_loop(0, full, body, 0)
-            step(full, True)
+            (loop(full, body) if isinstance(i, int) else lax.fori_loop(0, full, body, 0))
+            for extra in range(max(1, QT // KT)):
+                step(full + extra, True)
             return 0
 
-        lax.fori_loop(0, SEQ // QT, one_query_tile, 0)
+        loop(SEQ // QT, one_query_tile)
 
         def finish(t, sums):
             rows = lanes_at(t, QT)
@@ -268,16 +307,11 @@
                 [low_q.astype(F32), low_k.astype(F32), low_v.astype(F32)], axis=1
             )
             rows_low[rows, :] = joined
+            low_rows[rows, :] = joined.astype(BF)
             return sums + jnp.sum(joined, axis=0, keepdims=True)
 
         sums = lax.fori_loop(0, SEQ // QT, finish, jnp.zeros((1, 3 * DEPTH), F32))
         bias_grad[...] = sums
-
-        weight_grad[...] = (
-            dot_tn(normed[...], rows_low[...].astype(BF))
-            .astype(BF)
-            .reshape(FSDP, WIDTH // FSDP, 3 * DEPTH)
-        )
 
         def pack(c, _):
             place = order[c]
@@ -297,7 +331,7 @@
         kernel,
         [
             shape((CTX, HALF, 6 * DEPTH), BF),
-            shape((FSDP, WIDTH // FSDP, 3 * DEPTH), BF),
+            shape((SEQ, 3 * DEPTH), BF),
             shape((1, 3 * DEPTH), F32),
         ],
         [
@@ -310,10 +344,25 @@
             pltpu.VMEM((SEQ, 3 * DEPTH), F32),
         ],
         4 * 10**9,
-        9,
-        smem_first=True,
+        8,
+        smem=1,
         transcendentals=3 * 10**6,
-    )(order, upstream, normed, query, key, value, query_t, key_t, out_t, lse)
+    )(order, upstream, query, key, value, query_t, key_t, out_t, lse)
+
+
+def head_weight_grad(normed, rows):
+    def kernel(normed, rows, out):
+        out[...] = (
+            dot_tn(normed[...], rows[...]).astype(BF).reshape(FSDP, WIDTH // FSDP, 3 * DEPTH)
+        )
+
+    return vmem_call(
+        kernel,
+        [jax.ShapeDtypeStruct((FSDP, WIDTH // FSDP, 3 * DEPTH), BF)],
+        [],
+        2 * SEQ * WIDTH * 3 * DEPTH,
+        2,
+    )(normed, rows)[0]
 
 
 def unpack_heads(ref, lanes):
@@ -342,18 +391,16 @@
 def feed_forward(tokens, heads_out, cotangent, pack, out_bias, gain, shift, up_bias, down_bias):
     def kernel(
         tokens, heads_out, cotangent, pack, out_bias, gain, shift, up_bias, down_bias,
-        mixed, attended, normed, active, grad_pre, grad_branch, grad_heads, grad_residual,
-        vector_sums, up_sums,
+        mixed, pack_grad, grad_heads, grad_residual, vector_sums, up_sums,
     ):
         inputs = tokens[...].astype(F32)
         result_grad = cotangent[...]
         attended_low = unpack_heads(heads_out, 0)
-        attended[...] = attended_low
         w_out = pack[:, OUT_AT:UP_AT, :].reshape(WIDTH, WIDTH)
         residual = inputs + dot(attended_low, w_out) + out_bias[...]
         hat, inverse = normalise(residual)
         low = (hat * gain[...] + shift[...]).astype(BF)
-        normed[...] = low
+        low_t = low.T
         total = residual + down_bias[...]
         grad_normed = jnp.zeros((ROWS, WIDTH), F32)
         for j in range(HIDDEN // WIDTH):
@@ -363,17 +410,23 @@
             hidden = dot(low, w_up) + up_bias[:, lanes]
             acted, slope = gelu_parts(hidden)
             acted = acted.astype(BF)
-            active[:, lanes] = acted
+            pack_grad[2 * j : 2 * j + 2, DOWN_AT:PACK_ROWS, :] = (
+                dot(acted.T, result_grad).astype(BF).reshape(2, 384, WIDTH)
+            )
             total = total + dot(acted, w_down)
             pre = (dot_nt(result_grad, w_down) * slope).astype(BF)
-            grad_pre[:, lanes] = pre
+            pack_grad[:, UP_AT + 96 * j : UP_AT + 96 * (j + 1), :] = (
+                dot(low_t, pre).astype(BF).reshape(FSDP, 96, WIDTH)
+            )
             up_sums[:, lanes] = jnp.sum(pre.astype(F32), axis=0, keepdims=True)
             grad_normed = grad_normed + dot_nt(pre, w_up)
         mixed[...] = total.astype(BF)
         back = result_grad.astype(F32) + norm_back(grad_normed, hat, inverse, gain[...])
         grad_residual[...] = back
         branch = back.astype(BF)
-        grad_branch[...] = branch
+        pack_grad[:, OUT_AT:UP_AT, :] = (
+            dot(attended_low.T, branch).astype(BF).reshape(FSDP, 96, WIDTH)
+        )
         vector_sums[0:1, :] = jnp.sum(branch.astype(F32), axis=0, keepdims=True)
         vector_sums[1:2, :] = jnp.sum(grad_normed * hat, axis=0, keepdims=True)
         vector_sums[2:3, :] = jnp.sum(grad_normed, axis=0, keepdims=True)
@@ -392,11 +445,7 @@
         kernel,
         [
             shape((ROWS, WIDTH), BF),
-            shape((ROWS, WIDTH), BF),
-            shape((ROWS, WIDTH), BF),
-            shape((ROWS, HIDDEN), BF),
-            shape((ROWS, HIDDEN), BF),
-            shape((ROWS, WIDTH), BF),
+            shape((FSDP, PACK_ROWS, WIDTH), BF),
             shape((CTX, HALF, 2 * DEPTH), BF),
             shape((ROWS, WIDTH), F32),
             shape((4, WIDTH), F32),
@@ -408,21 +457,6 @@
     )(tokens, heads_out, cotangent, pack, out_bias, gain, shift, up_bias, down_bias)
 
 
-def weight_grads(left, right, blocks):
-    def kernel(left, right, out):
-        for j in range(blocks):
-            made = dot_tn(left[...], right[:, j * WIDTH : (j + 1) * WIDTH])
-            out[:, 96 * j : 96 * (j + 1), :] = made.astype(BF).reshape(FSDP, 96, WIDTH)
-
-    return vmem_call(
-        kernel,
-        [jax.ShapeDtypeStruct((FSDP, 96 * blocks, WIDTH), BF)],
-        [],
-        2 * ROWS * WIDTH * WIDTH * blocks,
-        2,
-    )(left, right)[0]
-
-
 def token_gradient(tokens, heads_grad, weight, gain, grad_residual):
     def kernel(tokens, heads_grad, weight, gain, grad_residual, tokens_grad, sums):
         projected = jnp.concatenate(
@@ -444,19 +478,183 @@
     )(tokens, heads_grad, weight, gain, grad_residual)
 
 
+def small_slots(place, weight_grad, bias_sums, first_sums, vector_sums, up_sums):
+    def kernel(place, weight_grad, bias_sums, first_sums, vector_sums, up_sums, slots):
+        slots[:, :96, :] = weight_grad[...]
+        tall = jnp.zeros((2, 3 * DEPTH), F32)
+        bias_rows = []
+        for part in (0, 2):
+            piece = bias_sums[:, part * DEPTH : (part + 1) * DEPTH]
+            for head in range(HEADS):
+                bias_rows.append(jnp.where(place[0] == head, piece, 0.0))
+        for owner in range(FSDP):
+            lanes = slice(96 * owner, 96 * (owner + 1))
+            values = dict(
+                first_gain=first_sums[0:1, lanes],
+                first_shift=first_sums[1:2, lanes],
+                qv_bias=jnp.concatenate(bias_rows[3 * owner : 3 * owner + 3], axis=1),
+                out_bias=vector_sums[0:1, lanes],
+                second_gain=vector_sums[1:2, lanes],
+                second_shift=vector_sums[2:3, lanes],
+                up_bias=up_sums[:, 384 * owner : 384 * (owner + 1)],
+                down_bias=vector_sums[3:4, lanes],
+            )
+            line = jnp.concatenate([values[name] for name, _ in VECTORS], axis=1)
+            rows = [line[:, 192 * r : 192 * (r + 1)] for r in range(6)]
+            slots[owner, 96:104, :] = jnp.concatenate(rows + [tall], axis=0).astype(BF)
+
+    return vmem_call(
+        kernel,
+        [jax.ShapeDtypeStruct((FSDP, 104, 3 * DEPTH), BF)],
+        [],
+        10**6,
+        5,
+        smem=1,
+    )(place, weight_grad, bias_sums, first_sums, vector_sums, up_sums)[0]
+
+
+def last_pieces(parts, smalls):
+    def kernel(parts, own, left, right, far, out):
+        total = parts[0].astype(F32)
+        for source in range(1, CTX):
+            total = total + parts[source].astype(F32)
+        small = (
+            own[...].astype(F32) + left[...].astype(F32) + right[...].astype(F32)
+            + far[...].astype(F32)
+        )
+        wide = jnp.concatenate([small[24 * k : 24 * (k + 1)] for k in range(4)], axis=1)
+        line = jnp.concatenate(
+            [
+                jnp.concatenate([small[96 + r : 97 + r] for r in range(4)], axis=1),
+                jnp.concatenate(
+                    [small[100:101], small[101:102], jnp.zeros((1, 6 * DEPTH), F32)], axis=1
+                ),
+            ],
+            axis=0,
+        )
+        joined = jnp.concatenate([total, wide, line], axis=0).astype(BF)
+        for target in range(CTX):
+            out[target] = joined
+
+    return vmem_call(
+        kernel,
+        [jax.ShapeDtypeStruct((CTX, LAST_ROWS, WIDTH), BF)],
+        [],
+        10**6,
+        5,
+    )(parts, *smalls)[0]
+
+
+def final_grads(pieces):
+    def kernel(pieces, grad_qkv, grad_out, grad_up, grad_down, *vector_refs):
+        shard = jnp.concatenate([pieces[n][:CTX_ROWS].astype(F32) for n in range(CTX)], axis=0)
+        grad_out[...] = shard[OUT_AT:UP_AT]
+        for j in range(HIDDEN // WIDTH):
+            grad_up[:, j * WIDTH : (j + 1) * WIDTH] = shard[UP_AT + 96 * j : UP_AT + 96 * (j + 1)]
+        grad_down[...] = shard[DOWN_AT:]
+        lines = jnp.zeros((2, WIDTH), F32)
+        for n in range(CTX):
+            lines = lines + pieces[n][CTX_ROWS + 24 : CTX_ROWS + 26].astype(F32)
+        line = jnp.concatenate([lines[0:1], lines[1:2]], axis=1)
+        at = 0
+        for ref, (_, width) in zip(vector_refs, VECTORS):
+            ref[...] = line[:, at : at + width]
+            at += width
+        heads = []
+        for head in range(HEADS):
+            wide = pieces[head][CTX_ROWS : CTX_ROWS + 24].astype(F32)
+            heads.append(
+                jnp.concatenate([wide[:, 192 * k : 192 * (k + 1)] for k in range(4)], axis=0)
+            )
+        for part in range(3):
+            grad_qkv[:, part * WIDTH : (part + 1) * WIDTH] = jnp.concatenate(
+                [head[:, part * DEPTH : (part + 1) * DEPTH] for head in heads], axis=1
+            )
+
+    shape = jax.ShapeDtypeStruct
+    return vmem_call(
+        kernel,
+        [
+            shape((96, 3 * WIDTH), F32),
+            shape((96, WIDTH), F32),
+            shape((96, HIDDEN), F32),
+            shape((384, WIDTH), F32),
+        ]
+        + [shape((1, width), F32) for _, width in VECTORS],
+        [],
+        10**6,
+        1,
+    )(pieces)
+
+
 def swap(slots, axes):
     return lax.all_to_all(slots, axes, 0, 0, tiled=True)
 
 
-def spread(piece, axes, count):
-    return swap(jnp.broadcast_to(piece[None], (count,) + piece.shape), axes)
-
-
-def reduce_over_ctx(shard):
-    rows = shard.shape[0] // CTX
-    parts = swap(shard.reshape(CTX, rows, WIDTH), "ctx")
-    mine = jnp.sum(parts.astype(F32), axis=0).astype(BF)
-    return spread(mine, "ctx", CTX).reshape(shard.shape).astype(F32)
+def shift_by(value, z=0, x=0, y=0, core=0):
+    pairs = []
+    for at_z in range(SIDE):
+        for at_x in range(SIDE):
+            for at_y in range(SIDE):
+                for at_core in range(2):
+                    source = (at_z * SIDE + at_x) * FSDP + at_y * 2 + at_core
+                    to_ctx = (at_z + z) % SIDE * SIDE + (at_x + x) % SIDE
+                    to_fsdp = (at_y + y) % SIDE * 2 + (at_core + core) % 2
+                    pairs.append((source, to_ctx * FSDP + to_fsdp))
+    return lax.ppermute(value, ("ctx", "fsdp"), pairs)
+
+
+def gather_rows(hat):
+    blocks = []
+    steps = (0, SIDE - 1, 1, 2)
+    for half, first, second in ((0, "x", "z"), (1, "z", "x")):
+        mine = hat[half * HALF : (half + 1) * HALF]
+        near = jnp.stack([mine] + [shift_by(mine, **{first: by}) for by in (1, -1, 2)])
+        ahead, behind = shift_by(near, **{second: 1}), shift_by(near, **{second: -1})
+        far_one = shift_by(ahead[:2], **{second: 1})
+        far_two = shift_by(behind[2:], **{second: -1})
+
+        def offsets(across, along):
+            return [(across, by) if second == "z" else (by, across) for by in along]
+
+        blocks += [
+            (half, offsets(0, steps), near),
+            (half, offsets(SIDE - 1, steps), ahead),
+            (half, offsets(1, steps), behind),
+            (half, offsets(2, steps[:2]), far_one),
+            (half, offsets(2, steps[2:]), far_two),
+        ]
+    return blocks
+
+
+def gather_small(piece):
+    at = lax.axis_index("fsdp")
+    at_y, at_core = at // 2, at % 2
+    ring = jnp.stack(
+        [piece, shift_by(piece, y=-1), shift_by(piece, y=2), shift_by(piece, y=1)]
+    )
+    other = shift_by(ring, core=1)
+    first = jnp.where(at_core == 0, ring, other)
+    second = jnp.where(at_core == 0, other, ring)
+    both = jnp.stack([first, second], axis=1)
+    turned = lax.dynamic_slice_in_dim(
+        jnp.concatenate([both, both], axis=0), (SIDE - at_y) % SIDE, SIDE, 0
+    )
+    return turned.reshape((FSDP,) + piece.shape)
+
+
+def scatter_small(slots):
+    at = lax.axis_index("fsdp")
+    at_y, at_core = at // 2, at % 2
+    pairs = slots.reshape((SIDE, 2) + slots.shape[1:])
+    mine = jnp.where(at_core == 0, pairs[:, 0], pairs[:, 1])
+    theirs = jnp.where(at_core == 0, pairs[:, 1], pairs[:, 0])
+    both = (mine.astype(F32) + shift_by(theirs, core=1).astype(F32)).astype(BF)
+
+    def slot(by):
+        return lax.dynamic_index_in_dim(both, (at_y + by) % SIDE, 0, keepdims=False)
+
+    return [slot(0)] + [shift_by(slot(by), y=by) for by in (1, -1, 2)]
 
 
 def local(
@@ -465,6 +663,7 @@
 ):
     my_tokens, my_cotangent = tokens[0], cotangent[0]
     place = lax.axis_index("ctx")
+    where = place.reshape(1).astype(jnp.int32)
     head = place % HEADS
     shards = dict(
         first_gain=first_gain, first_shift=first_shift, qv_bias=qv_bias, out_bias=out_bias,
@@ -472,7 +671,7 @@
     )
 
     with jax.named_scope("gather_tokens"):
-        all_tokens = spread(my_tokens, "ctx", CTX)
+        blocks = gather_rows(normalised_rows(my_tokens))
     with jax.named_scope("gather_weights"):
         pack = jnp.concatenate(
             [out_weight]
@@ -491,10 +690,9 @@
             axis=1,
         )
         vectors = jnp.concatenate([shards[name] for name, _ in VECTORS]).reshape(6, 3 * DEPTH)
-        small = jnp.concatenate(
-            [head_columns, vectors, jnp.zeros((10, 3 * DEPTH), BF)], axis=0
-        )
-        small = spread(small, "fsdp", FSDP)
+        small = gather_small(
+            jnp.concatenate([head_columns, vectors, jnp.zeros((10, 3 * DEPTH), BF)], axis=0)
+        )
         w_head = small[:, :96].reshape(WIDTH, 3 * DEPTH)
         vectors = small[:, 96:102].reshape(FSDP, VECTOR_WIDTH).astype(F32)
         whole, at = {}, 0
@@ -512,83 +710,42 @@
 
     with jax.named_scope("attention"):
         packed, normed, query, key, value, query_t, key_t, out_t, lse = head_forward(
-            pair_order, all_tokens, w_head, head_bias, whole["first_gain"], whole["first_shift"]
+            pair_order, where, blocks, w_head, head_bias, whole["first_gain"],
+            whole["first_shift"],
         )
         heads_out = swap(packed, "ctx")
 
     with jax.named_scope("feed_forward"):
-        (
-            mixed, attended, normed_two, active, grad_pre, grad_branch, grad_heads,
-            grad_residual, vector_sums, up_sums,
-        ) = feed_forward(
+        mixed, pack_grad, grad_heads, grad_residual, vector_sums, up_sums = feed_forward(
             my_tokens, heads_out, my_cotangent, pack, whole["out_bias"], whole["second_gain"],
             whole["second_shift"], whole["up_bias"], whole["down_bias"],
         )
         heads_up = swap(grad_heads, "ctx")
-
-    with jax.named_scope("feed_forward_weights"):
-        grad_down = lax.dot_general(
-            active, my_cotangent, (((0,), (0,)), ((), ())), preferred_element_type=F32
-        ).astype(BF).reshape(FSDP, 384, WIDTH)
-        grad_down = lax.psum_scatter(grad_down, "fsdp", scatter_dimension=0, tiled=False)
-        grad_up = weight_grads(normed_two, grad_pre, 4)
-        grad_up = lax.psum_scatter(grad_up, "fsdp", scatter_dimension=0, tiled=False)
-        grad_out = weight_grads(attended, grad_branch, 1)
-        grad_out = lax.psum_scatter(grad_out, "fsdp", scatter_dimension=0, tiled=False)
+        shard_grad = lax.psum_scatter(pack_grad, "fsdp", scatter_dimension=0, tiled=False)
 
     with jax.named_scope("attention_back"):
-        packed_grad, head_weight_grad, head_bias_grad = head_backward(
-            pair_order, heads_up, normed, query, key, value, query_t, key_t, out_t, lse
+        packed_grad, low_rows, bias_sums = head_backward(
+            pair_order, heads_up, query, key, value, query_t, key_t, out_t, lse
         )
         heads_grad = swap(packed_grad, "ctx")
-    with jax.named_scope("head_weights"):
-        parts = swap(head_weight_grad, "fsdp")
-        mine = jnp.sum(parts.astype(F32), axis=0).astype(BF)
-        head_parts = spread(mine, "ctx", CTX)[:HEADS].astype(F32)
-        grad_qkv = (
-            head_parts.reshape(HEADS, 96, 3, DEPTH).transpose(1, 2, 0, 3).reshape(96, 3 * WIDTH)
-        )
+        weight_grad = head_weight_grad(normed, low_rows)
 
     with jax.named_scope("token_gradient"):
         tokens_grad, first_sums = token_gradient(
             my_tokens, heads_grad, w_qkv, whole["first_gain"], grad_residual
         )
-
-    with jax.named_scope("vector_grads"):
-        holds = (jnp.arange(HEADS) == place).astype(F32)[:, None]
-        bias_sums = jnp.concatenate(
-            [
-                (holds * head_bias_grad[:, :DEPTH]).reshape(1, WIDTH),
-                (holds * head_bias_grad[:, 2 * DEPTH :]).reshape(1, WIDTH),
-            ],
-            axis=1,
-        )
-        sums = dict(
-            first_gain=first_sums[0:1], first_shift=first_sums[1:2], qv_bias=bias_sums,
-            out_bias=vector_sums[0:1], second_gain=vector_sums[1:2],
-            second_shift=vector_sums[2:3], up_bias=up_sums, down_bias=vector_sums[3:4],
-        )
-        sums = jnp.concatenate(
-            [sums[name].reshape(FSDP, width) for name, width in VECTORS], axis=1
-        ).astype(BF)
-        slots = jnp.broadcast_to(
-            sums.reshape(1, FSDP, VECTOR_WIDTH // 128, 128), (CTX, FSDP, VECTOR_WIDTH // 128, 128)
-        ).reshape(CTX * FSDP, VECTOR_WIDTH // 128, 128)
-        mine = jnp.sum(swap(slots, ("ctx", "fsdp")).astype(F32), axis=0).reshape(VECTOR_WIDTH)
-        grads, at = {}, 0
-        for name, width in VECTORS:
-            grads[name] = mine[at : at + width]
-            at += width
+        smalls = scatter_small(
+            small_slots(where, weight_grad, bias_sums, first_sums, vector_sums, up_sums)
+        )
 
     with jax.named_scope("sum_over_ctx"):
-        grad_down = reduce_over_ctx(grad_down)
-        grad_up = reduce_over_ctx(grad_up)
-        grad_up = jnp.concatenate(
-            [grad_up[96 * j : 96 * (j + 1)] for j in range(HIDDEN // WIDTH)], axis=1
-        )
-        grad_out = reduce_over_ctx(
-            jnp.concatenate([grad_out, jnp.zeros((32, WIDTH), BF)], axis=0)
-        )[:96]
+        parts = swap(shard_grad.reshape(CTX, CTX_ROWS, WIDTH), "ctx")
+        grad_qkv, grad_out, grad_up, grad_down, *vector_grads = final_grads(
+            swap(last_pieces(parts, smalls), "ctx")
+        )
+        grads = {
+            name: grad.reshape(width) for grad, (name, width) in zip(vector_grads, VECTORS)
+        }
 
     return (
         mixed[None], tokens_grad[None], grads["first_gain"], grads["first_shift"], grad_qkv,

time: 346 us -> 264 us (0.76)
  waiting for transfers between devices: 116 us -> 65.2 us
  local copies, waits for them, and re-layouts: 40.9 us -> 21.5 us
  blocking collectives: 53.9 us -> 45.5 us
  starting transfers between devices: 43.4 us -> 48 us
  matrix products: 3.53 us -> 0 us
    all_to_all x10 -> x3, waiting for transfers between devices: 108 us -> 5.1 us  [swap(): return lax.all_to_all(slots, axes, 0, 0, tiled=True)]
    ppermute x0 -> x22, starting transfers between devices: none -> 32.5 us  [shift_by(): return lax.ppermute(value, ('ctx', 'fsdp'), pairs)]
    all_to_all x10 -> x3, starting transfers between devices: 43.2 us -> 15.1 us  [swap(): return lax.all_to_all(slots, axes, 0, 0, tiled=True)]
    reduce_scatter x3 -> x1, waiting for transfers between devices: 6.98 us -> 29.5 us  [local(): lax.psum_scatter(pack_grad, 'fsdp', scatter_dimension=0, tiled=False)]
    all_gather x1, waiting for transfers between devices: 0.01 us -> 16.3 us  [local(): w_qkv = lax.all_gather(qkv_weight, 'fsdp', axis=0, tiled=True)]
    ppermute x0 -> x22, waiting for transfers between devices: none -> 13.6 us  [shift_by(): return lax.ppermute(value, ('ctx', 'fsdp'), pairs)]
    pallas_call x1, Pallas kernels: 24.7 us -> 13.2 us  [head_forward(): vmem_call(kernel, [shape((CTX, HALF, 2 * DEPTH), BF), shape((SEQ, WIDTH),...]
    pallas_call x4 -> x7, Pallas kernels: 37 us -> 45.9 us  [the longest x1 16.7 us: feed_forward(): vmem_call(kernel, [shape((ROWS, WIDTH), BF), shape((FSDP, PACK_ROWS, WIDT...]
  transfers between devices with their start and end apart: 15 -> 28, of which waited for: 11 -> 12; matrix products, arithmetic and copies ran while one was open for 11% -> 5% of each run, Pallas kernels for 15% -> 15%
where the time goes in v2:
time: 264 us; the launch traced here: 263 us
  waiting for transfers between devices  65.2 us (25%)
  Pallas kernels  63.7 us (24%)
  starting transfers between devices  48 us (18%)
  blocking collectives  45.5 us (17%)
  local copies, waits for them, and re-layouts  21.5 us (8%)
  between operations  14.4 us (5%)
  other arithmetic  4.64 us (2%)
    all_to_all x2, blocking collectives, swap(): return lax.all_to_all(slots, axes, 0, 0, tiled=True)  45.5 us
    ppermute x22, starting transfers between devices, shift_by(): return lax.ppermute(value, ('ctx', 'fsdp'), pairs)  32.5 us
    reduce_scatter x1, waiting for transfers between devices, local(): lax.psum_scatter(pack_grad, 'fsdp', scatter_dimension=0, tiled=False)  29.5 us
    pallas_call x1, Pallas kernels, feed_forward(): vmem_call(kernel, [shape((ROWS, WIDTH), BF), shape((FSDP, PACK_ROWS, WIDT...  16.7 us
    all_gather x1, waiting for transfers between devices, local(): w_qkv = lax.all_gather(qkv_weight, 'fsdp', axis=0, tiled=True)  16.3 us
    all_to_all x3, starting transfers between devices, swap(): return lax.all_to_all(slots, axes, 0, 0, tiled=True)  15.1 us
    pallas_call x1, Pallas kernels, head_backward(): vmem_call(kernel, [shape((CTX, HALF, 6 * DEPTH), BF), shape((SEQ, 3 * DEP...  13.7 us
    ppermute x22, waiting for transfers between devices, shift_by(): return lax.ppermute(value, ('ctx', 'fsdp'), pairs)  13.6 us
  transfers between devices with their start and end apart: 28, of which 12 were waited for; matrix products, arithmetic and copies ran while one was open for 5% of the time, Pallas kernels for 15%

profile of v2, /device:TPU:0, one launch (start us, length us, event | category | flops | bytes accessed | tf_op | source)
XLA Modules:
  0.0 262.8 jit_solution(717773482470339594)
XLA Ops:
  7.2 1.0 constant_dynamic-update-slice_fusion.1
  8.2 0.9 slice_dynamic-update-slice_fusion.3
  9.1 0.9 slice_dynamic-update-slice_fusion.2
  10.1 0.9 slice_dynamic-update-slice_fusion.1
  11.0 0.9 slice_dynamic-update-slice_fusion
  12.1 1.1 copy-done.2
  13.3 0.9 constant_dynamic-slice_fusion.4
  15.0 3.2 %collective-permute-start.14 = (bf16[112,192]{0,1:T(8,128)(2,1)S(1)}, bf16[112,192]{0,1:T(8,128)(2,1)S(1)}, u32[]{:S(2)}, u32[]{:S(2)}) collective-permute-start(bf16[112,192]{0,1:T(8,128)(2,1)S(1)} %maximum_maximum_fusion), channel_id=1, source_target_pairs={{0,6},{1,7},{2,0},{3,1},{4,2},{5,3},{6,4},{7,5},{8,14},{9,15},{10,... | collective-permute-start | bytes 129032 | tf_op jit(solution)/shard_map/gather_small/ppermute | solution.py:604
  18.2 0.6 collective-permute-start.15
  18.8 1.0 collective-permute-start.16
  19.8 1.8 gather_tokens.1
  21.6 1.0 slice_bitcast_fusion.3
  22.6 2.0 collective-permute-start.7
  24.6 2.2 collective-permute-start.8
  27.0 1.8 collective-permute-start.9
  28.8 1.5 collective-permute-start
  30.3 1.7 collective-permute-start.1
  32.1 1.9 collective-permute-start.2
  34.1 0.7 collective-permute-start.10
  34.8 0.9 collective-permute-done
  35.7 1.7 collective-permute-start.11
  37.4 1.5 collective-permute-done.2
  38.9 1.1 collective-permute-start.3
  40.0 2.2 collective-permute-start.4
  43.3 0.7 reshape.105.refs_12_.gain
  44.0 0.7 reshape.106.refs_13_
  44.7 0.9 copy.53
  45.7 1.4 collective-permute-done.10.refs_6_
  47.3 3.3 %collective-permute-start.13 = (bf16[2,64,768]{2,1,0:T(8,128)(2,1)S(1)}, bf16[2,64,768]{2,1,0:T(8,128)(2,1)S(1)}, u32[]{:S(2)}, u32[]{:S(2)}) collective-permute-start(bf16[2,64,768]{2,1,0:T(8,128)(2,1)S(1)} %slice.95), channel_id=1, source_target_pairs={{0,24},{1,25},{2,26},{3,27},{4,28},{5,29},{6,30},{7,31},{8,0},{9,1... | collective-permute-start | bytes 589832 | tf_op jit(solution)/shard_map/gather_tokens/ppermute | solution.py:604
  50.6 1.1 collective-permute-start.5
  51.7 2.5 collective-permute-start.6
  55.2 2.9 %collective-permute-done.5.refs_3_ = bf16[2,64,768]{2,1,0:T(8,128)(2,1)S(1)} collective-permute-done((bf16[2,64,768]{2,1,0:T(8,128)(2,1)S(1)}, bf16[2,64,768]{2,1,0:T(8,128)(2,1)S(1)}, u32[]{:S(2)}, u32[]{:S(2)}) %collective-permute-start.5) | collective-permute-done | bytes 196640 | tf_op jit(solution)/shard_map/gather_tokens/ppermute | solution.py:604
  58.8 13.2 %attention.1 = (bf16[16,64,128]{2,1,0:T(8,128)(2,1)}, bf16[2048,768]{1,0:T(8,128)(2,1)}, bf16[2048,64]{1,0:T(8,128)(2,1)}, bf16[2048,64]{1,0:T(8,128)(2,1)}, bf1...) custom-call(s32[16]{0:T(128)} %order.3, ...), custom_call_target="tpu_custom_call" | custom-call | flops 2000000000 | bytes 8388608 | tf_op jit(solution)/shard_map/attention/pallas_call | solution.py:222
  72.0 4.6 %all-to-all-start = ((bf16[16,64,128]{2,1,0:T(8,128)(2,1)}), bf16[16,64,128]{2,1,0:T(8,128)(2,1)S(1)}, u32[]{:S(2)}, u32[]{:S(2)}) async-start(bf16[16,64,128]{2,1,0:T(8,128)(2,1)} %get-tuple-element.46), calls=%async_computation | async-start | bytes 524288 | tf_op jit(solution)/shard_map/attention/all_to_all | solution.py:591
  76.8 0.7 reshape.107.out_bias
  77.5 0.7 reshape.108.gain
  78.1 0.7 reshape.109.shift
  78.8 0.7 reshape.111.down_bias
  80.1 5.1 %all-to-all-done.heads_out = bf16[16,64,128]{2,1,0:T(8,128)(2,1)S(1)} async-done(((bf16[16,64,128]{2,1,0:T(8,128)(2,1)}), bf16[16,64,128]{2,1,0:T(8,128)(2,1)S(1)}, u32[]{:S(2)}, u32[]{:S(2)}) %all-to-all-start) | async-done | bytes 262176 | tf_op jit(solution)/shard_map/attention/all_to_all | solution.py:591
  85.2 0.7 copy-done.6
  85.9 16.7 %feed_forward.1 = (bf16[128,768]{1,0:T(8,128)(2,1)}, bf16[8,864,768]{2,1,0:T(8,128)(2,1)}, bf16[16,64,128]{2,1,0:T(8,128)(2,1)}, f32[128,768]{1,0:T(8,128)}, f32[4,768]{1,0:T(4,128)}, /*index=5*/f32[1,3072]{1,0:T(1,128)}) custom-call(bf16[128,768]{1,0:T(8,128)(2,1)} %bitcast.73, bf16[16,64,128]{2,1,0:T(8,128)(2,1)} %copy-done.6, bf16[128,768]{1,0:T(8,128)(2,1)} %bitcast.92, ...), custom_call_target="tpu_custom_call" | custom-call | flops 4000000000 | bytes 8388608 | tf_op jit(solution)/shard_map/feed_forward/pallas_call | solution.py:444
  102.7 0.7 all-gather.4.cloned.1.call-update
  103.6 12.0 %all_to_all.25.upstream = bf16[16,64,128]{2,1,0:T(8,128)(2,1)} all-to-all(bf16[16,64,128]{2,1,0:T(8,128)(2,1)S(1)} %copy-done.7), channel_id=1, replica_groups=mesh['ctx'=16,'fsdp'=8] {'ctx'}, dimensions={0} | all-to-all | bytes 524288 | tf_op jit(solution)/shard_map/feed_forward/all_to_all | solution.py:591
  115.6 13.7 %attention_back.2 = (bf16[16,64,384]{2,1,0:T(8,128)(2,1)}, bf16[2048,192]{1,0:T(8,128)(2,1)}, f32[1,192]{1,0:T(1,128)}) custom-call(s32[16]{0:T(128)} %order.3, bf16[16,64,128]{2,1,0:T(8,128)(2,1)} %all_to_all.25.upstream, bf16[2048,64]{1,0:T(8,128)(2,1)} %get-tuple-element.49.query, bf16[2048,64]{1,0:T(8,128)(2,1)} %get-tuple-element.50.key, ...), custom_call_target="tpu_custom_call" | custom-call | flops 4000000000 | bytes 8388608 | tf_op jit(solution)/shard_map/attention_back/pallas_call | solution.py:330
  129.3 3.6 %all-to-all-start.2 = ((bf16[16,64,384]{2,1,0:T(8,128)(2,1)}), bf16[16,64,384]{2,1,0:T(8,128)(2,1)S(1)}, u32[]{:S(2)}, u32[]{:S(2)}) async-start(bf16[16,64,384]{2,1,0:T(8,128)(2,1)} %get-tuple-element.56), calls=%async_computation.2 | async-start | bytes 1572864 | tf_op jit(solution)/shard_map/attention_back/all_to_all | solution.py:591
  132.9 29.5 %reduce-scatter.2.cloned.1.call-done = bf16[1,864,768]{2,1,0:T(8,128)(2,1)} async-done(((bf16[8,864,768]{2,1,0:T(8,128)(2,1)}), bf16[1,864,768]{2,1,0:T(8,128)(2,1)}) %reduce-scatter.2.cloned.1.call-update) | async-done | bytes 1327120 | tf_op jit(solution)/shard_map/feed_forward/reduce_scatter | solution.py:724
  162.4 2.4 reduce_scatter.11
  164.8 0.9 copy-done.1
  165.7 6.9 %all-to-all-start.3 = ((bf16[16,54,768]{2,1,0:T(8,128)(2,1)}), bf16[16,54,768]{2,1,0:T(8,128)(2,1)S(1)}, u32[]{:S(2)}, u32[]{:S(2)}) async-start(bf16[16,54,768]{2,1,0:T(8,128)(2,1)} %reduce_scatter.11), calls=%async_computation.4 | async-start | bytes 2752512 | tf_op jit(solution)/shard_map/sum_over_ctx/all_to_all | solution.py:591
  172.7 4.3 %attention_back.3.weight_grad = bf16[8,96,192]{2,1,0:T(8,128)(2,1)} custom-call(bf16[2048,768]{1,0:T(8,128)(2,1)} %get-tuple-element.60.normed, bf16[2048,192]{1,0:T(8,128)(2,1)} %get-tuple-element.61.rows), custom_call_target="tpu_custom_call" | custom-call | flops 603979776 | bytes 8388608 | tf_op jit(solution)/shard_map/attention_back/pallas_call | solution.py:359
  177.0 16.3 %all-gather.4.cloned.1.call-done.weight = bf16[768,2304]{1,0:T(8,128)(2,1)} async-done(((bf16[96,2304]{1,0:T(8,128)(2,1)}), bf16[768,2304]{1,0:T(8,128)(2,1)}) %all-gather.4.cloned.1.call-update) | async-done | bytes 3538960 | tf_op jit(solution)/shard_map/gather_weights/all_gather | solution.py:683
  193.3 4.6 %token_gradient.2 = (f32[128,768]{1,0:T(8,128)}, f32[2,768]{1,0:T(2,128)}) custom-call(bf16[128,768]{1,0:T(8,128)(2,1)} %bitcast.74, bf16[16,64,384]{2,1,0:T(8,128)(2,1)} %copy-done.1, bf16[768,2304]{1,0:T(8,128)(2,1)} %all-gather.4.cloned.1.call-done.weight, f32[1,768]{1,0:T(1,128)} %reshape.105.refs_12_.gain, f32[128,768]{1,0:T(8,128)} %get-tuple-element.57.grad_residual), custom_call_target="tpu_custom_call" | custom-call | flops 452984832 | bytes 8388608 | tf_op jit(solution)/shard_map/token_gradient/pallas_call | solution.py:472
  197.8 2.5 token_gradient.3
  200.3 1.1 select_bitcast_fusion
  201.7 1.2 collective-permute-done.18
  202.9 1.1 fusion
  204.1 0.7 dynamic-slice_bitcast_fusion
  205.1 2.8 %collective-permute-start.20 = (bf16[104,192]{1,0:T(8,128)(2,1)S(1)}, bf16[104,192]{1,0:T(8,128)(2,1)S(1)}, u32[]{:S(2)}, u32[]{:S(2)}) collective-permute-start(bf16[104,192]{1,0:T(8,128)(2,1)S(1)} %get-tuple-element.84), channel_id=1, source_target_pairs={{0,6},{1,7},{2,0},{3,1},{4,2},{5,3},{6,4},{7,5},{8,14},{9,15},{10,... | collective-permute-start | bytes 119816 | tf_op jit(solution)/shard_map/token_gradient/ppermute | solution.py:604
  208.4 1.7 collective-permute-done.19.left
  210.4 3.2 %collective-permute-done.21.far = bf16[104,192]{1,0:T(8,128)(2,1)S(1)} collective-permute-done((bf16[104,192]{1,0:T(8,128)(2,1)S(1)}, bf16[104,192]{1,0:T(8,128)(2,1)S(1)}, u32[]{:S(2)}, u32[]{:S(2)}) %collective-permute-start.21) | collective-permute-done | bytes 39968 | tf_op jit(solution)/shard_map/token_gradient/ppermute | solution.py:604
  214.7 3.1 %sum_over_ctx.2 = bf16[16,80,768]{2,1,0:T(8,128)(2,1)} custom-call(bf16[16,54,768]{2,1,0:T(8,128)(2,1)} %copy-done, bf16[104,192]{1,0:T(8,128)(2,1)} %get-tuple-element.86.own, bf16[104,192]{1,0:T(8,128)(2,1)} %copy-done.12, bf16[104,192]{1,0:T(8,128)(2,1)} %copy-done.13, bf16[104,192]{1,0:T(8,128)(2,1)} %copy-done.14), custom_call_target="tpu_custom_call" | custom-call | flops 1000000 | bytes 8388608 | tf_op jit(solution)/shard_map/sum_over_ctx/pallas_call | solution.py:539
  217.8 33.5 %all_to_all.26.pieces = bf16[16,80,768]{2,1,0:T(8,128)(2,1)} all-to-all(bf16[16,80,768]{2,1,0:T(8,128)(2,1)} %sum_over_ctx.2), channel_id=1, replica_groups=mesh['ctx'=16,'fsdp'=8] {'ctx'}, dimensions={0} | all-to-all | bytes 3932160 | tf_op jit(solution)/shard_map/sum_over_ctx/all_to_all | solution.py:591
  251.3 3.7 %sum_over_ctx.3 = (f32[96,2304]{1,0:T(8,128)}, f32[96,768]{1,0:T(8,128)}, f32[96,3072]{1,0:T(8,128)}, f32[384,768]{1,0:T(8,128)}, f32[1,96]{1,0:T(1,128)}, /*ind...) custom-call(bf16[16,80,768]{2,1,0:T(8,128)(2,1)} %all_to_all.26.pieces), custom_call_target="tpu_custom_call" | custom-call | flops 1000000 | bytes 8388608 | tf_op jit(solution)/shard_map/sum_over_ctx/pallas_call | solution.py:575
  255.0 1.3 reduce
  (112 shorter events, 8.0 us)
Async XLA Ops:
  7.2 4.7 %copy-start.3 = (bf16[384,768]{1,0:T(8,128)(2,1)S(1)}, bf16[384,768]{1,0:T(8,128)(2,1)}, u32[]{:S(2)}) copy-start(bf16[384,768]{1,0:T(8,128)(2,1)} %param.28) | copy-start | bytes 1769476
  7.2 78.1 %all-gather.6.cloned.1.call-start = ((), (), s32[]{:S(2)}) async-start(), calls=%async_computation.8 | async-start | bytes 11943936 | tf_op jit(solution)/shard_map/gather_weights/all_gather | solution.py:682
  11.9 2.5 copy-start.15
  11.9 2.5 copy-start.16
  12.0 2.5 copy-start.17
  12.0 2.5 copy-start.18
  12.0 2.5 copy-start.19
  12.0 2.5 copy-start.20
  12.0 2.5 copy-start.21
  12.0 2.5 copy-start.22
  12.1 1.1 copy-start.2
  15.0 12.0 %collective-permute-start.14 = (bf16[112,192]{0,1:T(8,128)(2,1)S(1)}, bf16[112,192]{0,1:T(8,128)(2,1)S(1)}, u32[]{:S(2)}, u32[]{:S(2)}) collective-permute-start(bf16[112,192]{0,1:T(8,128)(2,1)S(1)} %maximum_maximum_fusion), channel_id=1, source_target_pairs={{0,6},{1,7},{2,0},{3,1},{4,2},{5,3},{6,4},{7,5},{8,14},{9,15},{10,... | collective-permute-start | bytes 129032 | tf_op jit(solution)/shard_map/gather_small/ppermute | solution.py:604
  18.2 10.6 %collective-permute-start.15 = (bf16[112,192]{0,1:T(8,128)(2,1)S(1)}, bf16[112,192]{0,1:T(8,128)(2,1)S(1)}, u32[]{:S(2)}, u32[]{:S(2)}) collective-permute-start(bf16[112,192]{0,1:T(8,128)(2,1)S(1)} %maximum_maximum_fusion), channel_id=1, source_target_pairs={{0,4},{1,5},{2,6},{3,7},{4,0},{5,1},{6,2},{7,3},{8,12},{9,13},{10,... | collective-permute-start | bytes 129032 | tf_op jit(solution)/shard_map/gather_small/ppermute | solution.py:604
  18.8 11.5 %collective-permute-start.16 = (bf16[112,192]{0,1:T(8,128)(2,1)S(1)}, bf16[112,192]{0,1:T(8,128)(2,1)S(1)}, u32[]{:S(2)}, u32[]{:S(2)}) collective-permute-start(bf16[112,192]{0,1:T(8,128)(2,1)S(1)} %maximum_maximum_fusion), channel_id=1, source_target_pairs={{0,2},{1,3},{2,4},{3,5},{4,6},{5,7},{6,0},{7,1},{8,10},{9,11},{10,... | collective-permute-start | bytes 129032 | tf_op jit(solution)/shard_map/gather_small/ppermute | solution.py:604
  22.6 9.5 %collective-permute-start.7 = (bf16[64,768]{1,0:T(8,128)(2,1)S(1)}, bf16[64,768]{1,0:T(8,128)(2,1)S(1)}, u32[]{:S(2)}, u32[]{:S(2)}) collective-permute-start(bf16[64,768]{1,0:T(8,128)(2,1)S(1)} %get-tuple-element.89), channel_id=1, source_target_pairs={{0,32},{1,33},{2,34},{3,35},{4,36},{5,37},{6,38},{7,39},{8,40},{9,... | collective-permute-start | bytes 294920 | tf_op jit(solution)/shard_map/gather_tokens/ppermute | solution.py:604
  24.6 9.5 %collective-permute-start.8 = (bf16[64,768]{1,0:T(8,128)(2,1)S(1)}, bf16[64,768]{1,0:T(8,128)(2,1)S(1)}, u32[]{:S(2)}, u32[]{:S(2)}) collective-permute-start(bf16[64,768]{1,0:T(8,128)(2,1)S(1)} %get-tuple-element.89), channel_id=1, source_target_pairs={{0,96},{1,97},{2,98},{3,99},{4,100},{5,101},{6,102},{7,103},{8,104... | collective-permute-start | bytes 294920 | tf_op jit(solution)/shard_map/gather_tokens/ppermute | solution.py:604
  27.0 7.0 %collective-permute-start.9 = (bf16[64,768]{1,0:T(8,128)(2,1)S(1)}, bf16[64,768]{1,0:T(8,128)(2,1)S(1)}, u32[]{:S(2)}, u32[]{:S(2)}) collective-permute-start(bf16[64,768]{1,0:T(8,128)(2,1)S(1)} %get-tuple-element.89), channel_id=1, source_target_pairs={{0,64},{1,65},{2,66},{3,67},{4,68},{5,69},{6,70},{7,71},{8,72},{9,... | collective-permute-start | bytes 294920 | tf_op jit(solution)/shard_map/gather_tokens/ppermute | solution.py:604
  28.8 6.9 %collective-permute-start = (bf16[64,768]{1,0:T(8,128)(2,1)S(1)}, bf16[64,768]{1,0:T(8,128)(2,1)S(1)}, u32[]{:S(2)}, u32[]{:S(2)}) collective-permute-start(bf16[64,768]{1,0:T(8,128)(2,1)S(1)} %get-tuple-element.90), channel_id=1, source_target_pairs={{0,8},{1,9},{2,10},{3,11},{4,12},{5,13},{6,14},{7,15},{8,16},{9,17... | collective-permute-start | bytes 294920 | tf_op jit(solution)/shard_map/gather_tokens/ppermute | solution.py:604
  30.3 7.1 %collective-permute-start.1 = (bf16[64,768]{1,0:T(8,128)(2,1)S(1)}, bf16[64,768]{1,0:T(8,128)(2,1)S(1)}, u32[]{:S(2)}, u32[]{:S(2)}) collective-permute-start(bf16[64,768]{1,0:T(8,128)(2,1)S(1)} %get-tuple-element.90), channel_id=1, source_target_pairs={{0,24},{1,25},{2,26},{3,27},{4,28},{5,29},{6,30},{7,31},{8,0},{9,1... | collective-permute-start | bytes 294920 | tf_op jit(solution)/shard_map/gather_tokens/ppermute | solution.py:604
  32.1 6.7 %collective-permute-start.2 = (bf16[64,768]{1,0:T(8,128)(2,1)S(1)}, bf16[64,768]{1,0:T(8,128)(2,1)S(1)}, u32[]{:S(2)}, u32[]{:S(2)}) collective-permute-start(bf16[64,768]{1,0:T(8,128)(2,1)S(1)} %get-tuple-element.90), channel_id=1, source_target_pairs={{0,16},{1,17},{2,18},{3,19},{4,20},{5,21},{6,22},{7,23},{8,24},{9,... | collective-permute-start | bytes 294920 | tf_op jit(solution)/shard_map/gather_tokens/ppermute | solution.py:604
  34.0 8.2 %collective-permute-start.17 = (bf16[4,112,192]{1,2,0:T(8,128)(2,1)S(1)}, bf16[4,112,192]{1,2,0:T(8,128)(2,1)S(1)}, u32[]{:S(2)}, u32[]{:S(2)}) collective-permute-start(bf16[4,112,192]{1,2,0:T(8,128)(2,1)S(1)} %pad_maximum_fusion.2), channel_id=1, source_target_pairs={{0,1},{1,0},{2,3},{3,2},{4,5},{5,4},{6,7},{7,6},{8,9},{9,8},{10,11... | collective-permute-start | bytes 516104 | tf_op jit(solution)/shard_map/gather_small/ppermute | solution.py:604
  34.1 8.6 %copy-start.4 = (bf16[4,64,768]{2,1,0:T(8,128)(2,1)}, bf16[4,64,768]{2,1,0:T(8,128)(2,1)S(1)}, u32[]{:S(2)}) copy-start(bf16[4,64,768]{2,1,0:T(8,128)(2,1)S(1)} %pad_maximum_fusion.1.refs_5_) | copy-start | bytes 1179652
  34.1 13.0 %collective-permute-start.10 = (bf16[4,64,768]{2,1,0:T(8,128)(2,1)S(1)}, bf16[4,64,768]{2,1,0:T(8,128)(2,1)S(1)}, u32[]{:S(2)}, u32[]{:S(2)}) collective-permute-start(bf16[4,64,768]{2,1,0:T(8,128)(2,1)S(1)} %pad_maximum_fusion.1.refs_5_), channel_id=1, source_target_pairs={{0,8},{1,9},{2,10},{3,11},{4,12},{5,13},{6,14},{7,15},{8,16},{9,17... | collective-permute-start | bytes 1179656 | tf_op jit(solution)/shard_map/gather_tokens/ppermute | solution.py:604
  35.7 11.5 %collective-permute-start.11 = (bf16[4,64,768]{2,1,0:T(8,128)(2,1)S(1)}, bf16[4,64,768]{2,1,0:T(8,128)(2,1)S(1)}, u32[]{:S(2)}, u32[]{:S(2)}) collective-permute-start(bf16[4,64,768]{2,1,0:T(8,128)(2,1)S(1)} %pad_maximum_fusion.1.refs_5_), channel_id=1, source_target_pairs={{0,24},{1,25},{2,26},{3,27},{4,28},{5,29},{6,30},{7,31},{8,0},{9,1... | collective-permute-start | bytes 1179656 | tf_op jit(solution)/shard_map/gather_tokens/ppermute | solution.py:604
  38.9 4.0 %copy-start.5 = (bf16[4,64,768]{2,1,0:T(8,128)(2,1)}, bf16[4,64,768]{2,1,0:T(8,128)(2,1)S(1)}, u32[]{:S(2)}) copy-start(bf16[4,64,768]{2,1,0:T(8,128)(2,1)S(1)} %pad_maximum_fusion.refs_0_) | copy-start | bytes 1179652
  38.9 11.6 %collective-permute-start.3 = (bf16[4,64,768]{2,1,0:T(8,128)(2,1)S(1)}, bf16[4,64,768]{2,1,0:T(8,128)(2,1)S(1)}, u32[]{:S(2)}, u32[]{:S(2)}) collective-permute-start(bf16[4,64,768]{2,1,0:T(8,128)(2,1)S(1)} %pad_maximum_fusion.refs_0_), channel_id=1, source_target_pairs={{0,32},{1,33},{2,34},{3,35},{4,36},{5,37},{6,38},{7,39},{8,40},{9,... | collective-permute-start | bytes 1179656 | tf_op jit(solution)/shard_map/gather_tokens/ppermute | solution.py:604
  40.0 11.6 %collective-permute-start.4 = (bf16[4,64,768]{2,1,0:T(8,128)(2,1)S(1)}, bf16[4,64,768]{2,1,0:T(8,128)(2,1)S(1)}, u32[]{:S(2)}, u32[]{:S(2)}) collective-permute-start(bf16[4,64,768]{2,1,0:T(8,128)(2,1)S(1)} %pad_maximum_fusion.refs_0_), channel_id=1, source_target_pairs={{0,96},{1,97},{2,98},{3,99},{4,100},{5,101},{6,102},{7,103},{8,104... | collective-permute-start | bytes 1179656 | tf_op jit(solution)/shard_map/gather_tokens/ppermute | solution.py:604
  47.1 10.9 %copy-start.8 = (bf16[4,64,768]{2,1,0:T(8,128)(2,1)}, bf16[4,64,768]{2,1,0:T(8,128)(2,1)S(1)}, u32[]{:S(2)}) copy-start(bf16[4,64,768]{2,1,0:T(8,128)(2,1)S(1)} %collective-permute-done.10.refs_6_) | copy-start | bytes 1179652
  47.1 8.0 %collective-permute-start.12 = (bf16[2,64,768]{2,1,0:T(8,128)(2,1)S(1)}, bf16[2,64,768]{2,1,0:T(8,128)(2,1)S(1)}, u32[]{:S(2)}, u32[]{:S(2)}) collective-permute-start(bf16[2,64,768]{2,1,0:T(8,128)(2,1)S(1)} %slice.94), channel_id=1, source_target_pairs={{0,8},{1,9},{2,10},{3,11},{4,12},{5,13},{6,14},{7,15},{8,16},{9,17... | collective-permute-start | bytes 589832 | tf_op jit(solution)/shard_map/gather_tokens/ppermute | solution.py:604
  47.2 10.8 %copy-start.9 = (bf16[4,64,768]{2,1,0:T(8,128)(2,1)}, bf16[4,64,768]{2,1,0:T(8,128)(2,1)S(1)}, u32[]{:S(2)}) copy-start(bf16[4,64,768]{2,1,0:T(8,128)(2,1)S(1)} %collective-permute-done.11.refs_7_) | copy-start | bytes 1179652
  47.3 7.9 %collective-permute-start.13 = (bf16[2,64,768]{2,1,0:T(8,128)(2,1)S(1)}, bf16[2,64,768]{2,1,0:T(8,128)(2,1)S(1)}, u32[]{:S(2)}, u32[]{:S(2)}) collective-permute-start(bf16[2,64,768]{2,1,0:T(8,128)(2,1)S(1)} %slice.95), channel_id=1, source_target_pairs={{0,24},{1,25},{2,26},{3,27},{4,28},{5,29},{6,30},{7,31},{8,0},{9,1... | collective-permute-start | bytes 589832 | tf_op jit(solution)/shard_map/gather_tokens/ppermute | solution.py:604
  50.5 7.5 %copy-start.10 = (bf16[4,64,768]{2,1,0:T(8,128)(2,1)}, bf16[4,64,768]{2,1,0:T(8,128)(2,1)S(1)}, u32[]{:S(2)}) copy-start(bf16[4,64,768]{2,1,0:T(8,128)(2,1)S(1)} %collective-permute-done.3.refs_1_) | copy-start | bytes 1179652
  50.6 7.5 %collective-permute-start.5 = (bf16[2,64,768]{2,1,0:T(8,128)(2,1)S(1)}, bf16[2,64,768]{2,1,0:T(8,128)(2,1)S(1)}, u32[]{:S(2)}, u32[]{:S(2)}) collective-permute-start(bf16[2,64,768]{2,1,0:T(8,128)(2,1)S(1)} %slice.91), channel_id=1, source_target_pairs={{0,32},{1,33},{2,34},{3,35},{4,36},{5,37},{6,38},{7,39},{8,40},{9,... | collective-permute-start | bytes 589832 | tf_op jit(solution)/shard_map/gather_tokens/ppermute | solution.py:604
  51.6 6.4 %copy-start.11 = (bf16[4,64,768]{2,1,0:T(8,128)(2,1)}, bf16[4,64,768]{2,1,0:T(8,128)(2,1)S(1)}, u32[]{:S(2)}) copy-start(bf16[4,64,768]{2,1,0:T(8,128)(2,1)S(1)} %collective-permute-done.4.refs_2_) | copy-start | bytes 1179652
  51.7 6.4 %collective-permute-start.6 = (bf16[2,64,768]{2,1,0:T(8,128)(2,1)S(1)}, bf16[2,64,768]{2,1,0:T(8,128)(2,1)S(1)}, u32[]{:S(2)}, u32[]{:S(2)}) collective-permute-start(bf16[2,64,768]{2,1,0:T(8,128)(2,1)S(1)} %slice.92), channel_id=1, source_target_pairs={{0,96},{1,97},{2,98},{3,99},{4,100},{5,101},{6,102},{7,103},{8,104... | collective-permute-start | bytes 589832 | tf_op jit(solution)/shard_map/gather_tokens/ppermute | solution.py:604
  55.2 2.9 %copy-start.23 = (bf16[2,64,768]{2,1,0:T(8,128)(2,1)}, bf16[2,64,768]{2,1,0:T(8,128)(2,1)S(1)}, u32[]{:S(2)}) copy-start(bf16[2,64,768]{2,1,0:T(8,128)(2,1)S(1)} %collective-permute-done.12.refs_8_) | copy-start | bytes 589828
  55.2 2.9 %copy-start.24 = (bf16[2,64,768]{2,1,0:T(8,128)(2,1)}, bf16[2,64,768]{2,1,0:T(8,128)(2,1)S(1)}, u32[]{:S(2)}) copy-start(bf16[2,64,768]{2,1,0:T(8,128)(2,1)S(1)} %collective-permute-done.13.refs_9_) | copy-start | bytes 589828
  58.0 0.7 copy-start.25
  58.0 0.7 copy-start.26
  72.0 13.3 %all-to-all-start = ((bf16[16,64,128]{2,1,0:T(8,128)(2,1)}), bf16[16,64,128]{2,1,0:T(8,128)(2,1)S(1)}, u32[]{:S(2)}, u32[]{:S(2)}) async-start(bf16[16,64,128]{2,1,0:T(8,128)(2,1)} %get-tuple-element.46), calls=%async_computation | async-start | bytes 524288 | tf_op jit(solution)/shard_map/attention/all_to_all | solution.py:591
  76.5 85.9 %reduce-scatter.2.cloned.1.call-start = ((), (), s32[]{:S(2)}) async-start(), calls=%async_computation.7 | async-start | bytes 11943936 | tf_op jit(solution)/shard_map/feed_forward/reduce_scatter | solution.py:724
  85.2 0.7 copy-start.6
  102.6 1.0 copy-start.7
  102.7 90.6 %all-gather.4.cloned.1.call-start = ((), (), s32[]{:S(2)}) async-start(), calls=%async_computation.6 | async-start | bytes 3981312 | tf_op jit(solution)/shard_map/gather_weights/all_gather | solution.py:683
  129.3 35.6 %all-to-all-start.2 = ((bf16[16,64,384]{2,1,0:T(8,128)(2,1)}), bf16[16,64,384]{2,1,0:T(8,128)(2,1)S(1)}, u32[]{:S(2)}, u32[]{:S(2)}) async-start(bf16[16,64,384]{2,1,0:T(8,128)(2,1)} %get-tuple-element.56), calls=%async_computation.2 | async-start | bytes 1572864 | tf_op jit(solution)/shard_map/attention_back/all_to_all | solution.py:591
  164.8 0.9 copy-start.1
  165.7 47.9 %all-to-all-start.3 = ((bf16[16,54,768]{2,1,0:T(8,128)(2,1)}), bf16[16,54,768]{2,1,0:T(8,128)(2,1)S(1)}, u32[]{:S(2)}, u32[]{:S(2)}) async-start(bf16[16,54,768]{2,1,0:T(8,128)(2,1)} %reduce_scatter.11), calls=%async_computation.4 | async-start | bytes 2752512 | tf_op jit(solution)/shard_map/sum_over_ctx/all_to_all | solution.py:591
  201.4 1.5 collective-permute-start.18
  204.7 5.3 %collective-permute-start.19 = (bf16[104,192]{1,0:T(8,128)(2,1)S(1)}, bf16[104,192]{1,0:T(8,128)(2,1)S(1)}, u32[]{:S(2)}, u32[]{:S(2)}) collective-permute-start(bf16[104,192]{1,0:T(8,128)(2,1)S(1)} %get-tuple-element.85), channel_id=1, source_target_pairs={{0,2},{1,3},{2,4},{3,5},{4,6},{5,7},{6,0},{7,1},{8,10},{9,11},{10,... | collective-permute-start | bytes 119816 | tf_op jit(solution)/shard_map/token_gradient/ppermute | solution.py:604
  205.1 5.3 %collective-permute-start.20 = (bf16[104,192]{1,0:T(8,128)(2,1)S(1)}, bf16[104,192]{1,0:T(8,128)(2,1)S(1)}, u32[]{:S(2)}, u32[]{:S(2)}) collective-permute-start(bf16[104,192]{1,0:T(8,128)(2,1)S(1)} %get-tuple-element.84), channel_id=1, source_target_pairs={{0,6},{1,7},{2,0},{3,1},{4,2},{5,3},{6,4},{7,5},{8,14},{9,15},{10,... | collective-permute-start | bytes 119816 | tf_op jit(solution)/shard_map/token_gradient/ppermute | solution.py:604
  208.0 5.6 %collective-permute-start.21 = (bf16[104,192]{1,0:T(8,128)(2,1)S(1)}, bf16[104,192]{1,0:T(8,128)(2,1)S(1)}, u32[]{:S(2)}, u32[]{:S(2)}) collective-permute-start(bf16[104,192]{1,0:T(8,128)(2,1)S(1)} %get-tuple-element.83), channel_id=1, source_target_pairs={{0,4},{1,5},{2,6},{3,7},{4,0},{5,1},{6,2},{7,3},{8,12},{9,13},{10,... | collective-permute-start | bytes 119816 | tf_op jit(solution)/shard_map/token_gradient/ppermute | solution.py:604
  210.1 3.5 %copy-start.12 = (bf16[104,192]{1,0:T(8,128)(2,1)}, bf16[104,192]{1,0:T(8,128)(2,1)S(1)}, u32[]{:S(2)}) copy-start(bf16[104,192]{1,0:T(8,128)(2,1)S(1)} %collective-permute-done.19.left) | copy-start | bytes 119812
  210.4 3.2 %copy-start.13 = (bf16[104,192]{1,0:T(8,128)(2,1)}, bf16[104,192]{1,0:T(8,128)(2,1)S(1)}, u32[]{:S(2)}) copy-start(bf16[104,192]{1,0:T(8,128)(2,1)S(1)} %collective-permute-done.20.right) | copy-start | bytes 119812
  213.6 0.6 copy-start.14
  213.6 1.1 copy-start
Sparse Core Ops, SparseCore 0:
  13.3 61.5 all-gather.5
  102.8 59.5 reduce-scatter.1
  164.2 28.9 all-gather.3

commit v3 on v2

--- a/solution.py
+++ b/solution.py
@@ -18,6 +18,7 @@
 QT = 512
 KT = 512
 EPSILON = 1e-05
+SCALE_LOG2 = DEPTH ** -0.5 * 1.4426950408889634
 NEGATIVE = -1e30
 VMEM_LIMIT = 56 * 1024 * 1024
 
@@ -37,8 +38,8 @@
 VECTOR_WIDTH = sum(width for _, width in VECTORS)
 
 OUT_AT, UP_AT, DOWN_AT, PACK_ROWS = 0, 96, 480, 864
-CTX_ROWS = PACK_ROWS // CTX
-LAST_ROWS = CTX_ROWS + 26
+SHARE = PACK_ROWS // CTX
+EARLY_ROWS = 32
 
 
 def dot(left, right):
@@ -104,6 +105,20 @@
     )
 
 
+def packed_weights(out_weight, up_weight, down_weight):
+    def kernel(out_weight, up_weight, down_weight, pack):
+        pack[OUT_AT:UP_AT, :] = out_weight[...]
+        for j in range(HIDDEN // WIDTH):
+            pack[UP_AT + 96 * j : UP_AT + 96 * (j + 1), :] = up_weight[
+                :, j * WIDTH : (j + 1) * WIDTH
+            ]
+        pack[DOWN_AT:PACK_ROWS, :] = down_weight[...]
+
+    return vmem_call(
+        kernel, [jax.ShapeDtypeStruct((PACK_ROWS, WIDTH), BF)], [], 10**6, 3
+    )(out_weight, up_weight, down_weight)[0]
+
+
 def normalised_rows(tokens):
     def kernel(tokens, hat):
         hat[...] = normalise(tokens[...].astype(F32))[0].astype(BF)
@@ -115,21 +130,21 @@
 
 def head_forward_kernel(
     order, where, blocks, weight, bias, gain, shift,
-    packed, normed, query, key, value, query_t, key_t, out_t, lse,
+    packed, hats, query, key, value, query_t, key_t, out_t, lse,
     value_t,
 ):
     at_z, at_x = where[0] // SIDE, lax.rem(where[0], SIDE)
 
     for half, offsets, block in blocks:
         count = len(offsets)
-        hat = block[...].reshape(count * HALF, WIDTH).astype(F32)
-        low = (hat * gain[...] + shift[...]).astype(BF)
+        hat_low = block[...].reshape(count * HALF, WIDTH)
+        low = (hat_low.astype(F32) * gain[...] + shift[...]).astype(BF)
         made = (dot(low, weight[...]) + bias[...]).astype(BF)
         for n, (dz, dx) in enumerate(offsets):
             place = order[lax.rem(at_z + dz, SIDE) * SIDE + lax.rem(at_x + dx, SIDE)]
             to = block_at(place if half == 0 else 2 * CTX - 1 - place)
             rows = slice(n * HALF, (n + 1) * HALF)
-            normed[to, :] = low[rows]
+            hats[to, :] = hat_low[rows]
             query[to, :] = made[rows, 0:DEPTH]
             key[to, :] = made[rows, DEPTH : 2 * DEPTH]
             value[to, :] = made[rows, 2 * DEPTH :]
@@ -149,14 +164,14 @@
         def step(j, carry, masked):
             top, total, acc = carry
             rows = lanes_at(j, KT)
-            scores = dot(key[rows, :], queries) * (DEPTH ** -0.5)
+            scores = dot(key[rows, :], queries) * SCALE_LOG2
             if masked:
                 key_place = j * KT + lax.broadcasted_iota(jnp.int32, (KT, QT), 0)
                 query_place = i * QT + lax.broadcasted_iota(jnp.int32, (KT, QT), 1)
                 scores = jnp.where(key_place <= query_place, scores, NEGATIVE)
             fresh = jnp.maximum(top, jnp.max(scores, axis=0, keepdims=True))
-            raised = jnp.exp(scores - fresh)
-            fade = jnp.exp(top - fresh)
+            raised = jnp.exp2(scores - fresh)
+            fade = jnp.exp2(top - fresh)
             total = total * fade + jnp.sum(raised, axis=0, keepdims=True)
             acc = acc * fade + dot(value_t[:, rows], raised.astype(BF))
             return fresh, total, acc
@@ -178,7 +193,7 @@
         top, total, acc = carry
         result = acc / total
         out_t[:, lanes] = result
-        lse[pl.ds(i, 1), :] = top + jnp.log(total)
+        lse[pl.ds(i, 1), :] = top + jnp.log2(total)
         return 0
 
     loop(SEQ // QT, attend)
@@ -191,14 +206,14 @@
         block_refs, refs = refs[: len(layout)], refs[len(layout) :]
         (
             weight, bias, gain, shift,
-            packed, normed, query, key, value, query_t, key_t, out_t, lse,
+            packed, hats, query, key, value, query_t, key_t, out_t, lse,
             value_t, out_rows,
         ) = refs
         head_forward_kernel(
             order, where,
             [(half, offsets, ref) for (half, offsets), ref in zip(layout, block_refs)],
             weight, bias, gain, shift,
-            packed, normed, query, key, value, query_t, key_t, out_t, lse,
+            packed, hats, query, key, value, query_t, key_t, out_t, lse,
             value_t,
         )
 
@@ -271,16 +286,14 @@
 
             def step(j, masked):
                 rows = lanes_at(j, KT)
-                scores = dot(key[rows, :], query_t[:, lanes]) * (DEPTH ** -0.5)
-                probs = jnp.exp(scores - lse[pl.ds(i, 1), :])
+                scores = dot(key[rows, :], query_t[:, lanes]) * SCALE_LOG2
+                probs = jnp.exp2(scores - lse[pl.ds(i, 1), :])
                 if masked:
                     key_place = j * KT + lax.broadcasted_iota(jnp.int32, (KT, QT), 0)
                     query_place = i * QT + lax.broadcasted_iota(jnp.int32, (KT, QT), 1)
                     probs = jnp.where(key_place <= query_place, probs, 0.0)
                 slopes = dot(value[rows, :], grad_out_t[:, lanes])
-                grad_scores = (
-                    probs * (slopes - delta[pl.ds(i, 1), :]) * (DEPTH ** -0.5)
-                ).astype(BF)
+                grad_scores = (probs * (slopes - delta[pl.ds(i, 1), :])).astype(BF)
                 grad_v[rows, :] += dot(probs.astype(BF), grad_out[lanes, :])
                 grad_k[rows, :] += dot(grad_scores, query[lanes, :])
                 grad_q_t[:, lanes] += dot(key_t[:, rows], grad_scores)
@@ -300,8 +313,8 @@
 
         def finish(t, sums):
             rows = lanes_at(t, QT)
-            low_q = grad_q_t[:, rows].T.astype(BF)
-            low_k = grad_k[rows, :].astype(BF)
+            low_q = (grad_q_t[:, rows].T * (DEPTH ** -0.5)).astype(BF)
+            low_k = (grad_k[rows, :] * (DEPTH ** -0.5)).astype(BF)
             low_v = grad_v[rows, :].astype(BF)
             joined = jnp.concatenate(
                 [low_q.astype(F32), low_k.astype(F32), low_v.astype(F32)], axis=1
@@ -350,21 +363,6 @@
     )(order, upstream, query, key, value, query_t, key_t, out_t, lse)
 
 
-def head_weight_grad(normed, rows):
-    def kernel(normed, rows, out):
-        out[...] = (
-            dot_tn(normed[...], rows[...]).astype(BF).reshape(FSDP, WIDTH // FSDP, 3 * DEPTH)
-        )
-
-    return vmem_call(
-        kernel,
-        [jax.ShapeDtypeStruct((FSDP, WIDTH // FSDP, 3 * DEPTH), BF)],
-        [],
-        2 * SEQ * WIDTH * 3 * DEPTH,
-        2,
-    )(normed, rows)[0]
-
-
 def unpack_heads(ref, lanes):
     upper, lower = [], []
     for head in range(HEADS):
@@ -388,14 +386,30 @@
     return active, grad
 
 
-def feed_forward(tokens, heads_out, cotangent, pack, out_bias, gain, shift, up_bias, down_bias):
+def pack_piece(source, held, sems, index):
+    if index == 0:
+        rows = (slice(0, FSDP), pl.ds(OUT_AT, 96))
+    elif index <= 4:
+        rows = (slice(0, FSDP), pl.ds(UP_AT + 96 * (index - 1), 96))
+    else:
+        rows = (pl.ds(2 * (index - 5), 2), pl.ds(DOWN_AT, 384))
+    return pltpu.make_async_copy(source.at[rows], held.at[rows], sems.at[index])
+
+
+def feed_forward(pack, tokens, heads_out, cotangent, out_bias, gain, shift, up_bias, down_bias):
     def kernel(
-        tokens, heads_out, cotangent, pack, out_bias, gain, shift, up_bias, down_bias,
-        mixed, pack_grad, grad_heads, grad_residual, vector_sums, up_sums,
+        source, tokens, heads_out, cotangent, out_bias, gain, shift, up_bias, down_bias,
+        mixed, mix_grad, grad_heads, grad_residual, vector_sums, up_sums,
+        pack, sems,
     ):
+        order = [0] + [index for j in range(4) for index in (1 + j, 5 + j)]
+        copies = {index: pack_piece(source, pack, sems, index) for index in order}
+        for index in order:
+            copies[index].start()
         inputs = tokens[...].astype(F32)
         result_grad = cotangent[...]
         attended_low = unpack_heads(heads_out, 0)
+        copies[0].wait()
         w_out = pack[:, OUT_AT:UP_AT, :].reshape(WIDTH, WIDTH)
         residual = inputs + dot(attended_low, w_out) + out_bias[...]
         hat, inverse = normalise(residual)
@@ -405,17 +419,20 @@
         grad_normed = jnp.zeros((ROWS, WIDTH), F32)
         for j in range(HIDDEN // WIDTH):
             lanes = slice(j * WIDTH, (j + 1) * WIDTH)
+            copies[1 + j].wait()
             w_up = pack[:, UP_AT + 96 * j : UP_AT + 96 * (j + 1), :].reshape(WIDTH, WIDTH)
+            hidden = dot(low, w_up) + up_bias[:, lanes]
+            copies[5 + j].wait()
             w_down = pack[2 * j : 2 * j + 2, DOWN_AT:PACK_ROWS, :].reshape(WIDTH, WIDTH)
-            hidden = dot(low, w_up) + up_bias[:, lanes]
+            upstream = dot_nt(result_grad, w_down)
             acted, slope = gelu_parts(hidden)
             acted = acted.astype(BF)
-            pack_grad[2 * j : 2 * j + 2, DOWN_AT:PACK_ROWS, :] = (
+            mix_grad[2 * j : 2 * j + 2, DOWN_AT:, :] = (
                 dot(acted.T, result_grad).astype(BF).reshape(2, 384, WIDTH)
             )
             total = total + dot(acted, w_down)
-            pre = (dot_nt(result_grad, w_down) * slope).astype(BF)
-            pack_grad[:, UP_AT + 96 * j : UP_AT + 96 * (j + 1), :] = (
+            pre = (upstream * slope).astype(BF)
+            mix_grad[:, UP_AT + 96 * j : UP_AT + 96 * (j + 1), :] = (
                 dot(low_t, pre).astype(BF).reshape(FSDP, 96, WIDTH)
             )
             up_sums[:, lanes] = jnp.sum(pre.astype(F32), axis=0, keepdims=True)
@@ -424,13 +441,6 @@
         back = result_grad.astype(F32) + norm_back(grad_normed, hat, inverse, gain[...])
         grad_residual[...] = back
         branch = back.astype(BF)
-        pack_grad[:, OUT_AT:UP_AT, :] = (
-            dot(attended_low.T, branch).astype(BF).reshape(FSDP, 96, WIDTH)
-        )
-        vector_sums[0:1, :] = jnp.sum(branch.astype(F32), axis=0, keepdims=True)
-        vector_sums[1:2, :] = jnp.sum(grad_normed * hat, axis=0, keepdims=True)
-        vector_sums[2:3, :] = jnp.sum(grad_normed, axis=0, keepdims=True)
-        vector_sums[3:4, :] = jnp.sum(result_grad.astype(F32), axis=0, keepdims=True)
         grad_attended = dot_nt(branch, w_out)
         for head in range(HEADS):
             lanes = slice(head * DEPTH, (head + 1) * DEPTH)
@@ -439,59 +449,82 @@
             ).astype(BF)
         for head in range(HEADS, CTX):
             grad_heads[head] = jnp.zeros((HALF, 2 * DEPTH), BF)
+        mix_grad[:, OUT_AT:UP_AT, :] = (
+            dot(attended_low.T, branch).astype(BF).reshape(FSDP, 96, WIDTH)
+        )
+        vector_sums[0:1, :] = jnp.sum(branch.astype(F32), axis=0, keepdims=True)
+        vector_sums[1:2, :] = jnp.sum(grad_normed * hat, axis=0, keepdims=True)
+        vector_sums[2:3, :] = jnp.sum(grad_normed, axis=0, keepdims=True)
+        vector_sums[3:4, :] = jnp.sum(result_grad.astype(F32), axis=0, keepdims=True)
 
     shape = jax.ShapeDtypeStruct
+    outs = [
+        shape((ROWS, WIDTH), BF),
+        shape((FSDP, PACK_ROWS, WIDTH), BF),
+        shape((CTX, HALF, 2 * DEPTH), BF),
+        shape((ROWS, WIDTH), F32),
+        shape((4, WIDTH), F32),
+        shape((1, HIDDEN), F32),
+    ]
+    return pl.pallas_call(
+        kernel,
+        out_shape=outs,
+        in_specs=[pl.BlockSpec(memory_space=pl.ANY)]
+        + [pl.BlockSpec(memory_space=pltpu.VMEM)] * 8,
+        out_specs=[pl.BlockSpec(memory_space=pltpu.VMEM)] * len(outs),
+        scratch_shapes=[
+            pltpu.VMEM((FSDP, PACK_ROWS, WIDTH), BF),
+            pltpu.SemaphoreType.DMA((9,)),
+        ],
+        compiler_params=pltpu.CompilerParams(vmem_limit_bytes=VMEM_LIMIT),
+        cost_estimate=pl.CostEstimate(
+            flops=4 * 10**9, bytes_accessed=24 * 2**20, transcendentals=4 * 10**5
+        ),
+    )(pack, tokens, heads_out, cotangent, out_bias, gain, shift, up_bias, down_bias)
+
+
+def token_gradient(weight, tokens, heads_grad, gain, grad_residual):
+    def kernel(weight, tokens, heads_grad, gain, grad_residual, tokens_grad):
+        hat, inverse = normalise(tokens[...].astype(F32))
+        projected = jnp.concatenate(
+            [unpack_heads(heads_grad, 2 * DEPTH * part) for part in range(3)], axis=1
+        )
+        grad_normed = dot_nt(projected, weight[...])
+        tokens_grad[...] = grad_residual[...] + norm_back(grad_normed, hat, inverse, gain[...])
+
     return vmem_call(
         kernel,
-        [
-            shape((ROWS, WIDTH), BF),
-            shape((FSDP, PACK_ROWS, WIDTH), BF),
-            shape((CTX, HALF, 2 * DEPTH), BF),
-            shape((ROWS, WIDTH), F32),
-            shape((4, WIDTH), F32),
-            shape((1, HIDDEN), F32),
-        ],
-        [],
-        4 * 10**9,
-        9,
-    )(tokens, heads_out, cotangent, pack, out_bias, gain, shift, up_bias, down_bias)
-
-
-def token_gradient(tokens, heads_grad, weight, gain, grad_residual):
-    def kernel(tokens, heads_grad, weight, gain, grad_residual, tokens_grad, sums):
-        projected = jnp.concatenate(
-            [unpack_heads(heads_grad, 2 * DEPTH * part) for part in range(3)], axis=1
-        )
-        grad_normed = dot_nt(projected, weight[...])
-        hat, inverse = normalise(tokens[...].astype(F32))
-        tokens_grad[...] = grad_residual[...] + norm_back(grad_normed, hat, inverse, gain[...])
-        sums[0:1, :] = jnp.sum(grad_normed * hat, axis=0, keepdims=True)
-        sums[1:2, :] = jnp.sum(grad_normed, axis=0, keepdims=True)
-
-    shape = jax.ShapeDtypeStruct
-    return vmem_call(
-        kernel,
-        [shape((ROWS, WIDTH), F32), shape((2, WIDTH), F32)],
+        [jax.ShapeDtypeStruct((ROWS, WIDTH), F32)],
         [],
         2 * ROWS * WIDTH * 3 * WIDTH,
         5,
-    )(tokens, heads_grad, weight, gain, grad_residual)
-
-
-def small_slots(place, weight_grad, bias_sums, first_sums, vector_sums, up_sums):
-    def kernel(place, weight_grad, bias_sums, first_sums, vector_sums, up_sums, slots):
-        slots[:, :96, :] = weight_grad[...]
+    )(weight, tokens, heads_grad, gain, grad_residual)[0]
+
+
+def early_slots(where, hats, rows, weight, gain, shift, bias_sums, vector_sums, up_sums):
+    def kernel(where, hats, rows, weight, gain, shift, bias_sums, vector_sums, up_sums, slots):
+        place = where[0]
+
+        made = dot_tn(rows[...], hats[...])
+        column = jnp.broadcast_to(bias_sums[...], (8, 3 * DEPTH)).T[:, :1]
+        weight_t = weight[...].astype(F32).T
+        first_gain = jnp.sum(weight_t * made, axis=0, keepdims=True)
+        first_shift = jnp.sum(weight_t * column, axis=0, keepdims=True)
+        weight_grad = (made * gain[...] + column * shift[...]).T
+        for owner in range(FSDP):
+            slots[owner, :96, :] = weight_grad[96 * owner : 96 * (owner + 1)].astype(BF)
+
         tall = jnp.zeros((2, 3 * DEPTH), F32)
         bias_rows = []
         for part in (0, 2):
             piece = bias_sums[:, part * DEPTH : (part + 1) * DEPTH]
             for head in range(HEADS):
-                bias_rows.append(jnp.where(place[0] == head, piece, 0.0))
+                bias_rows.append(jnp.where(place == head, piece, 0.0))
         for owner in range(FSDP):
             lanes = slice(96 * owner, 96 * (owner + 1))
             values = dict(
-                first_gain=first_sums[0:1, lanes],
-                first_shift=first_sums[1:2, lanes],
+                first_gain=first_gain[:, lanes],
+                first_shift=first_shift[:, lanes],
                 qv_bias=jnp.concatenate(bias_rows[3 * owner : 3 * owner + 3], axis=1),
                 out_bias=vector_sums[0:1, lanes],
                 second_gain=vector_sums[1:2, lanes],
@@ -500,87 +533,91 @@
                 down_bias=vector_sums[3:4, lanes],
             )
             line = jnp.concatenate([values[name] for name, _ in VECTORS], axis=1)
-            rows = [line[:, 192 * r : 192 * (r + 1)] for r in range(6)]
-            slots[owner, 96:104, :] = jnp.concatenate(rows + [tall], axis=0).astype(BF)
+            pieces = [line[:, 192 * r : 192 * (r + 1)] for r in range(6)] + [tall]
+            slots[owner, 96:, :] = jnp.concatenate(pieces, axis=0).astype(BF)
 
     return vmem_call(
         kernel,
         [jax.ShapeDtypeStruct((FSDP, 104, 3 * DEPTH), BF)],
         [],
+        2 * SEQ * WIDTH * 3 * DEPTH,
+        8,
+        smem=1,
+    )(where, hats, rows, weight, gain, shift, bias_sums, vector_sums, up_sums)[0]
+
+
+def early_sums(parts):
+    def kernel(own, left, right, far, out):
+        total = (
+            own[...].astype(F32) + left[...].astype(F32) + right[...].astype(F32)
+            + far[...].astype(F32)
+        )
+        head = jnp.concatenate([total[24 * k : 24 * (k + 1)] for k in range(4)], axis=1)
+        line = jnp.concatenate([total[96:104], jnp.zeros((8, 9 * DEPTH), F32)], axis=1)
+        out[...] = jnp.concatenate([head, line], axis=0).astype(BF)
+
+    return vmem_call(kernel, [jax.ShapeDtypeStruct((EARLY_ROWS, WIDTH), BF)], [], 10**6, 4)(*parts)[0]
+
+
+def early_grads(pieces):
+    def kernel(pieces, grad_qkv, *vector_refs):
+        lines = jnp.zeros((8, 3 * DEPTH), F32)
+        heads = []
+        for n in range(CTX):
+            piece = pieces[n].astype(F32)
+            lines = lines + piece[24:, : 3 * DEPTH]
+            if n < HEADS:
+                heads.append(
+                    jnp.concatenate(
+                        [piece[:24, 192 * k : 192 * (k + 1)] for k in range(4)], axis=0
+                    )
+                )
+        line = jnp.concatenate([lines[r : r + 1] for r in range(6)], axis=1)
+        at = 0
+        for ref, (_, width) in zip(vector_refs, VECTORS):
+            ref[...] = line[:, at : at + width]
+            at += width
+        for part in range(3):
+            grad_qkv[:, part * WIDTH : (part + 1) * WIDTH] = jnp.concatenate(
+                [head[:, part * DEPTH : (part + 1) * DEPTH] for head in heads], axis=1
+            )
+
+    shape = jax.ShapeDtypeStruct
+    return vmem_call(
+        kernel,
+        [shape((96, 3 * WIDTH), F32)] + [shape((1, width), F32) for _, width in VECTORS],
+        [],
         10**6,
-        5,
-        smem=1,
-    )(place, weight_grad, bias_sums, first_sums, vector_sums, up_sums)[0]
-
-
-def last_pieces(parts, smalls):
-    def kernel(parts, own, left, right, far, out):
+        1,
+    )(pieces)
+
+
+def last_pieces(parts):
+    def kernel(parts, out):
         total = parts[0].astype(F32)
         for source in range(1, CTX):
             total = total + parts[source].astype(F32)
-        small = (
-            own[...].astype(F32) + left[...].astype(F32) + right[...].astype(F32)
-            + far[...].astype(F32)
-        )
-        wide = jnp.concatenate([small[24 * k : 24 * (k + 1)] for k in range(4)], axis=1)
-        line = jnp.concatenate(
-            [
-                jnp.concatenate([small[96 + r : 97 + r] for r in range(4)], axis=1),
-                jnp.concatenate(
-                    [small[100:101], small[101:102], jnp.zeros((1, 6 * DEPTH), F32)], axis=1
-                ),
-            ],
-            axis=0,
-        )
-        joined = jnp.concatenate([total, wide, line], axis=0).astype(BF)
+        total = total.astype(BF)
         for target in range(CTX):
-            out[target] = joined
+            out[target] = total
 
     return vmem_call(
-        kernel,
-        [jax.ShapeDtypeStruct((CTX, LAST_ROWS, WIDTH), BF)],
-        [],
-        10**6,
-        5,
-    )(parts, *smalls)[0]
-
-
-def final_grads(pieces):
-    def kernel(pieces, grad_qkv, grad_out, grad_up, grad_down, *vector_refs):
-        shard = jnp.concatenate([pieces[n][:CTX_ROWS].astype(F32) for n in range(CTX)], axis=0)
+        kernel, [jax.ShapeDtypeStruct((CTX, SHARE, WIDTH), BF)], [], 10**6, 1
+    )(parts)[0]
+
+
+def last_grads(pieces):
+    def kernel(pieces, grad_out, grad_up, grad_down):
+        shard = jnp.concatenate([pieces[n].astype(F32) for n in range(CTX)], axis=0)
         grad_out[...] = shard[OUT_AT:UP_AT]
         for j in range(HIDDEN // WIDTH):
             grad_up[:, j * WIDTH : (j + 1) * WIDTH] = shard[UP_AT + 96 * j : UP_AT + 96 * (j + 1)]
         grad_down[...] = shard[DOWN_AT:]
-        lines = jnp.zeros((2, WIDTH), F32)
-        for n in range(CTX):
-            lines = lines + pieces[n][CTX_ROWS + 24 : CTX_ROWS + 26].astype(F32)
-        line = jnp.concatenate([lines[0:1], lines[1:2]], axis=1)
-        at = 0
-        for ref, (_, width) in zip(vector_refs, VECTORS):
-            ref[...] = line[:, at : at + width]
-            at += width
-        heads = []
-        for head in range(HEADS):
-            wide = pieces[head][CTX_ROWS : CTX_ROWS + 24].astype(F32)
-            heads.append(
-                jnp.concatenate([wide[:, 192 * k : 192 * (k + 1)] for k in range(4)], axis=0)
-            )
-        for part in range(3):
-            grad_qkv[:, part * WIDTH : (part + 1) * WIDTH] = jnp.concatenate(
-                [head[:, part * DEPTH : (part + 1) * DEPTH] for head in heads], axis=1
-            )
 
     shape = jax.ShapeDtypeStruct
     return vmem_call(
         kernel,
-        [
-            shape((96, 3 * WIDTH), F32),
-            shape((96, WIDTH), F32),
-            shape((96, HIDDEN), F32),
-            shape((384, WIDTH), F32),
-        ]
-        + [shape((1, width), F32) for _, width in VECTORS],
+        [shape((96, WIDTH), F32), shape((96, HIDDEN), F32), shape((384, WIDTH), F32)],
         [],
         10**6,
         1,
@@ -589,6 +626,10 @@
 
 def swap(slots, axes):
     return lax.all_to_all(slots, axes, 0, 0, tiled=True)
+
+
+def spread(piece, axes, count):
+    return swap(jnp.broadcast_to(piece[None], (count,) + piece.shape), axes)
 
 
 def shift_by(value, z=0, x=0, y=0, core=0):
@@ -604,11 +645,11 @@
     return lax.ppermute(value, ("ctx", "fsdp"), pairs)
 
 
-def gather_rows(hat):
+def gather_rows(values):
     blocks = []
     steps = (0, SIDE - 1, 1, 2)
     for half, first, second in ((0, "x", "z"), (1, "z", "x")):
-        mine = hat[half * HALF : (half + 1) * HALF]
+        mine = values[half * HALF : (half + 1) * HALF]
         near = jnp.stack([mine] + [shift_by(mine, **{first: by}) for by in (1, -1, 2)])
         ahead, behind = shift_by(near, **{second: 1}), shift_by(near, **{second: -1})
         far_one = shift_by(ahead[:2], **{second: 1})
@@ -673,14 +714,8 @@
     with jax.named_scope("gather_tokens"):
         blocks = gather_rows(normalised_rows(my_tokens))
     with jax.named_scope("gather_weights"):
-        pack = jnp.concatenate(
-            [out_weight]
-            + [up_weight[:, j * WIDTH : (j + 1) * WIDTH] for j in range(HIDDEN // WIDTH)]
-            + [down_weight],
-            axis=0,
-        )
+        pack = packed_weights(out_weight, up_weight, down_weight)
         pack = lax.all_gather(pack, "fsdp", axis=0, tiled=False)
-        w_qkv = lax.all_gather(qkv_weight, "fsdp", axis=0, tiled=True)
     with jax.named_scope("gather_small"):
         head_columns = jnp.concatenate(
             [
@@ -709,43 +744,54 @@
         )
 
     with jax.named_scope("attention"):
-        packed, normed, query, key, value, query_t, key_t, out_t, lse = head_forward(
+        packed, hats, query, key, value, query_t, key_t, out_t, lse = head_forward(
             pair_order, where, blocks, w_head, head_bias, whole["first_gain"],
             whole["first_shift"],
         )
         heads_out = swap(packed, "ctx")
 
     with jax.named_scope("feed_forward"):
-        mixed, pack_grad, grad_heads, grad_residual, vector_sums, up_sums = feed_forward(
-            my_tokens, heads_out, my_cotangent, pack, whole["out_bias"], whole["second_gain"],
+        mixed, mix_grad, grad_heads, grad_residual, vector_sums, up_sums = feed_forward(
+            pack, my_tokens, heads_out, my_cotangent, whole["out_bias"], whole["second_gain"],
             whole["second_shift"], whole["up_bias"], whole["down_bias"],
         )
+        mix_shard = lax.psum_scatter(mix_grad, "fsdp", scatter_dimension=0, tiled=False)
         heads_up = swap(grad_heads, "ctx")
-        shard_grad = lax.psum_scatter(pack_grad, "fsdp", scatter_dimension=0, tiled=False)
 
     with jax.named_scope("attention_back"):
         packed_grad, low_rows, bias_sums = head_backward(
             pair_order, heads_up, query, key, value, query_t, key_t, out_t, lse
         )
         heads_grad = swap(packed_grad, "ctx")
-        weight_grad = head_weight_grad(normed, low_rows)
-
-    with jax.named_scope("token_gradient"):
-        tokens_grad, first_sums = token_gradient(
-            my_tokens, heads_grad, w_qkv, whole["first_gain"], grad_residual
-        )
-        smalls = scatter_small(
-            small_slots(where, weight_grad, bias_sums, first_sums, vector_sums, up_sums)
-        )
+
+    with jax.named_scope("early_grads"):
+        early = early_sums(
+            scatter_small(
+                early_slots(
+                    where, hats, low_rows, w_head, whole["first_gain"], whole["first_shift"],
+                    bias_sums, vector_sums, up_sums,
+                )
+            )
+        )
+        early, heads_grad = lax.optimization_barrier((early, heads_grad))
+        early = spread(early, "ctx", CTX)
 
     with jax.named_scope("sum_over_ctx"):
-        parts = swap(shard_grad.reshape(CTX, CTX_ROWS, WIDTH), "ctx")
-        grad_qkv, grad_out, grad_up, grad_down, *vector_grads = final_grads(
-            swap(last_pieces(parts, smalls), "ctx")
-        )
+        mix_shard, early = lax.optimization_barrier((mix_shard, early))
+        parts = swap(mix_shard.reshape(CTX, SHARE, WIDTH), "ctx")
+        shares, early = lax.optimization_barrier((last_pieces(parts), early))
+        grad_out, grad_up, grad_down = last_grads(swap(shares, "ctx"))
+        grad_qkv, *vector_grads = early_grads(early)
         grads = {
             name: grad.reshape(width) for grad, (name, width) in zip(vector_grads, VECTORS)
         }
+
+    with jax.named_scope("token_gradient"):
+        late_weight, heads_grad = lax.optimization_barrier((qkv_weight, heads_grad))
+        w_qkv = lax.all_gather(late_weight, "fsdp", axis=0, tiled=True)
+        tokens_grad = token_gradient(
+            w_qkv, my_tokens, heads_grad, whole["first_gain"], grad_residual
+        )
 
     return (
         mixed[None], tokens_grad[None], grads["first_gain"], grads["first_shift"], grad_qkv,

time: 264 us -> 231 us (0.88)
  waiting for transfers between devices: 65.2 us -> 29.5 us
  blocking collectives: 45.5 us -> 53.7 us
  local copies, waits for them, and re-layouts: 21.5 us -> 16.3 us
    reduce_scatter x1, waiting for transfers between devices: 29.5 us -> 0.01 us  [local(): lax.psum_scatter(mix_grad, 'fsdp', scatter_dimension=0, tiled=False)]
    all_gather x1, waiting for transfers between devices: 16.3 us -> 0.02 us  [local(): w_qkv = lax.all_gather(late_weight, 'fsdp', axis=0, tiled=True)]
    all_to_all x3, waiting for transfers between devices: 5.1 us -> 15.1 us  [swap(): return lax.all_to_all(slots, axes, 0, 0, tiled=True)]
    all_to_all x2 -> x3, blocking collectives: 45.5 us -> 53.7 us  [swap(): return lax.all_to_all(slots, axes, 0, 0, tiled=True)]
    unnamed x65 -> x56, local copies, waits for them, and re-layouts: 10.6 us -> 5.28 us
    all_to_all x3, starting transfers between devices: 15.1 us -> 11.9 us  [swap(): return lax.all_to_all(slots, axes, 0, 0, tiled=True)]
    pallas_call x6 -> x8, Pallas kernels: 34.9 us -> 37.5 us  [the longest x1 16.4 us: feed_forward(): pl.pallas_call(kernel, out_shape=outs, in_specs=[pl.BlockSpec(memory_spac...]
  transfers between devices with their start and end apart: 28 -> 28, of which waited for: 12 -> 11; matrix products, arithmetic and copies ran while one was open for 5% -> 7% of each run, Pallas kernels for 15% -> 19%
where the time goes in v3:
time: 231 us; the launch traced here: 230 us
  Pallas kernels  65.4 us (28%)
  blocking collectives  53.7 us (23%)
  starting transfers between devices  45.7 us (20%)
  waiting for transfers between devices  29.5 us (13%)
  local copies, waits for them, and re-layouts  16.3 us (7%)
  between operations  14.4 us (6%)
  other arithmetic  4.68 us (2%)
    all_to_all x3, blocking collectives, swap(): return lax.all_to_all(slots, axes, 0, 0, tiled=True)  53.7 us
    ppermute x22, starting transfers between devices, shift_by(): return lax.ppermute(value, ('ctx', 'fsdp'), pairs)  33.5 us
    pallas_call x1, Pallas kernels, feed_forward(): pl.pallas_call(kernel, out_shape=outs, in_specs=[pl.BlockSpec(memory_spac...  16.4 us
    all_to_all x3, waiting for transfers between devices, swap(): return lax.all_to_all(slots, axes, 0, 0, tiled=True)  15.1 us
    ppermute x22, waiting for transfers between devices, shift_by(): return lax.ppermute(value, ('ctx', 'fsdp'), pairs)  14.3 us
    pallas_call x1, Pallas kernels, head_backward(): vmem_call(kernel, [shape((CTX, HALF, 6 * DEPTH), BF), shape((SEQ, 3 * DEP...  13.5 us
    pallas_call x1, Pallas kernels, head_forward(): vmem_call(kernel, [shape((CTX, HALF, 2 * DEPTH), BF), shape((SEQ, WIDTH),...  12.5 us
    all_to_all x3, starting transfers between devices, swap(): return lax.all_to_all(slots, axes, 0, 0, tiled=True)  11.9 us
  transfers between devices with their start and end apart: 28, of which 11 were waited for; matrix products, arithmetic and copies ran while one was open for 7% of the time, Pallas kernels for 19%

profile of v3, /device:TPU:0, one launch (start us, length us, event | category | flops | bytes accessed | tf_op | source)
XLA Modules:
  0.0 229.7 jit_solution(13188677664553892763)
XLA Ops:
  7.2 2.5 %gather_weights.1 = bf16[864,768]{1,0:T(8,128)(2,1)} custom-call(bf16[96,768]{1,0:T(8,128)(2,1)} %out_weight.1, bf16[96,3072]{1,0:T(8,128)(2,1)} %up_weight.1, bf16[384,768]{1,0:T(8,128)(2,1)} %down_weight.1), custom_call_target="tpu_custom_call" | custom-call | flops 1000000 | bytes 8388608 | tf_op jit(solution)/shard_map/gather_weights/pallas_call | solution.py:117
  9.8 0.9 constant_dynamic-slice_fusion.4
  11.6 3.2 %collective-permute-start.14 = (bf16[112,192]{0,1:T(8,128)(2,1)S(1)}, bf16[112,192]{0,1:T(8,128)(2,1)S(1)}, u32[]{:S(2)}, u32[]{:S(2)}) collective-permute-start(bf16[112,192]{0,1:T(8,128)(2,1)S(1)} %maximum_maximum_fusion), channel_id=1, source_target_pairs={{0,6},{1,7},{2,0},{3,1},{4,2},{5,3},{6,4},{7,5},{8,14},{9,15},{10,... | collective-permute-start | bytes 129032 | tf_op jit(solution)/shard_map/gather_small/ppermute | solution.py:645
  14.8 0.6 collective-permute-start.15
  15.4 1.0 collective-permute-start.16
  16.4 1.8 gather_tokens.1
  18.2 1.0 slice_bitcast_fusion.3
  19.2 4.0 %collective-permute-start.9 = (bf16[64,768]{1,0:T(8,128)(2,1)S(1)}, bf16[64,768]{1,0:T(8,128)(2,1)S(1)}, u32[]{:S(2)}, u32[]{:S(2)}) collective-permute-start(bf16[64,768]{1,0:T(8,128)(2,1)S(1)} %get-tuple-element.101), channel_id=1, source_target_pairs={{0,64},{1,65},{2,66},{3,67},{4,68},{5,69},{6,70},{7,71},{8,72},{9,... | collective-permute-start | bytes 294920 | tf_op jit(solution)/shard_map/gather_tokens/ppermute | solution.py:645
  23.1 1.0 collective-permute-start.7
  24.4 2.2 collective-permute-start.8
  26.6 1.5 collective-permute-start
  28.1 1.7 collective-permute-start.1
  29.9 1.9 collective-permute-start.2
  31.9 0.7 collective-permute-start.10
  32.6 0.9 collective-permute-done
  33.5 1.7 collective-permute-start.11
  35.2 1.5 collective-permute-done.2
  36.8 3.2 %collective-permute-start.4 = (bf16[4,64,768]{2,1,0:T(8,128)(2,1)S(1)}, bf16[4,64,768]{2,1,0:T(8,128)(2,1)S(1)}, u32[]{:S(2)}, u32[]{:S(2)}) collective-permute-start(bf16[4,64,768]{2,1,0:T(8,128)(2,1)S(1)} %pad_maximum_fusion.refs_0_), channel_id=1, source_target_pairs={{0,96},{1,97},{2,98},{3,99},{4,100},{5,101},{6,102},{7,103},{8,104... | collective-permute-start | bytes 1179656 | tf_op jit(solution)/shard_map/gather_tokens/ppermute | solution.py:645
  41.1 0.7 reshape.109.refs_12_.gain
  41.8 0.7 reshape.110.refs_13_.shift
  42.4 1.0 copy.53
  43.5 1.4 collective-permute-done.10.refs_6_
  45.0 3.3 %collective-permute-start.13 = (bf16[2,64,768]{2,1,0:T(8,128)(2,1)S(1)}, bf16[2,64,768]{2,1,0:T(8,128)(2,1)S(1)}, u32[]{:S(2)}, u32[]{:S(2)}) collective-permute-start(bf16[2,64,768]{2,1,0:T(8,128)(2,1)S(1)} %slice.79), channel_id=1, source_target_pairs={{0,24},{1,25},{2,26},{3,27},{4,28},{5,29},{6,30},{7,31},{8,0},{9,1... | collective-permute-start | bytes 589832 | tf_op jit(solution)/shard_map/gather_tokens/ppermute | solution.py:645
  48.5 3.5 %collective-permute-start.6 = (bf16[2,64,768]{2,1,0:T(8,128)(2,1)S(1)}, bf16[2,64,768]{2,1,0:T(8,128)(2,1)S(1)}, u32[]{:S(2)}, u32[]{:S(2)}) collective-permute-start(bf16[2,64,768]{2,1,0:T(8,128)(2,1)S(1)} %slice.76), channel_id=1, source_target_pairs={{0,96},{1,97},{2,98},{3,99},{4,100},{5,101},{6,102},{7,103},{8,104... | collective-permute-start | bytes 589832 | tf_op jit(solution)/shard_map/gather_tokens/ppermute | solution.py:645
  53.0 2.9 %collective-permute-done.5.refs_3_ = bf16[2,64,768]{2,1,0:T(8,128)(2,1)S(1)} collective-permute-done((bf16[2,64,768]{2,1,0:T(8,128)(2,1)S(1)}, bf16[2,64,768]{2,1,0:T(8,128)(2,1)S(1)}, u32[]{:S(2)}, u32[]{:S(2)}) %collective-permute-start.5) | collective-permute-done | bytes 196640 | tf_op jit(solution)/shard_map/gather_tokens/ppermute | solution.py:645
  55.9 0.6 copy-done.23
  56.6 12.5 %attention.1 = (bf16[16,64,128]{2,1,0:T(8,128)(2,1)}, bf16[2048,768]{1,0:T(8,128)(2,1)}, bf16[2048,64]{1,0:T(8,128)(2,1)}, bf16[2048,64]{1,0:T(8,128)(2,1)}, bf1...) custom-call(s32[16]{0:T(128)} %order.3, ...), custom_call_target="tpu_custom_call" | custom-call | flops 2000000000 | bytes 8388608 | tf_op jit(solution)/shard_map/attention/pallas_call | solution.py:237
  69.1 4.6 %all-to-all-start = ((bf16[16,64,128]{2,1,0:T(8,128)(2,1)}), bf16[16,64,128]{2,1,0:T(8,128)(2,1)S(1)}, u32[]{:S(2)}, u32[]{:S(2)}) async-start(bf16[16,64,128]{2,1,0:T(8,128)(2,1)} %get-tuple-element.52), calls=%async_computation | async-start | bytes 524288 | tf_op jit(solution)/shard_map/attention/all_to_all | solution.py:628
  73.9 0.7 reshape.111.out_bias
  74.6 0.7 reshape.112.gain
  75.2 0.7 reshape.113.shift
  75.9 0.7 reshape.115.down_bias
  76.6 0.6 copy.64
  77.3 5.1 %all-to-all-done.heads_out = bf16[16,64,128]{2,1,0:T(8,128)(2,1)S(1)} async-done(((bf16[16,64,128]{2,1,0:T(8,128)(2,1)}), bf16[16,64,128]{2,1,0:T(8,128)(2,1)S(1)}, u32[]{:S(2)}, u32[]{:S(2)}) %all-to-all-start) | async-done | bytes 262176 | tf_op jit(solution)/shard_map/attention/all_to_all | solution.py:628
  82.4 0.7 copy-done.4
  83.0 16.4 %feed_forward.1 = (bf16[128,768]{1,0:T(8,128)(2,1)}, bf16[8,864,768]{2,1,0:T(8,128)(2,1)}, bf16[16,64,128]{2,1,0:T(8,128)(2,1)}, f32[128,768]{1,0:T(8,128)}, f32[4,768]{1,0:T(4,128)}, /*index=5*/f32[1,3072]{1,0:T(1,128)}) custom-call(bf16[8,864,768]{2,1,0:T(8,128)(2,1)} %bitcast.94, bf16[128,768]{1,0:T(8,128)(2,1)} %bitcast.77, ...), custom_call_target="tpu_custom_call" | custom-call | flops 4000000000 | bytes 25165824 | tf_op jit(solution)/shard_map/feed_forward/pallas_call | solution.py:469
  99.5 0.9 copy-done.5
  100.4 12.0 %all_to_all.30.upstream = bf16[16,64,128]{2,1,0:T(8,128)(2,1)} all-to-all(bf16[16,64,128]{2,1,0:T(8,128)(2,1)S(1)} %copy-done.5), channel_id=1, replica_groups=mesh['ctx'=16,'fsdp'=8] {'ctx'}, dimensions={0} | all-to-all | bytes 524288 | tf_op jit(solution)/shard_map/feed_forward/all_to_all | solution.py:628
  112.3 13.5 %attention_back.1 = (bf16[16,64,384]{2,1,0:T(8,128)(2,1)}, bf16[2048,192]{1,0:T(8,128)(2,1)}, f32[1,192]{1,0:T(1,128)}) custom-call(s32[16]{0:T(128)} %order.3, bf16[16,64,128]{2,1,0:T(8,128)(2,1)} %all_to_all.30.upstream, bf16[2048,64]{1,0:T(8,128)(2,1)} %get-tuple-element.56.query, bf16[2048,64]{1,0:T(8,128)(2,1)} %get-tuple-element.57.key, ...), custom_call_target="tpu_custom_call" | custom-call | flops 4000000000 | bytes 8388608 | tf_op jit(solution)/shard_map/attention_back/pallas_call | solution.py:343
  125.9 3.6 %all-to-all-start.2 = ((bf16[16,64,384]{2,1,0:T(8,128)(2,1)}), bf16[16,64,384]{2,1,0:T(8,128)(2,1)S(1)}, u32[]{:S(2)}, u32[]{:S(2)}) async-start(bf16[16,64,384]{2,1,0:T(8,128)(2,1)} %get-tuple-element.67), calls=%async_computation.2 | async-start | bytes 1572864 | tf_op jit(solution)/shard_map/attention_back/all_to_all | solution.py:628
  129.6 4.5 %early_grads.2 = bf16[8,104,192]{2,1,0:T(8,128)(2,1)} custom-call(s32[1]{0:T(128)} %bitcast.2.where, bf16[2048,768]{1,0:T(8,128)(2,1)} %get-tuple-element.54.hats, bf16[2048,192]{1,0:T(8,128)(2,1)} %get-tuple-element.63.rows, bf16[768,192]{1,0:T(8,128)(2,1)} %bitcast.74, f32[1,768]{1,0:T(1,128)} %reshape.109.refs_12_.gain, ...), custom_call_target="tpu_custom_call" | custom-call | flops 603979776 | bytes 8388608 | tf_op jit(solution)/shard_map/early_grads/pallas_call | solution.py:539
  134.0 1.1 select_bitcast_fusion
  135.3 1.4 collective-permute-done.18
  136.6 1.1 fusion
  137.8 0.7 dynamic-slice_bitcast_fusion
  138.4 1.7 collective-permute-start.19
  140.1 1.5 collective-permute-start.20
  142.2 2.3 %collective-permute-done.19.left = bf16[104,192]{1,0:T(8,128)(2,1)S(1)} collective-permute-done((bf16[104,192]{1,0:T(8,128)(2,1)S(1)}, bf16[104,192]{1,0:T(8,128)(2,1)S(1)}, u32[]{:S(2)}, u32[]{:S(2)}) %collective-permute-start.19) | collective-permute-done | bytes 39968 | tf_op jit(solution)/shard_map/early_grads/ppermute | solution.py:645
  144.5 0.9 collective-permute-done.20.right
  145.4 2.6 %collective-permute-done.21.far = bf16[104,192]{1,0:T(8,128)(2,1)S(1)} collective-permute-done((bf16[104,192]{1,0:T(8,128)(2,1)S(1)}, bf16[104,192]{1,0:T(8,128)(2,1)S(1)}, u32[]{:S(2)}, u32[]{:S(2)}) %collective-permute-start.21) | collective-permute-done | bytes 39968 | tf_op jit(solution)/shard_map/early_grads/ppermute | solution.py:645
  148.0 0.6 copy-done.12
  148.6 1.6 early_grads.3
  150.2 0.9 broadcast_in_dim.22
  151.2 20.0 %all_to_all.31.pieces = bf16[16,32,768]{2,1,0:T(8,128)(2,1)} all-to-all(bf16[16,32,768]{2,1,0:T(8,128)(2,1)S(1)} %broadcast_in_dim.22), channel_id=1, replica_groups=mesh['ctx'=16,'fsdp'=8] {'ctx'}, dimensions={0} | all-to-all | bytes 1572864 | tf_op jit(solution)/shard_map/early_grads/all_to_all | solution.py:628
  171.2 1.5 reshape.117
  172.7 21.7 %all_to_all.32.parts = bf16[16,54,768]{2,1,0:T(8,128)(2,1)} all-to-all(bf16[16,54,768]{2,1,0:T(8,128)(2,1)S(1)} %reshape.117), channel_id=1, replica_groups=mesh['ctx'=16,'fsdp'=8] {'ctx'}, dimensions={0} | all-to-all | bytes 2654208 | tf_op jit(solution)/shard_map/sum_over_ctx/all_to_all | solution.py:628
  194.5 2.7 %sum_over_ctx.3 = bf16[16,54,768]{2,1,0:T(8,128)(2,1)} custom-call(bf16[16,54,768]{2,1,0:T(8,128)(2,1)} %all_to_all.32.parts), custom_call_target="tpu_custom_call" | custom-call | flops 1000000 | bytes 8388608 | tf_op jit(solution)/shard_map/sum_over_ctx/pallas_call | solution.py:604
  197.1 3.7 %all-to-all-start.5 = ((bf16[16,54,768]{2,1,0:T(8,128)(2,1)}), bf16[16,54,768]{2,1,0:T(8,128)(2,1)S(1)}, u32[]{:S(2)}, u32[]{:S(2)}) async-start(bf16[16,54,768]{2,1,0:T(8,128)(2,1)} %sum_over_ctx.3), calls=%async_computation.6 | async-start | bytes 2752512 | tf_op jit(solution)/shard_map/sum_over_ctx/all_to_all | solution.py:628
  200.9 4.6 %token_gradient.1 = f32[128,768]{1,0:T(8,128)} custom-call(bf16[768,2304]{1,0:T(8,128)(2,1)} %all-gather.4.cloned.1.call-done.weight, bf16[128,768]{1,0:T(8,128)(2,1)} %bitcast.78, bf16[16,64,384]{2,1,0:T(8,128)(2,1)} %copy-done.1, f32[1,768]{1,0:T(1,128)} %reshape.109.refs_12_.gain, f32[128,768]{1,0:T(8,128)} %get-tuple-element.71.grad_residual), custom_call_target="tpu_custom_call" | custom-call | flops 452984832 | bytes 8388608 | tf_op jit(solution)/shard_map/token_gradient/pallas_call | solution.py:495
  205.5 2.4 %sum_over_ctx.4 = (f32[96,2304]{1,0:T(8,128)}, f32[1,96]{1,0:T(1,128)}, f32[1,96]{1,0:T(1,128)}, f32[1,192]{1,0:T(1,128)}, f32[1,96]{1,0:T(1,128)}, /*index=5*/f...) custom-call(bf16[16,32,768]{2,1,0:T(8,128)(2,1)} %all_to_all.31.pieces), custom_call_target="tpu_custom_call" | custom-call | flops 1000000 | bytes 8388608 | tf_op jit(solution)/shard_map/sum_over_ctx/pallas_call | solution.py:586
  207.8 1.3 reduce
  209.1 10.0 %all-to-all-done.5.pieces = bf16[16,54,768]{2,1,0:T(8,128)(2,1)S(1)} async-done(((bf16[16,54,768]{2,1,0:T(8,128)(2,1)}), bf16[16,54,768]{2,1,0:T(8,128)(2,1)S(1)}, u32[]{:S(2)}, u32[]{:S(2)}) %all-to-all-start.5) | async-done | bytes 1327136 | tf_op jit(solution)/shard_map/sum_over_ctx/all_to_all | solution.py:628
  219.1 1.1 copy-done
  220.3 2.9 %sum_over_ctx.5 = (f32[96,768]{1,0:T(8,128)}, f32[96,3072]{1,0:T(8,128)}, f32[384,768]{1,0:T(8,128)}) custom-call(bf16[16,54,768]{2,1,0:T(8,128)(2,1)} %copy-done), custom_call_target="tpu_custom_call" | custom-call | flops 1000000 | bytes 8388608 | tf_op jit(solution)/shard_map/sum_over_ctx/pallas_call | solution.py:618
  (106 shorter events, 4.8 us)
Async XLA Ops:
  7.2 75.2 %all-gather.6.cloned.1.call-start = ((), (), s32[]{:S(2)}) async-start(), calls=%async_computation.9 | async-start | bytes 11943936 | tf_op jit(solution)/shard_map/gather_weights/all_gather | solution.py:718
  9.7 1.3 copy-start.13
  9.7 1.3 copy-start.14
  9.7 1.3 copy-start.15
  9.7 1.3 copy-start.16
  9.7 1.3 copy-start.17
  9.7 1.3 copy-start.18
  9.7 1.3 copy-start.19
  9.8 1.3 copy-start.20
  11.6 12.8 %collective-permute-start.14 = (bf16[112,192]{0,1:T(8,128)(2,1)S(1)}, bf16[112,192]{0,1:T(8,128)(2,1)S(1)}, u32[]{:S(2)}, u32[]{:S(2)}) collective-permute-start(bf16[112,192]{0,1:T(8,128)(2,1)S(1)} %maximum_maximum_fusion), channel_id=1, source_target_pairs={{0,6},{1,7},{2,0},{3,1},{4,2},{5,3},{6,4},{7,5},{8,14},{9,15},{10,... | collective-permute-start | bytes 129032 | tf_op jit(solution)/shard_map/gather_small/ppermute | solution.py:645
  14.8 11.8 %collective-permute-start.15 = (bf16[112,192]{0,1:T(8,128)(2,1)S(1)}, bf16[112,192]{0,1:T(8,128)(2,1)S(1)}, u32[]{:S(2)}, u32[]{:S(2)}) collective-permute-start(bf16[112,192]{0,1:T(8,128)(2,1)S(1)} %maximum_maximum_fusion), channel_id=1, source_target_pairs={{0,4},{1,5},{2,6},{3,7},{4,0},{5,1},{6,2},{7,3},{8,12},{9,13},{10,... | collective-permute-start | bytes 129032 | tf_op jit(solution)/shard_map/gather_small/ppermute | solution.py:645
  15.4 12.7 %collective-permute-start.16 = (bf16[112,192]{0,1:T(8,128)(2,1)S(1)}, bf16[112,192]{0,1:T(8,128)(2,1)S(1)}, u32[]{:S(2)}, u32[]{:S(2)}) collective-permute-start(bf16[112,192]{0,1:T(8,128)(2,1)S(1)} %maximum_maximum_fusion), channel_id=1, source_target_pairs={{0,2},{1,3},{2,4},{3,5},{4,6},{5,7},{6,0},{7,1},{8,10},{9,11},{10,... | collective-permute-start | bytes 129032 | tf_op jit(solution)/shard_map/gather_small/ppermute | solution.py:645
  19.2 10.7 %collective-permute-start.9 = (bf16[64,768]{1,0:T(8,128)(2,1)S(1)}, bf16[64,768]{1,0:T(8,128)(2,1)S(1)}, u32[]{:S(2)}, u32[]{:S(2)}) collective-permute-start(bf16[64,768]{1,0:T(8,128)(2,1)S(1)} %get-tuple-element.101), channel_id=1, source_target_pairs={{0,64},{1,65},{2,66},{3,67},{4,68},{5,69},{6,70},{7,71},{8,72},{9,... | collective-permute-start | bytes 294920 | tf_op jit(solution)/shard_map/gather_tokens/ppermute | solution.py:645
  23.1 8.7 %collective-permute-start.7 = (bf16[64,768]{1,0:T(8,128)(2,1)S(1)}, bf16[64,768]{1,0:T(8,128)(2,1)S(1)}, u32[]{:S(2)}, u32[]{:S(2)}) collective-permute-start(bf16[64,768]{1,0:T(8,128)(2,1)S(1)} %get-tuple-element.101), channel_id=1, source_target_pairs={{0,32},{1,33},{2,34},{3,35},{4,36},{5,37},{6,38},{7,39},{8,40},{9,... | collective-permute-start | bytes 294920 | tf_op jit(solution)/shard_map/gather_tokens/ppermute | solution.py:645
  24.4 7.4 %collective-permute-start.8 = (bf16[64,768]{1,0:T(8,128)(2,1)S(1)}, bf16[64,768]{1,0:T(8,128)(2,1)S(1)}, u32[]{:S(2)}, u32[]{:S(2)}) collective-permute-start(bf16[64,768]{1,0:T(8,128)(2,1)S(1)} %get-tuple-element.101), channel_id=1, source_target_pairs={{0,96},{1,97},{2,98},{3,99},{4,100},{5,101},{6,102},{7,103},{8,104... | collective-permute-start | bytes 294920 | tf_op jit(solution)/shard_map/gather_tokens/ppermute | solution.py:645
  26.6 6.9 %collective-permute-start = (bf16[64,768]{1,0:T(8,128)(2,1)S(1)}, bf16[64,768]{1,0:T(8,128)(2,1)S(1)}, u32[]{:S(2)}, u32[]{:S(2)}) collective-permute-start(bf16[64,768]{1,0:T(8,128)(2,1)S(1)} %get-tuple-element.102), channel_id=1, source_target_pairs={{0,8},{1,9},{2,10},{3,11},{4,12},{5,13},{6,14},{7,15},{8,16},{9,17... | collective-permute-start | bytes 294920 | tf_op jit(solution)/shard_map/gather_tokens/ppermute | solution.py:645
  28.1 7.1 %collective-permute-start.1 = (bf16[64,768]{1,0:T(8,128)(2,1)S(1)}, bf16[64,768]{1,0:T(8,128)(2,1)S(1)}, u32[]{:S(2)}, u32[]{:S(2)}) collective-permute-start(bf16[64,768]{1,0:T(8,128)(2,1)S(1)} %get-tuple-element.102), channel_id=1, source_target_pairs={{0,24},{1,25},{2,26},{3,27},{4,28},{5,29},{6,30},{7,31},{8,0},{9,1... | collective-permute-start | bytes 294920 | tf_op jit(solution)/shard_map/gather_tokens/ppermute | solution.py:645
  29.9 6.7 %collective-permute-start.2 = (bf16[64,768]{1,0:T(8,128)(2,1)S(1)}, bf16[64,768]{1,0:T(8,128)(2,1)S(1)}, u32[]{:S(2)}, u32[]{:S(2)}) collective-permute-start(bf16[64,768]{1,0:T(8,128)(2,1)S(1)} %get-tuple-element.102), channel_id=1, source_target_pairs={{0,16},{1,17},{2,18},{3,19},{4,20},{5,21},{6,22},{7,23},{8,24},{9,... | collective-permute-start | bytes 294920 | tf_op jit(solution)/shard_map/gather_tokens/ppermute | solution.py:645
  31.8 8.2 %collective-permute-start.17 = (bf16[4,112,192]{1,2,0:T(8,128)(2,1)S(1)}, bf16[4,112,192]{1,2,0:T(8,128)(2,1)S(1)}, u32[]{:S(2)}, u32[]{:S(2)}) collective-permute-start(bf16[4,112,192]{1,2,0:T(8,128)(2,1)S(1)} %pad_maximum_fusion.2), channel_id=1, source_target_pairs={{0,1},{1,0},{2,3},{3,2},{4,5},{5,4},{6,7},{7,6},{8,9},{9,8},{10,11... | collective-permute-start | bytes 516104 | tf_op jit(solution)/shard_map/gather_small/ppermute | solution.py:645
  31.9 8.6 %copy-start.2 = (bf16[4,64,768]{2,1,0:T(8,128)(2,1)}, bf16[4,64,768]{2,1,0:T(8,128)(2,1)S(1)}, u32[]{:S(2)}) copy-start(bf16[4,64,768]{2,1,0:T(8,128)(2,1)S(1)} %pad_maximum_fusion.1.refs_5_) | copy-start | bytes 1179652
  31.9 13.0 %collective-permute-start.10 = (bf16[4,64,768]{2,1,0:T(8,128)(2,1)S(1)}, bf16[4,64,768]{2,1,0:T(8,128)(2,1)S(1)}, u32[]{:S(2)}, u32[]{:S(2)}) collective-permute-start(bf16[4,64,768]{2,1,0:T(8,128)(2,1)S(1)} %pad_maximum_fusion.1.refs_5_), channel_id=1, source_target_pairs={{0,8},{1,9},{2,10},{3,11},{4,12},{5,13},{6,14},{7,15},{8,16},{9,17... | collective-permute-start | bytes 1179656 | tf_op jit(solution)/shard_map/gather_tokens/ppermute | solution.py:645
  33.5 11.5 %collective-permute-start.11 = (bf16[4,64,768]{2,1,0:T(8,128)(2,1)S(1)}, bf16[4,64,768]{2,1,0:T(8,128)(2,1)S(1)}, u32[]{:S(2)}, u32[]{:S(2)}) collective-permute-start(bf16[4,64,768]{2,1,0:T(8,128)(2,1)S(1)} %pad_maximum_fusion.1.refs_5_), channel_id=1, source_target_pairs={{0,24},{1,25},{2,26},{3,27},{4,28},{5,29},{6,30},{7,31},{8,0},{9,1... | collective-permute-start | bytes 1179656 | tf_op jit(solution)/shard_map/gather_tokens/ppermute | solution.py:645
  36.7 4.0 %copy-start.3 = (bf16[4,64,768]{2,1,0:T(8,128)(2,1)}, bf16[4,64,768]{2,1,0:T(8,128)(2,1)S(1)}, u32[]{:S(2)}) copy-start(bf16[4,64,768]{2,1,0:T(8,128)(2,1)S(1)} %pad_maximum_fusion.refs_0_) | copy-start | bytes 1179652
  36.7 11.6 %collective-permute-start.3 = (bf16[4,64,768]{2,1,0:T(8,128)(2,1)S(1)}, bf16[4,64,768]{2,1,0:T(8,128)(2,1)S(1)}, u32[]{:S(2)}, u32[]{:S(2)}) collective-permute-start(bf16[4,64,768]{2,1,0:T(8,128)(2,1)S(1)} %pad_maximum_fusion.refs_0_), channel_id=1, source_target_pairs={{0,32},{1,33},{2,34},{3,35},{4,36},{5,37},{6,38},{7,39},{8,40},{9,... | collective-permute-start | bytes 1179656 | tf_op jit(solution)/shard_map/gather_tokens/ppermute | solution.py:645
  36.8 11.6 %collective-permute-start.4 = (bf16[4,64,768]{2,1,0:T(8,128)(2,1)S(1)}, bf16[4,64,768]{2,1,0:T(8,128)(2,1)S(1)}, u32[]{:S(2)}, u32[]{:S(2)}) collective-permute-start(bf16[4,64,768]{2,1,0:T(8,128)(2,1)S(1)} %pad_maximum_fusion.refs_0_), channel_id=1, source_target_pairs={{0,96},{1,97},{2,98},{3,99},{4,100},{5,101},{6,102},{7,103},{8,104... | collective-permute-start | bytes 1179656 | tf_op jit(solution)/shard_map/gather_tokens/ppermute | solution.py:645
  44.9 10.9 %copy-start.6 = (bf16[4,64,768]{2,1,0:T(8,128)(2,1)}, bf16[4,64,768]{2,1,0:T(8,128)(2,1)S(1)}, u32[]{:S(2)}) copy-start(bf16[4,64,768]{2,1,0:T(8,128)(2,1)S(1)} %collective-permute-done.10.refs_6_) | copy-start | bytes 1179652
  44.9 8.0 %collective-permute-start.12 = (bf16[2,64,768]{2,1,0:T(8,128)(2,1)S(1)}, bf16[2,64,768]{2,1,0:T(8,128)(2,1)S(1)}, u32[]{:S(2)}, u32[]{:S(2)}) collective-permute-start(bf16[2,64,768]{2,1,0:T(8,128)(2,1)S(1)} %slice.78), channel_id=1, source_target_pairs={{0,8},{1,9},{2,10},{3,11},{4,12},{5,13},{6,14},{7,15},{8,16},{9,17... | collective-permute-start | bytes 589832 | tf_op jit(solution)/shard_map/gather_tokens/ppermute | solution.py:645
  45.0 10.8 %copy-start.7 = (bf16[4,64,768]{2,1,0:T(8,128)(2,1)}, bf16[4,64,768]{2,1,0:T(8,128)(2,1)S(1)}, u32[]{:S(2)}) copy-start(bf16[4,64,768]{2,1,0:T(8,128)(2,1)S(1)} %collective-permute-done.11.refs_7_) | copy-start | bytes 1179652
  45.0 7.9 %collective-permute-start.13 = (bf16[2,64,768]{2,1,0:T(8,128)(2,1)S(1)}, bf16[2,64,768]{2,1,0:T(8,128)(2,1)S(1)}, u32[]{:S(2)}, u32[]{:S(2)}) collective-permute-start(bf16[2,64,768]{2,1,0:T(8,128)(2,1)S(1)} %slice.79), channel_id=1, source_target_pairs={{0,24},{1,25},{2,26},{3,27},{4,28},{5,29},{6,30},{7,31},{8,0},{9,1... | collective-permute-start | bytes 589832 | tf_op jit(solution)/shard_map/gather_tokens/ppermute | solution.py:645
  48.3 7.5 %copy-start.8 = (bf16[4,64,768]{2,1,0:T(8,128)(2,1)}, bf16[4,64,768]{2,1,0:T(8,128)(2,1)S(1)}, u32[]{:S(2)}) copy-start(bf16[4,64,768]{2,1,0:T(8,128)(2,1)S(1)} %collective-permute-done.3.refs_1_) | copy-start | bytes 1179652
  48.3 7.5 %collective-permute-start.5 = (bf16[2,64,768]{2,1,0:T(8,128)(2,1)S(1)}, bf16[2,64,768]{2,1,0:T(8,128)(2,1)S(1)}, u32[]{:S(2)}, u32[]{:S(2)}) collective-permute-start(bf16[2,64,768]{2,1,0:T(8,128)(2,1)S(1)} %slice.75), channel_id=1, source_target_pairs={{0,32},{1,33},{2,34},{3,35},{4,36},{5,37},{6,38},{7,39},{8,40},{9,... | collective-permute-start | bytes 589832 | tf_op jit(solution)/shard_map/gather_tokens/ppermute | solution.py:645
  48.4 7.4 %copy-start.9 = (bf16[4,64,768]{2,1,0:T(8,128)(2,1)}, bf16[4,64,768]{2,1,0:T(8,128)(2,1)S(1)}, u32[]{:S(2)}) copy-start(bf16[4,64,768]{2,1,0:T(8,128)(2,1)S(1)} %collective-permute-done.4.refs_2_) | copy-start | bytes 1179652
  48.5 7.3 %collective-permute-start.6 = (bf16[2,64,768]{2,1,0:T(8,128)(2,1)S(1)}, bf16[2,64,768]{2,1,0:T(8,128)(2,1)S(1)}, u32[]{:S(2)}, u32[]{:S(2)}) collective-permute-start(bf16[2,64,768]{2,1,0:T(8,128)(2,1)S(1)} %slice.76), channel_id=1, source_target_pairs={{0,96},{1,97},{2,98},{3,99},{4,100},{5,101},{6,102},{7,103},{8,104... | collective-permute-start | bytes 589832 | tf_op jit(solution)/shard_map/gather_tokens/ppermute | solution.py:645
  52.9 2.9 %copy-start.21 = (bf16[2,64,768]{2,1,0:T(8,128)(2,1)}, bf16[2,64,768]{2,1,0:T(8,128)(2,1)S(1)}, u32[]{:S(2)}) copy-start(bf16[2,64,768]{2,1,0:T(8,128)(2,1)S(1)} %collective-permute-done.12.refs_8_) | copy-start | bytes 589828
  53.0 2.9 %copy-start.22 = (bf16[2,64,768]{2,1,0:T(8,128)(2,1)}, bf16[2,64,768]{2,1,0:T(8,128)(2,1)S(1)}, u32[]{:S(2)}) copy-start(bf16[2,64,768]{2,1,0:T(8,128)(2,1)S(1)} %collective-permute-done.13.refs_9_) | copy-start | bytes 589828
  55.8 0.7 copy-start.23
  55.8 0.7 copy-start.24
  69.1 13.3 %all-to-all-start = ((bf16[16,64,128]{2,1,0:T(8,128)(2,1)}), bf16[16,64,128]{2,1,0:T(8,128)(2,1)S(1)}, u32[]{:S(2)}, u32[]{:S(2)}) async-start(bf16[16,64,128]{2,1,0:T(8,128)(2,1)} %get-tuple-element.52), calls=%async_computation | async-start | bytes 524288 | tf_op jit(solution)/shard_map/attention/all_to_all | solution.py:628
  73.7 97.5 %reduce-scatter.2.cloned.1.call-start = ((), (), s32[]{:S(2)}) async-start(), calls=%async_computation.8 | async-start | bytes 11943936 | tf_op jit(solution)/shard_map/feed_forward/reduce_scatter | solution.py:758
  82.3 0.7 copy-start.4
  99.4 1.0 copy-start.5
  125.9 24.3 %all-to-all-start.2 = ((bf16[16,64,384]{2,1,0:T(8,128)(2,1)}), bf16[16,64,384]{2,1,0:T(8,128)(2,1)S(1)}, u32[]{:S(2)}, u32[]{:S(2)}) async-start(bf16[16,64,384]{2,1,0:T(8,128)(2,1)} %get-tuple-element.67), calls=%async_computation.2 | async-start | bytes 1572864 | tf_op jit(solution)/shard_map/attention_back/all_to_all | solution.py:628
  129.5 71.3 %all-gather.4.cloned.1.call-start = ((), (), s32[]{:S(2)}) async-start(), calls=%async_computation.7 | async-start | bytes 3981312 | tf_op jit(solution)/shard_map/token_gradient/all_gather | solution.py:791
  135.1 1.5 collective-permute-start.18
  138.4 6.1 %collective-permute-start.19 = (bf16[104,192]{1,0:T(8,128)(2,1)S(1)}, bf16[104,192]{1,0:T(8,128)(2,1)S(1)}, u32[]{:S(2)}, u32[]{:S(2)}) collective-permute-start(bf16[104,192]{1,0:T(8,128)(2,1)S(1)} %get-tuple-element.97), channel_id=1, source_target_pairs={{0,2},{1,3},{2,4},{3,5},{4,6},{5,7},{6,0},{7,1},{8,10},{9,11},{10,... | collective-permute-start | bytes 119816 | tf_op jit(solution)/shard_map/early_grads/ppermute | solution.py:645
  140.1 5.3 %collective-permute-start.20 = (bf16[104,192]{1,0:T(8,128)(2,1)S(1)}, bf16[104,192]{1,0:T(8,128)(2,1)S(1)}, u32[]{:S(2)}, u32[]{:S(2)}) collective-permute-start(bf16[104,192]{1,0:T(8,128)(2,1)S(1)} %get-tuple-element.96), channel_id=1, source_target_pairs={{0,6},{1,7},{2,0},{3,1},{4,2},{5,3},{6,4},{7,5},{8,14},{9,15},{10,... | collective-permute-start | bytes 119816 | tf_op jit(solution)/shard_map/early_grads/ppermute | solution.py:645
  141.7 6.3 %collective-permute-start.21 = (bf16[104,192]{1,0:T(8,128)(2,1)S(1)}, bf16[104,192]{1,0:T(8,128)(2,1)S(1)}, u32[]{:S(2)}, u32[]{:S(2)}) collective-permute-start(bf16[104,192]{1,0:T(8,128)(2,1)S(1)} %get-tuple-element.95), channel_id=1, source_target_pairs={{0,4},{1,5},{2,6},{3,7},{4,0},{5,1},{6,2},{7,3},{8,12},{9,13},{10,... | collective-permute-start | bytes 119816 | tf_op jit(solution)/shard_map/early_grads/ppermute | solution.py:645
  144.5 3.4 %copy-start.10 = (bf16[104,192]{1,0:T(8,128)(2,1)}, bf16[104,192]{1,0:T(8,128)(2,1)S(1)}, u32[]{:S(2)}) copy-start(bf16[104,192]{1,0:T(8,128)(2,1)S(1)} %collective-permute-done.19.left) | copy-start | bytes 119812
  145.4 2.6 %copy-start.11 = (bf16[104,192]{1,0:T(8,128)(2,1)}, bf16[104,192]{1,0:T(8,128)(2,1)S(1)}, u32[]{:S(2)}) copy-start(bf16[104,192]{1,0:T(8,128)(2,1)S(1)} %collective-permute-done.20.right) | copy-start | bytes 119812
  148.0 0.6 copy-start.12
  150.2 21.0 %copy-start.1 = (bf16[16,64,384]{2,1,0:T(8,128)(2,1)}, bf16[16,64,384]{2,1,0:T(8,128)(2,1)S(1)}, u32[]{:S(2)}) copy-start(bf16[16,64,384]{2,1,0:T(8,128)(2,1)S(1)} %all-to-all-done.2.heads_grad) | copy-start | bytes 2359300
  197.1 22.0 %all-to-all-start.5 = ((bf16[16,54,768]{2,1,0:T(8,128)(2,1)}), bf16[16,54,768]{2,1,0:T(8,128)(2,1)S(1)}, u32[]{:S(2)}, u32[]{:S(2)}) async-start(bf16[16,54,768]{2,1,0:T(8,128)(2,1)} %sum_over_ctx.3), calls=%async_computation.6 | async-start | bytes 2752512 | tf_op jit(solution)/shard_map/sum_over_ctx/all_to_all | solution.py:628
  219.1 1.1 copy-start
Sparse Core Ops, SparseCore 0:
  9.9 61.5 all-gather.5
  99.6 61.9 reduce-scatter.1
  163.4 29.2 all-gather.3

commit v4 on v3

--- a/solution.py
+++ b/solution.py
@@ -399,13 +399,20 @@
 def feed_forward(pack, tokens, heads_out, cotangent, out_bias, gain, shift, up_bias, down_bias):
     def kernel(
         source, tokens, heads_out, cotangent, out_bias, gain, shift, up_bias, down_bias,
-        mixed, mix_grad, grad_heads, grad_residual, vector_sums, up_sums,
-        pack, sems,
+        mixed, grads_out, grad_heads, grad_residual, vector_sums, up_sums,
+        pack, sems, mix_grad, out_sems,
     ):
         order = [0] + [index for j in range(4) for index in (1 + j, 5 + j)]
         copies = {index: pack_piece(source, pack, sems, index) for index in order}
         for index in order:
             copies[index].start()
+
+        def send(index):
+            copy = pack_piece(mix_grad, grads_out, out_sems, index)
+            copy.start()
+            return copy
+
+        sent = []
         inputs = tokens[...].astype(F32)
         result_grad = cotangent[...]
         attended_low = unpack_heads(heads_out, 0)
@@ -430,11 +437,13 @@
             mix_grad[2 * j : 2 * j + 2, DOWN_AT:, :] = (
                 dot(acted.T, result_grad).astype(BF).reshape(2, 384, WIDTH)
             )
+            sent.append(send(5 + j))
             total = total + dot(acted, w_down)
             pre = (upstream * slope).astype(BF)
             mix_grad[:, UP_AT + 96 * j : UP_AT + 96 * (j + 1), :] = (
                 dot(low_t, pre).astype(BF).reshape(FSDP, 96, WIDTH)
             )
+            sent.append(send(1 + j))
             up_sums[:, lanes] = jnp.sum(pre.astype(F32), axis=0, keepdims=True)
             grad_normed = grad_normed + dot_nt(pre, w_up)
         mixed[...] = total.astype(BF)
@@ -452,10 +461,13 @@
         mix_grad[:, OUT_AT:UP_AT, :] = (
             dot(attended_low.T, branch).astype(BF).reshape(FSDP, 96, WIDTH)
         )
+        sent.append(send(0))
         vector_sums[0:1, :] = jnp.sum(branch.astype(F32), axis=0, keepdims=True)
         vector_sums[1:2, :] = jnp.sum(grad_normed * hat, axis=0, keepdims=True)
         vector_sums[2:3, :] = jnp.sum(grad_normed, axis=0, keepdims=True)
         vector_sums[3:4, :] = jnp.sum(result_grad.astype(F32), axis=0, keepdims=True)
+        for copy in sent:
+            copy.wait()
 
     shape = jax.ShapeDtypeStruct
     outs = [
@@ -471,8 +483,13 @@
         out_shape=outs,
         in_specs=[pl.BlockSpec(memory_space=pl.ANY)]
         + [pl.BlockSpec(memory_space=pltpu.VMEM)] * 8,
-        out_specs=[pl.BlockSpec(memory_space=pltpu.VMEM)] * len(outs),
+        out_specs=[
+            pl.BlockSpec(memory_space=pl.ANY if index == 1 else pltpu.VMEM)
+            for index in range(len(outs))
+        ],
         scratch_shapes=[
+            pltpu.VMEM((FSDP, PACK_ROWS, WIDTH), BF),
+            pltpu.SemaphoreType.DMA((9,)),
             pltpu.VMEM((FSDP, PACK_ROWS, WIDTH), BF),
             pltpu.SemaphoreType.DMA((9,)),
         ],
@@ -712,8 +729,12 @@
     )
 
     with jax.named_scope("gather_tokens"):
-        blocks = gather_rows(normalised_rows(my_tokens))
+        hat = normalised_rows(my_tokens)
+        blocks = gather_rows(hat)
     with jax.named_scope("gather_weights"):
+        out_weight, up_weight, down_weight, _ = lax.optimization_barrier(
+            (out_weight, up_weight, down_weight, hat)
+        )
         pack = packed_weights(out_weight, up_weight, down_weight)
         pack = lax.all_gather(pack, "fsdp", axis=0, tiled=False)
     with jax.named_scope("gather_small"):

time: 231 us -> 228 us (0.987)
    unnamed x56 -> x58, local copies, waits for them, and re-layouts: 5.28 us -> 5.31 us
  transfers between devices with their start and end apart: 28 -> 28, of which waited for: 11 -> 11; matrix products, arithmetic and copies ran while one was open for 7% -> 7% of each run, Pallas kernels for 19% -> 18%
where the time goes in v4:
time: 228 us; the launch traced here: 227 us
  Pallas kernels  63.2 us (28%)
  blocking collectives  53.7 us (24%)
  starting transfers between devices  45.8 us (20%)
  waiting for transfers between devices  29.4 us (13%)
  local copies, waits for them, and re-layouts  15.5 us (7%)
  between operations  14.4 us (6%)
  other arithmetic  4.68 us (2%)
    all_to_all x3, blocking collectives, swap(): return lax.all_to_all(slots, axes, 0, 0, tiled=True)  53.7 us
    ppermute x22, starting transfers between devices, shift_by(): return lax.ppermute(value, ('ctx', 'fsdp'), pairs)  33.6 us
    all_to_all x3, waiting for transfers between devices, swap(): return lax.all_to_all(slots, axes, 0, 0, tiled=True)  15.1 us
    pallas_call x1, Pallas kernels, feed_forward(): pl.pallas_call(kernel, out_shape=outs, in_specs=[pl.BlockSpec(memory_spac...  14.2 us
    ppermute x22, waiting for transfers between devices, shift_by(): return lax.ppermute(value, ('ctx', 'fsdp'), pairs)  14.2 us
    pallas_call x1, Pallas kernels, head_backward(): vmem_call(kernel, [shape((CTX, HALF, 6 * DEPTH), BF), shape((SEQ, 3 * DEP...  13.6 us
    pallas_call x1, Pallas kernels, head_forward(): vmem_call(kernel, [shape((CTX, HALF, 2 * DEPTH), BF), shape((SEQ, WIDTH),...  12.5 us
    all_to_all x3, starting transfers between devices, swap(): return lax.all_to_all(slots, axes, 0, 0, tiled=True)  11.9 us
  transfers between devices with their start and end apart: 28, of which 11 were waited for; matrix products, arithmetic and copies ran while one was open for 7% of the time, Pallas kernels for 18%

profile of v4, /device:TPU:0, one launch (start us, length us, event | category | flops | bytes accessed | tf_op | source)
XLA Modules:
  0.0 226.7 jit_solution(518377991489102080)
XLA Ops:
  7.2 1.8 gather_tokens.1
  9.1 2.5 %gather_weights.1 = bf16[864,768]{1,0:T(8,128)(2,1)} custom-call(bf16[96,768]{1,0:T(8,128)(2,1)} %out_weight, bf16[96,3072]{1,0:T(8,128)(2,1)} %up_weight, bf16[384,768]{1,0:T(8,128)(2,1)} %down_weight), custom_call_target="tpu_custom_call" | custom-call | flops 1000000 | bytes 8388608 | tf_op jit(solution)/shard_map/gather_weights/pallas_call | solution.py:117
  11.7 0.9 constant_dynamic-slice_fusion.4
  13.5 3.2 %collective-permute-start.14 = (bf16[112,192]{0,1:T(8,128)(2,1)S(1)}, bf16[112,192]{0,1:T(8,128)(2,1)S(1)}, u32[]{:S(2)}, u32[]{:S(2)}) collective-permute-start(bf16[112,192]{0,1:T(8,128)(2,1)S(1)} %maximum_maximum_fusion), channel_id=1, source_target_pairs={{0,6},{1,7},{2,0},{3,1},{4,2},{5,3},{6,4},{7,5},{8,14},{9,15},{10,... | collective-permute-start | bytes 129032 | tf_op jit(solution)/shard_map/gather_small/ppermute | solution.py:662
  16.7 0.6 collective-permute-start.15
  17.3 1.0 collective-permute-start.16
  18.3 4.0 %collective-permute-start.9 = (bf16[64,768]{1,0:T(8,128)(2,1)S(1)}, bf16[64,768]{1,0:T(8,128)(2,1)S(1)}, u32[]{:S(2)}, u32[]{:S(2)}) collective-permute-start(bf16[64,768]{1,0:T(8,128)(2,1)S(1)} %get-tuple-element.107), channel_id=1, source_target_pairs={{0,64},{1,65},{2,66},{3,67},{4,68},{5,69},{6,70},{7,71},{8,72},{9,... | collective-permute-start | bytes 294920 | tf_op jit(solution)/shard_map/gather_tokens/ppermute | solution.py:662
  22.3 1.0 collective-permute-start.7
  23.5 2.2 collective-permute-start.8
  25.8 1.5 collective-permute-start
  27.2 1.7 collective-permute-start.1
  29.1 1.9 collective-permute-start.2
  31.0 0.7 collective-permute-start.10
  31.7 0.9 collective-permute-done
  32.6 1.7 collective-permute-start.11
  34.3 1.5 collective-permute-done.2
  36.0 3.2 %collective-permute-start.4 = (bf16[4,64,768]{2,1,0:T(8,128)(2,1)S(1)}, bf16[4,64,768]{2,1,0:T(8,128)(2,1)S(1)}, u32[]{:S(2)}, u32[]{:S(2)}) collective-permute-start(bf16[4,64,768]{2,1,0:T(8,128)(2,1)S(1)} %pad_maximum_fusion.refs_0_), channel_id=1, source_target_pairs={{0,96},{1,97},{2,98},{3,99},{4,100},{5,101},{6,102},{7,103},{8,104... | collective-permute-start | bytes 1179656 | tf_op jit(solution)/shard_map/gather_tokens/ppermute | solution.py:662
  40.2 0.7 reshape.109.refs_12_.gain
  40.9 0.7 reshape.110.refs_13_.shift
  41.6 1.0 copy.53
  42.6 1.4 collective-permute-done.10.refs_6_
  44.2 3.3 %collective-permute-start.13 = (bf16[2,64,768]{2,1,0:T(8,128)(2,1)S(1)}, bf16[2,64,768]{2,1,0:T(8,128)(2,1)S(1)}, u32[]{:S(2)}, u32[]{:S(2)}) collective-permute-start(bf16[2,64,768]{2,1,0:T(8,128)(2,1)S(1)} %slice.79), channel_id=1, source_target_pairs={{0,24},{1,25},{2,26},{3,27},{4,28},{5,29},{6,30},{7,31},{8,0},{9,1... | collective-permute-start | bytes 589832 | tf_op jit(solution)/shard_map/gather_tokens/ppermute | solution.py:662
  47.6 3.5 %collective-permute-start.6 = (bf16[2,64,768]{2,1,0:T(8,128)(2,1)S(1)}, bf16[2,64,768]{2,1,0:T(8,128)(2,1)S(1)}, u32[]{:S(2)}, u32[]{:S(2)}) collective-permute-start(bf16[2,64,768]{2,1,0:T(8,128)(2,1)S(1)} %slice.76), channel_id=1, source_target_pairs={{0,96},{1,97},{2,98},{3,99},{4,100},{5,101},{6,102},{7,103},{8,104... | collective-permute-start | bytes 589832 | tf_op jit(solution)/shard_map/gather_tokens/ppermute | solution.py:662
  52.1 2.9 %collective-permute-done.5.refs_3_ = bf16[2,64,768]{2,1,0:T(8,128)(2,1)S(1)} collective-permute-done((bf16[2,64,768]{2,1,0:T(8,128)(2,1)S(1)}, bf16[2,64,768]{2,1,0:T(8,128)(2,1)S(1)}, u32[]{:S(2)}, u32[]{:S(2)}) %collective-permute-start.5) | collective-permute-done | bytes 196640 | tf_op jit(solution)/shard_map/gather_tokens/ppermute | solution.py:662
  55.0 0.6 copy-done.24
  55.7 12.5 %attention.1 = (bf16[16,64,128]{2,1,0:T(8,128)(2,1)}, bf16[2048,768]{1,0:T(8,128)(2,1)}, bf16[2048,64]{1,0:T(8,128)(2,1)}, bf16[2048,64]{1,0:T(8,128)(2,1)}, bf1...) custom-call(s32[16]{0:T(128)} %order.3, ...), custom_call_target="tpu_custom_call" | custom-call | flops 2000000000 | bytes 8388608 | tf_op jit(solution)/shard_map/attention/pallas_call | solution.py:237
  68.2 4.5 %all-to-all-start = ((bf16[16,64,128]{2,1,0:T(8,128)(2,1)}), bf16[16,64,128]{2,1,0:T(8,128)(2,1)S(1)}, u32[]{:S(2)}, u32[]{:S(2)}) async-start(bf16[16,64,128]{2,1,0:T(8,128)(2,1)} %get-tuple-element.58), calls=%async_computation | async-start | bytes 524288 | tf_op jit(solution)/shard_map/attention/all_to_all | solution.py:645
  73.0 0.7 reshape.111.out_bias
  73.7 0.7 reshape.112.gain
  74.3 0.7 reshape.113.shift
  75.0 0.7 reshape.115.down_bias
  75.7 0.6 copy.64
  76.3 5.1 %all-to-all-done.heads_out = bf16[16,64,128]{2,1,0:T(8,128)(2,1)S(1)} async-done(((bf16[16,64,128]{2,1,0:T(8,128)(2,1)}), bf16[16,64,128]{2,1,0:T(8,128)(2,1)S(1)}, u32[]{:S(2)}, u32[]{:S(2)}) %all-to-all-start) | async-done | bytes 262176 | tf_op jit(solution)/shard_map/attention/all_to_all | solution.py:645
  81.4 0.7 copy-done.5
  82.1 14.2 %feed_forward.1 = (bf16[128,768]{1,0:T(8,128)(2,1)}, bf16[8,864,768]{2,1,0:T(8,128)(2,1)}, bf16[16,64,128]{2,1,0:T(8,128)(2,1)}, f32[128,768]{1,0:T(8,128)}, f32[4,768]{1,0:T(4,128)}, /*index=5*/f32[1,3072]{1,0:T(1,128)}) custom-call(bf16[8,864,768]{2,1,0:T(8,128)(2,1)} %bitcast.94, bf16[128,768]{1,0:T(8,128)(2,1)} %bitcast.77, ...), custom_call_target="tpu_custom_call" | custom-call | flops 4000000000 | bytes 25165824 | tf_op jit(solution)/shard_map/feed_forward/pallas_call | solution.py:481
  96.4 0.9 copy-done.6
  97.3 11.9 %all_to_all.30.upstream = bf16[16,64,128]{2,1,0:T(8,128)(2,1)} all-to-all(bf16[16,64,128]{2,1,0:T(8,128)(2,1)S(1)} %copy-done.6), channel_id=1, replica_groups=mesh['ctx'=16,'fsdp'=8] {'ctx'}, dimensions={0} | all-to-all | bytes 524288 | tf_op jit(solution)/shard_map/feed_forward/all_to_all | solution.py:645
  109.3 13.6 %attention_back.1 = (bf16[16,64,384]{2,1,0:T(8,128)(2,1)}, bf16[2048,192]{1,0:T(8,128)(2,1)}, f32[1,192]{1,0:T(1,128)}) custom-call(s32[16]{0:T(128)} %order.3, bf16[16,64,128]{2,1,0:T(8,128)(2,1)} %all_to_all.30.upstream, bf16[2048,64]{1,0:T(8,128)(2,1)} %get-tuple-element.62.query, bf16[2048,64]{1,0:T(8,128)(2,1)} %get-tuple-element.63.key, ...), custom_call_target="tpu_custom_call" | custom-call | flops 4000000000 | bytes 8388608 | tf_op jit(solution)/shard_map/attention_back/pallas_call | solution.py:343
  122.8 3.6 %all-to-all-start.2 = ((bf16[16,64,384]{2,1,0:T(8,128)(2,1)}), bf16[16,64,384]{2,1,0:T(8,128)(2,1)S(1)}, u32[]{:S(2)}, u32[]{:S(2)}) async-start(bf16[16,64,384]{2,1,0:T(8,128)(2,1)} %get-tuple-element.73), calls=%async_computation.2 | async-start | bytes 1572864 | tf_op jit(solution)/shard_map/attention_back/all_to_all | solution.py:645
  126.5 4.5 %early_grads.2 = bf16[8,104,192]{2,1,0:T(8,128)(2,1)} custom-call(s32[1]{0:T(128)} %bitcast.2.where, bf16[2048,768]{1,0:T(8,128)(2,1)} %get-tuple-element.60.hats, bf16[2048,192]{1,0:T(8,128)(2,1)} %get-tuple-element.69.rows, bf16[768,192]{1,0:T(8,128)(2,1)} %bitcast.74, f32[1,768]{1,0:T(1,128)} %reshape.109.refs_12_.gain, ...), custom_call_target="tpu_custom_call" | custom-call | flops 603979776 | bytes 8388608 | tf_op jit(solution)/shard_map/early_grads/pallas_call | solution.py:556
  131.0 1.1 select_bitcast_fusion
  132.2 1.4 collective-permute-done.18
  133.6 1.1 fusion
  134.7 0.7 dynamic-slice_bitcast_fusion
  135.4 1.7 collective-permute-start.19
  137.1 1.5 collective-permute-start.20
  138.6 0.6 collective-permute-start.21
  139.2 2.2 collective-permute-done.19.left
  141.5 0.9 collective-permute-done.20.right
  142.4 2.5 %collective-permute-done.21.far = bf16[104,192]{1,0:T(8,128)(2,1)S(1)} collective-permute-done((bf16[104,192]{1,0:T(8,128)(2,1)S(1)}, bf16[104,192]{1,0:T(8,128)(2,1)S(1)}, u32[]{:S(2)}, u32[]{:S(2)}) %collective-permute-start.21) | collective-permute-done | bytes 39968 | tf_op jit(solution)/shard_map/early_grads/ppermute | solution.py:662
  144.9 0.6 copy-done.13
  145.5 1.6 early_grads.3
  147.1 0.9 broadcast_in_dim.22
  148.1 20.1 %all_to_all.31.pieces = bf16[16,32,768]{2,1,0:T(8,128)(2,1)} all-to-all(bf16[16,32,768]{2,1,0:T(8,128)(2,1)S(1)} %broadcast_in_dim.22), channel_id=1, replica_groups=mesh['ctx'=16,'fsdp'=8] {'ctx'}, dimensions={0} | all-to-all | bytes 1572864 | tf_op jit(solution)/shard_map/early_grads/all_to_all | solution.py:645
  168.2 1.5 reshape.117
  169.7 21.7 %all_to_all.32.parts = bf16[16,54,768]{2,1,0:T(8,128)(2,1)} all-to-all(bf16[16,54,768]{2,1,0:T(8,128)(2,1)S(1)} %reshape.117), channel_id=1, replica_groups=mesh['ctx'=16,'fsdp'=8] {'ctx'}, dimensions={0} | all-to-all | bytes 2654208 | tf_op jit(solution)/shard_map/sum_over_ctx/all_to_all | solution.py:645
  191.4 2.6 %sum_over_ctx.3 = bf16[16,54,768]{2,1,0:T(8,128)(2,1)} custom-call(bf16[16,54,768]{2,1,0:T(8,128)(2,1)} %all_to_all.32.parts), custom_call_target="tpu_custom_call" | custom-call | flops 1000000 | bytes 8388608 | tf_op jit(solution)/shard_map/sum_over_ctx/pallas_call | solution.py:621
  194.1 3.7 %all-to-all-start.5 = ((bf16[16,54,768]{2,1,0:T(8,128)(2,1)}), bf16[16,54,768]{2,1,0:T(8,128)(2,1)S(1)}, u32[]{:S(2)}, u32[]{:S(2)}) async-start(bf16[16,54,768]{2,1,0:T(8,128)(2,1)} %sum_over_ctx.3), calls=%async_computation.6 | async-start | bytes 2752512 | tf_op jit(solution)/shard_map/sum_over_ctx/all_to_all | solution.py:645
  197.8 4.6 %token_gradient.1 = f32[128,768]{1,0:T(8,128)} custom-call(bf16[768,2304]{1,0:T(8,128)(2,1)} %all-gather.4.cloned.1.call-done.weight, bf16[128,768]{1,0:T(8,128)(2,1)} %bitcast.78, bf16[16,64,384]{2,1,0:T(8,128)(2,1)} %copy-done.1, f32[1,768]{1,0:T(1,128)} %reshape.109.refs_12_.gain, f32[128,768]{1,0:T(8,128)} %get-tuple-element.77.grad_residual), custom_call_target="tpu_custom_call" | custom-call | flops 452984832 | bytes 8388608 | tf_op jit(solution)/shard_map/token_gradient/pallas_call | solution.py:512
  202.4 2.4 %sum_over_ctx.4 = (f32[96,2304]{1,0:T(8,128)}, f32[1,96]{1,0:T(1,128)}, f32[1,96]{1,0:T(1,128)}, f32[1,192]{1,0:T(1,128)}, f32[1,96]{1,0:T(1,128)}, /*index=5*/f...) custom-call(bf16[16,32,768]{2,1,0:T(8,128)(2,1)} %all_to_all.31.pieces), custom_call_target="tpu_custom_call" | custom-call | flops 1000000 | bytes 8388608 | tf_op jit(solution)/shard_map/sum_over_ctx/pallas_call | solution.py:603
  204.8 1.3 reduce
  206.1 10.0 %all-to-all-done.5.pieces = bf16[16,54,768]{2,1,0:T(8,128)(2,1)S(1)} async-done(((bf16[16,54,768]{2,1,0:T(8,128)(2,1)}), bf16[16,54,768]{2,1,0:T(8,128)(2,1)S(1)}, u32[]{:S(2)}, u32[]{:S(2)}) %all-to-all-start.5) | async-done | bytes 1327136 | tf_op jit(solution)/shard_map/sum_over_ctx/all_to_all | solution.py:645
  216.1 1.1 copy-done
  217.2 2.9 %sum_over_ctx.5 = (f32[96,768]{1,0:T(8,128)}, f32[96,3072]{1,0:T(8,128)}, f32[384,768]{1,0:T(8,128)}) custom-call(bf16[16,54,768]{2,1,0:T(8,128)(2,1)} %copy-done), custom_call_target="tpu_custom_call" | custom-call | flops 1000000 | bytes 8388608 | tf_op jit(solution)/shard_map/sum_over_ctx/pallas_call | solution.py:635
  (108 shorter events, 4.3 us)
Async XLA Ops:
  7.2 74.3 %all-gather.6.cloned.1.call-start = ((), (), s32[]{:S(2)}) async-start(), calls=%async_computation.9 | async-start | bytes 11943936 | tf_op jit(solution)/shard_map/gather_weights/all_gather | solution.py:739
  11.5 1.4 copy-start.14
  11.5 1.4 copy-start.15
  11.5 1.4 copy-start.16
  11.5 1.4 copy-start.17
  11.5 1.4 copy-start.18
  11.6 1.4 copy-start.19
  11.6 1.4 copy-start.20
  11.6 1.4 copy-start.21
  11.6 6.7 %copy-start.2 = (bf16[128,768]{1,0:T(8,128)(2,1)S(1)}, bf16[128,768]{1,0:T(8,128)(2,1)}, u32[]{:S(2)}) copy-start(bf16[128,768]{1,0:T(8,128)(2,1)} %gather_tokens.1) | copy-start | bytes 589828
  13.5 10.0 %collective-permute-start.14 = (bf16[112,192]{0,1:T(8,128)(2,1)S(1)}, bf16[112,192]{0,1:T(8,128)(2,1)S(1)}, u32[]{:S(2)}, u32[]{:S(2)}) collective-permute-start(bf16[112,192]{0,1:T(8,128)(2,1)S(1)} %maximum_maximum_fusion), channel_id=1, source_target_pairs={{0,6},{1,7},{2,0},{3,1},{4,2},{5,3},{6,4},{7,5},{8,14},{9,15},{10,... | collective-permute-start | bytes 129032 | tf_op jit(solution)/shard_map/gather_small/ppermute | solution.py:662
  16.7 9.1 %collective-permute-start.15 = (bf16[112,192]{0,1:T(8,128)(2,1)S(1)}, bf16[112,192]{0,1:T(8,128)(2,1)S(1)}, u32[]{:S(2)}, u32[]{:S(2)}) collective-permute-start(bf16[112,192]{0,1:T(8,128)(2,1)S(1)} %maximum_maximum_fusion), channel_id=1, source_target_pairs={{0,4},{1,5},{2,6},{3,7},{4,0},{5,1},{6,2},{7,3},{8,12},{9,13},{10,... | collective-permute-start | bytes 129032 | tf_op jit(solution)/shard_map/gather_small/ppermute | solution.py:662
  17.3 9.9 %collective-permute-start.16 = (bf16[112,192]{0,1:T(8,128)(2,1)S(1)}, bf16[112,192]{0,1:T(8,128)(2,1)S(1)}, u32[]{:S(2)}, u32[]{:S(2)}) collective-permute-start(bf16[112,192]{0,1:T(8,128)(2,1)S(1)} %maximum_maximum_fusion), channel_id=1, source_target_pairs={{0,2},{1,3},{2,4},{3,5},{4,6},{5,7},{6,0},{7,1},{8,10},{9,11},{10,... | collective-permute-start | bytes 129032 | tf_op jit(solution)/shard_map/gather_small/ppermute | solution.py:662
  18.3 10.7 %collective-permute-start.9 = (bf16[64,768]{1,0:T(8,128)(2,1)S(1)}, bf16[64,768]{1,0:T(8,128)(2,1)S(1)}, u32[]{:S(2)}, u32[]{:S(2)}) collective-permute-start(bf16[64,768]{1,0:T(8,128)(2,1)S(1)} %get-tuple-element.107), channel_id=1, source_target_pairs={{0,64},{1,65},{2,66},{3,67},{4,68},{5,69},{6,70},{7,71},{8,72},{9,... | collective-permute-start | bytes 294920 | tf_op jit(solution)/shard_map/gather_tokens/ppermute | solution.py:662
  22.3 8.7 %collective-permute-start.7 = (bf16[64,768]{1,0:T(8,128)(2,1)S(1)}, bf16[64,768]{1,0:T(8,128)(2,1)S(1)}, u32[]{:S(2)}, u32[]{:S(2)}) collective-permute-start(bf16[64,768]{1,0:T(8,128)(2,1)S(1)} %get-tuple-element.107), channel_id=1, source_target_pairs={{0,32},{1,33},{2,34},{3,35},{4,36},{5,37},{6,38},{7,39},{8,40},{9,... | collective-permute-start | bytes 294920 | tf_op jit(solution)/shard_map/gather_tokens/ppermute | solution.py:662
  23.5 7.4 %collective-permute-start.8 = (bf16[64,768]{1,0:T(8,128)(2,1)S(1)}, bf16[64,768]{1,0:T(8,128)(2,1)S(1)}, u32[]{:S(2)}, u32[]{:S(2)}) collective-permute-start(bf16[64,768]{1,0:T(8,128)(2,1)S(1)} %get-tuple-element.107), channel_id=1, source_target_pairs={{0,96},{1,97},{2,98},{3,99},{4,100},{5,101},{6,102},{7,103},{8,104... | collective-permute-start | bytes 294920 | tf_op jit(solution)/shard_map/gather_tokens/ppermute | solution.py:662
  25.8 6.9 %collective-permute-start = (bf16[64,768]{1,0:T(8,128)(2,1)S(1)}, bf16[64,768]{1,0:T(8,128)(2,1)S(1)}, u32[]{:S(2)}, u32[]{:S(2)}) collective-permute-start(bf16[64,768]{1,0:T(8,128)(2,1)S(1)} %get-tuple-element.108), channel_id=1, source_target_pairs={{0,8},{1,9},{2,10},{3,11},{4,12},{5,13},{6,14},{7,15},{8,16},{9,17... | collective-permute-start | bytes 294920 | tf_op jit(solution)/shard_map/gather_tokens/ppermute | solution.py:662
  27.2 7.1 %collective-permute-start.1 = (bf16[64,768]{1,0:T(8,128)(2,1)S(1)}, bf16[64,768]{1,0:T(8,128)(2,1)S(1)}, u32[]{:S(2)}, u32[]{:S(2)}) collective-permute-start(bf16[64,768]{1,0:T(8,128)(2,1)S(1)} %get-tuple-element.108), channel_id=1, source_target_pairs={{0,24},{1,25},{2,26},{3,27},{4,28},{5,29},{6,30},{7,31},{8,0},{9,1... | collective-permute-start | bytes 294920 | tf_op jit(solution)/shard_map/gather_tokens/ppermute | solution.py:662
  29.1 6.7 %collective-permute-start.2 = (bf16[64,768]{1,0:T(8,128)(2,1)S(1)}, bf16[64,768]{1,0:T(8,128)(2,1)S(1)}, u32[]{:S(2)}, u32[]{:S(2)}) collective-permute-start(bf16[64,768]{1,0:T(8,128)(2,1)S(1)} %get-tuple-element.108), channel_id=1, source_target_pairs={{0,16},{1,17},{2,18},{3,19},{4,20},{5,21},{6,22},{7,23},{8,24},{9,... | collective-permute-start | bytes 294920 | tf_op jit(solution)/shard_map/gather_tokens/ppermute | solution.py:662
  31.0 8.2 %collective-permute-start.17 = (bf16[4,112,192]{1,2,0:T(8,128)(2,1)S(1)}, bf16[4,112,192]{1,2,0:T(8,128)(2,1)S(1)}, u32[]{:S(2)}, u32[]{:S(2)}) collective-permute-start(bf16[4,112,192]{1,2,0:T(8,128)(2,1)S(1)} %pad_maximum_fusion.2), channel_id=1, source_target_pairs={{0,1},{1,0},{2,3},{3,2},{4,5},{5,4},{6,7},{7,6},{8,9},{9,8},{10,11... | collective-permute-start | bytes 516104 | tf_op jit(solution)/shard_map/gather_small/ppermute | solution.py:662
  31.0 8.6 %copy-start.3 = (bf16[4,64,768]{2,1,0:T(8,128)(2,1)}, bf16[4,64,768]{2,1,0:T(8,128)(2,1)S(1)}, u32[]{:S(2)}) copy-start(bf16[4,64,768]{2,1,0:T(8,128)(2,1)S(1)} %pad_maximum_fusion.1.refs_5_) | copy-start | bytes 1179652
  31.0 13.0 %collective-permute-start.10 = (bf16[4,64,768]{2,1,0:T(8,128)(2,1)S(1)}, bf16[4,64,768]{2,1,0:T(8,128)(2,1)S(1)}, u32[]{:S(2)}, u32[]{:S(2)}) collective-permute-start(bf16[4,64,768]{2,1,0:T(8,128)(2,1)S(1)} %pad_maximum_fusion.1.refs_5_), channel_id=1, source_target_pairs={{0,8},{1,9},{2,10},{3,11},{4,12},{5,13},{6,14},{7,15},{8,16},{9,17... | collective-permute-start | bytes 1179656 | tf_op jit(solution)/shard_map/gather_tokens/ppermute | solution.py:662
  32.6 11.5 %collective-permute-start.11 = (bf16[4,64,768]{2,1,0:T(8,128)(2,1)S(1)}, bf16[4,64,768]{2,1,0:T(8,128)(2,1)S(1)}, u32[]{:S(2)}, u32[]{:S(2)}) collective-permute-start(bf16[4,64,768]{2,1,0:T(8,128)(2,1)S(1)} %pad_maximum_fusion.1.refs_5_), channel_id=1, source_target_pairs={{0,24},{1,25},{2,26},{3,27},{4,28},{5,29},{6,30},{7,31},{8,0},{9,1... | collective-permute-start | bytes 1179656 | tf_op jit(solution)/shard_map/gather_tokens/ppermute | solution.py:662
  35.9 4.0 %copy-start.4 = (bf16[4,64,768]{2,1,0:T(8,128)(2,1)}, bf16[4,64,768]{2,1,0:T(8,128)(2,1)S(1)}, u32[]{:S(2)}) copy-start(bf16[4,64,768]{2,1,0:T(8,128)(2,1)S(1)} %pad_maximum_fusion.refs_0_) | copy-start | bytes 1179652
  35.9 11.6 %collective-permute-start.3 = (bf16[4,64,768]{2,1,0:T(8,128)(2,1)S(1)}, bf16[4,64,768]{2,1,0:T(8,128)(2,1)S(1)}, u32[]{:S(2)}, u32[]{:S(2)}) collective-permute-start(bf16[4,64,768]{2,1,0:T(8,128)(2,1)S(1)} %pad_maximum_fusion.refs_0_), channel_id=1, source_target_pairs={{0,32},{1,33},{2,34},{3,35},{4,36},{5,37},{6,38},{7,39},{8,40},{9,... | collective-permute-start | bytes 1179656 | tf_op jit(solution)/shard_map/gather_tokens/ppermute | solution.py:662
  36.0 11.6 %collective-permute-start.4 = (bf16[4,64,768]{2,1,0:T(8,128)(2,1)S(1)}, bf16[4,64,768]{2,1,0:T(8,128)(2,1)S(1)}, u32[]{:S(2)}, u32[]{:S(2)}) collective-permute-start(bf16[4,64,768]{2,1,0:T(8,128)(2,1)S(1)} %pad_maximum_fusion.refs_0_), channel_id=1, source_target_pairs={{0,96},{1,97},{2,98},{3,99},{4,100},{5,101},{6,102},{7,103},{8,104... | collective-permute-start | bytes 1179656 | tf_op jit(solution)/shard_map/gather_tokens/ppermute | solution.py:662
  44.0 10.9 %copy-start.7 = (bf16[4,64,768]{2,1,0:T(8,128)(2,1)}, bf16[4,64,768]{2,1,0:T(8,128)(2,1)S(1)}, u32[]{:S(2)}) copy-start(bf16[4,64,768]{2,1,0:T(8,128)(2,1)S(1)} %collective-permute-done.10.refs_6_) | copy-start | bytes 1179652
  44.1 8.0 %collective-permute-start.12 = (bf16[2,64,768]{2,1,0:T(8,128)(2,1)S(1)}, bf16[2,64,768]{2,1,0:T(8,128)(2,1)S(1)}, u32[]{:S(2)}, u32[]{:S(2)}) collective-permute-start(bf16[2,64,768]{2,1,0:T(8,128)(2,1)S(1)} %slice.78), channel_id=1, source_target_pairs={{0,8},{1,9},{2,10},{3,11},{4,12},{5,13},{6,14},{7,15},{8,16},{9,17... | collective-permute-start | bytes 589832 | tf_op jit(solution)/shard_map/gather_tokens/ppermute | solution.py:662
  44.1 10.8 %copy-start.8 = (bf16[4,64,768]{2,1,0:T(8,128)(2,1)}, bf16[4,64,768]{2,1,0:T(8,128)(2,1)S(1)}, u32[]{:S(2)}) copy-start(bf16[4,64,768]{2,1,0:T(8,128)(2,1)S(1)} %collective-permute-done.11.refs_7_) | copy-start | bytes 1179652
  44.2 7.9 %collective-permute-start.13 = (bf16[2,64,768]{2,1,0:T(8,128)(2,1)S(1)}, bf16[2,64,768]{2,1,0:T(8,128)(2,1)S(1)}, u32[]{:S(2)}, u32[]{:S(2)}) collective-permute-start(bf16[2,64,768]{2,1,0:T(8,128)(2,1)S(1)} %slice.79), channel_id=1, source_target_pairs={{0,24},{1,25},{2,26},{3,27},{4,28},{5,29},{6,30},{7,31},{8,0},{9,1... | collective-permute-start | bytes 589832 | tf_op jit(solution)/shard_map/gather_tokens/ppermute | solution.py:662
  47.5 7.5 %copy-start.9 = (bf16[4,64,768]{2,1,0:T(8,128)(2,1)}, bf16[4,64,768]{2,1,0:T(8,128)(2,1)S(1)}, u32[]{:S(2)}) copy-start(bf16[4,64,768]{2,1,0:T(8,128)(2,1)S(1)} %collective-permute-done.3.refs_1_) | copy-start | bytes 1179652
  47.5 7.5 %collective-permute-start.5 = (bf16[2,64,768]{2,1,0:T(8,128)(2,1)S(1)}, bf16[2,64,768]{2,1,0:T(8,128)(2,1)S(1)}, u32[]{:S(2)}, u32[]{:S(2)}) collective-permute-start(bf16[2,64,768]{2,1,0:T(8,128)(2,1)S(1)} %slice.75), channel_id=1, source_target_pairs={{0,32},{1,33},{2,34},{3,35},{4,36},{5,37},{6,38},{7,39},{8,40},{9,... | collective-permute-start | bytes 589832 | tf_op jit(solution)/shard_map/gather_tokens/ppermute | solution.py:662
  47.6 7.4 %copy-start.10 = (bf16[4,64,768]{2,1,0:T(8,128)(2,1)}, bf16[4,64,768]{2,1,0:T(8,128)(2,1)S(1)}, u32[]{:S(2)}) copy-start(bf16[4,64,768]{2,1,0:T(8,128)(2,1)S(1)} %collective-permute-done.4.refs_2_) | copy-start | bytes 1179652
  47.6 7.3 %collective-permute-start.6 = (bf16[2,64,768]{2,1,0:T(8,128)(2,1)S(1)}, bf16[2,64,768]{2,1,0:T(8,128)(2,1)S(1)}, u32[]{:S(2)}, u32[]{:S(2)}) collective-permute-start(bf16[2,64,768]{2,1,0:T(8,128)(2,1)S(1)} %slice.76), channel_id=1, source_target_pairs={{0,96},{1,97},{2,98},{3,99},{4,100},{5,101},{6,102},{7,103},{8,104... | collective-permute-start | bytes 589832 | tf_op jit(solution)/shard_map/gather_tokens/ppermute | solution.py:662
  52.1 2.9 %copy-start.22 = (bf16[2,64,768]{2,1,0:T(8,128)(2,1)}, bf16[2,64,768]{2,1,0:T(8,128)(2,1)S(1)}, u32[]{:S(2)}) copy-start(bf16[2,64,768]{2,1,0:T(8,128)(2,1)S(1)} %collective-permute-done.12.refs_8_) | copy-start | bytes 589828
  52.1 2.9 %copy-start.23 = (bf16[2,64,768]{2,1,0:T(8,128)(2,1)}, bf16[2,64,768]{2,1,0:T(8,128)(2,1)S(1)}, u32[]{:S(2)}) copy-start(bf16[2,64,768]{2,1,0:T(8,128)(2,1)S(1)} %collective-permute-done.13.refs_9_) | copy-start | bytes 589828
  54.9 0.7 copy-start.24
  55.0 0.7 copy-start.25
  68.2 13.2 %all-to-all-start = ((bf16[16,64,128]{2,1,0:T(8,128)(2,1)}), bf16[16,64,128]{2,1,0:T(8,128)(2,1)S(1)}, u32[]{:S(2)}, u32[]{:S(2)}) async-start(bf16[16,64,128]{2,1,0:T(8,128)(2,1)} %get-tuple-element.58), calls=%async_computation | async-start | bytes 524288 | tf_op jit(solution)/shard_map/attention/all_to_all | solution.py:645
  72.7 95.4 %reduce-scatter.2.cloned.1.call-start = ((), (), s32[]{:S(2)}) async-start(), calls=%async_computation.8 | async-start | bytes 11943936 | tf_op jit(solution)/shard_map/feed_forward/reduce_scatter | solution.py:779
  81.4 0.7 copy-start.5
  96.4 1.0 copy-start.6
  122.8 24.3 %all-to-all-start.2 = ((bf16[16,64,384]{2,1,0:T(8,128)(2,1)}), bf16[16,64,384]{2,1,0:T(8,128)(2,1)S(1)}, u32[]{:S(2)}, u32[]{:S(2)}) async-start(bf16[16,64,384]{2,1,0:T(8,128)(2,1)} %get-tuple-element.73), calls=%async_computation.2 | async-start | bytes 1572864 | tf_op jit(solution)/shard_map/attention_back/all_to_all | solution.py:645
  126.4 71.4 %all-gather.4.cloned.1.call-start = ((), (), s32[]{:S(2)}) async-start(), calls=%async_computation.7 | async-start | bytes 3981312 | tf_op jit(solution)/shard_map/token_gradient/all_gather | solution.py:812
  132.0 1.5 collective-permute-start.18
  135.4 6.1 %collective-permute-start.19 = (bf16[104,192]{1,0:T(8,128)(2,1)S(1)}, bf16[104,192]{1,0:T(8,128)(2,1)S(1)}, u32[]{:S(2)}, u32[]{:S(2)}) collective-permute-start(bf16[104,192]{1,0:T(8,128)(2,1)S(1)} %get-tuple-element.103), channel_id=1, source_target_pairs={{0,2},{1,3},{2,4},{3,5},{4,6},{5,7},{6,0},{7,1},{8,10},{9,11},{10,... | collective-permute-start | bytes 119816 | tf_op jit(solution)/shard_map/early_grads/ppermute | solution.py:662
  137.1 5.3 %collective-permute-start.20 = (bf16[104,192]{1,0:T(8,128)(2,1)S(1)}, bf16[104,192]{1,0:T(8,128)(2,1)S(1)}, u32[]{:S(2)}, u32[]{:S(2)}) collective-permute-start(bf16[104,192]{1,0:T(8,128)(2,1)S(1)} %get-tuple-element.102), channel_id=1, source_target_pairs={{0,6},{1,7},{2,0},{3,1},{4,2},{5,3},{6,4},{7,5},{8,14},{9,15},{10,... | collective-permute-start | bytes 119816 | tf_op jit(solution)/shard_map/early_grads/ppermute | solution.py:662
  138.6 6.3 %collective-permute-start.21 = (bf16[104,192]{1,0:T(8,128)(2,1)S(1)}, bf16[104,192]{1,0:T(8,128)(2,1)S(1)}, u32[]{:S(2)}, u32[]{:S(2)}) collective-permute-start(bf16[104,192]{1,0:T(8,128)(2,1)S(1)} %get-tuple-element.101), channel_id=1, source_target_pairs={{0,4},{1,5},{2,6},{3,7},{4,0},{5,1},{6,2},{7,3},{8,12},{9,13},{10,... | collective-permute-start | bytes 119816 | tf_op jit(solution)/shard_map/early_grads/ppermute | solution.py:662
  141.5 3.4 %copy-start.11 = (bf16[104,192]{1,0:T(8,128)(2,1)}, bf16[104,192]{1,0:T(8,128)(2,1)S(1)}, u32[]{:S(2)}) copy-start(bf16[104,192]{1,0:T(8,128)(2,1)S(1)} %collective-permute-done.19.left) | copy-start | bytes 119812
  142.4 2.5 %copy-start.12 = (bf16[104,192]{1,0:T(8,128)(2,1)}, bf16[104,192]{1,0:T(8,128)(2,1)S(1)}, u32[]{:S(2)}) copy-start(bf16[104,192]{1,0:T(8,128)(2,1)S(1)} %collective-permute-done.20.right) | copy-start | bytes 119812
  144.9 0.6 copy-start.13
  147.1 21.0 %copy-start.1 = (bf16[16,64,384]{2,1,0:T(8,128)(2,1)}, bf16[16,64,384]{2,1,0:T(8,128)(2,1)S(1)}, u32[]{:S(2)}) copy-start(bf16[16,64,384]{2,1,0:T(8,128)(2,1)S(1)} %all-to-all-done.2.heads_grad) | copy-start | bytes 2359300
  194.1 22.0 %all-to-all-start.5 = ((bf16[16,54,768]{2,1,0:T(8,128)(2,1)}), bf16[16,54,768]{2,1,0:T(8,128)(2,1)S(1)}, u32[]{:S(2)}, u32[]{:S(2)}) async-start(bf16[16,54,768]{2,1,0:T(8,128)(2,1)} %sum_over_ctx.3), calls=%async_computation.6 | async-start | bytes 2752512 | tf_op jit(solution)/shard_map/sum_over_ctx/all_to_all | solution.py:645
  216.1 1.1 copy-start
Sparse Core Ops, SparseCore 0:
  11.7 61.5 all-gather.5
  96.5 62.1 reduce-scatter.1
  160.5 29.2 all-gather.3

commit v5 on v4

--- a/solution.py
+++ b/solution.py
@@ -89,14 +89,19 @@
     return pl.ds(pl.multiple_of(index * size, size), size)
 
 
-def vmem_call(kernel, out_shape, scratch, flops, in_vmem, smem=0, transcendentals=0):
+def vmem_call(
+    kernel, out_shape, scratch, flops, in_vmem, smem=0, transcendentals=0, far_outs=()
+):
     specs = [pl.BlockSpec(memory_space=pltpu.VMEM)] * in_vmem
     specs = [pl.BlockSpec(memory_space=pltpu.SMEM)] * smem + specs
     return pl.pallas_call(
         kernel,
         out_shape=out_shape,
         in_specs=specs,
-        out_specs=[pl.BlockSpec(memory_space=pltpu.VMEM)] * len(out_shape),
+        out_specs=[
+            pl.BlockSpec(memory_space=pl.ANY if index in far_outs else pltpu.VMEM)
+            for index in range(len(out_shape))
+        ],
         scratch_shapes=scratch,
         compiler_params=pltpu.CompilerParams(vmem_limit_bytes=VMEM_LIMIT),
         cost_estimate=pl.CostEstimate(
@@ -131,7 +136,7 @@
 def head_forward_kernel(
     order, where, blocks, weight, bias, gain, shift,
     packed, hats, query, key, value, query_t, key_t, out_t, lse,
-    value_t,
+    value_t, projected,
 ):
     at_z, at_x = where[0] // SIDE, lax.rem(where[0], SIDE)
 
@@ -148,6 +153,8 @@
             query[to, :] = made[rows, 0:DEPTH]
             key[to, :] = made[rows, DEPTH : 2 * DEPTH]
             value[to, :] = made[rows, 2 * DEPTH :]
+
+    projected()
 
     def turn(t, _):
         rows = lanes_at(t, QT)
@@ -206,15 +213,16 @@
         block_refs, refs = refs[: len(layout)], refs[len(layout) :]
         (
             weight, bias, gain, shift,
-            packed, hats, query, key, value, query_t, key_t, out_t, lse,
-            value_t, out_rows,
+            packed, hats_out, query, key, value, query_t, key_t, out_t, lse,
+            value_t, out_rows, hats, sem,
         ) = refs
+        leave = pltpu.make_async_copy(hats, hats_out, sem.at[0])
         head_forward_kernel(
             order, where,
             [(half, offsets, ref) for (half, offsets), ref in zip(layout, block_refs)],
             weight, bias, gain, shift,
             packed, hats, query, key, value, query_t, key_t, out_t, lse,
-            value_t,
+            value_t, leave.start,
         )
 
         def turn_back(t, _):
@@ -232,6 +240,7 @@
             return 0
 
         lax.fori_loop(0, CTX, pack, 0)
+        leave.wait()
 
     shape = jax.ShapeDtypeStruct
     return vmem_call(
@@ -247,11 +256,17 @@
             shape((DEPTH, SEQ), F32),
             shape((SEQ // QT, QT), F32),
         ],
-        [pltpu.VMEM((DEPTH, SEQ), BF), pltpu.VMEM((SEQ, DEPTH), F32)],
+        [
+            pltpu.VMEM((DEPTH, SEQ), BF),
+            pltpu.VMEM((SEQ, DEPTH), F32),
+            pltpu.VMEM((SEQ, WIDTH), BF),
+            pltpu.SemaphoreType.DMA((1,)),
+        ],
         2 * 10**9,
         len(blocks) + 4,
         smem=2,
         transcendentals=3 * 10**6,
+        far_outs=(1,),
     )(order, where, *[block for _, _, block in blocks], weight, bias, gain, shift)
 
 
@@ -450,6 +465,10 @@
         back = result_grad.astype(F32) + norm_back(grad_normed, hat, inverse, gain[...])
         grad_residual[...] = back
         branch = back.astype(BF)
+        mix_grad[:, OUT_AT:UP_AT, :] = (
+            dot(attended_low.T, branch).astype(BF).reshape(FSDP, 96, WIDTH)
+        )
+        sent.append(send(0))
         grad_attended = dot_nt(branch, w_out)
         for head in range(HEADS):
             lanes = slice(head * DEPTH, (head + 1) * DEPTH)
@@ -458,10 +477,6 @@
             ).astype(BF)
         for head in range(HEADS, CTX):
             grad_heads[head] = jnp.zeros((HALF, 2 * DEPTH), BF)
-        mix_grad[:, OUT_AT:UP_AT, :] = (
-            dot(attended_low.T, branch).astype(BF).reshape(FSDP, 96, WIDTH)
-        )
-        sent.append(send(0))
         vector_sums[0:1, :] = jnp.sum(branch.astype(F32), axis=0, keepdims=True)
         vector_sums[1:2, :] = jnp.sum(grad_normed * hat, axis=0, keepdims=True)
         vector_sums[2:3, :] = jnp.sum(grad_normed, axis=0, keepdims=True)
@@ -571,9 +586,11 @@
         )
         head = jnp.concatenate([total[24 * k : 24 * (k + 1)] for k in range(4)], axis=1)
         line = jnp.concatenate([total[96:104], jnp.zeros((8, 9 * DEPTH), F32)], axis=1)
-        out[...] = jnp.concatenate([head, line], axis=0).astype(BF)
-
-    return vmem_call(kernel, [jax.ShapeDtypeStruct((EARLY_ROWS, WIDTH), BF)], [], 10**6, 4)(*parts)[0]
+        joined = jnp.concatenate([head, line], axis=0).astype(BF)
+        for target in range(CTX):
+            out[target] = joined
+
+    return vmem_call(kernel, [jax.ShapeDtypeStruct((CTX, EARLY_ROWS, WIDTH), BF)], [], 10**6, 4)(*parts)[0]
 
 
 def early_grads(pieces):
@@ -645,10 +662,6 @@
     return lax.all_to_all(slots, axes, 0, 0, tiled=True)
 
 
-def spread(piece, axes, count):
-    return swap(jnp.broadcast_to(piece[None], (count,) + piece.shape), axes)
-
-
 def shift_by(value, z=0, x=0, y=0, core=0):
     pairs = []
     for at_z in range(SIDE):
@@ -795,11 +808,12 @@
             )
         )
         early, heads_grad = lax.optimization_barrier((early, heads_grad))
-        early = spread(early, "ctx", CTX)
+        early = swap(early, "ctx")
 
     with jax.named_scope("sum_over_ctx"):
-        mix_shard, early = lax.optimization_barrier((mix_shard, early))
-        parts = swap(mix_shard.reshape(CTX, SHARE, WIDTH), "ctx")
+        slots = mix_shard.reshape(CTX, SHARE, WIDTH)
+        slots, early = lax.optimization_barrier((slots, early))
+        parts = swap(slots, "ctx")
         shares, early = lax.optimization_barrier((last_pieces(parts), early))
         grad_out, grad_up, grad_down = last_grads(swap(shares, "ctx"))
         grad_qkv, *vector_grads = early_grads(early)

time: 228 us -> 225 us (0.987)
  blocking collectives: 53.7 us -> 33.8 us
  waiting for transfers between devices: 29.4 us -> 41 us
  starting transfers between devices: 45.8 us -> 53 us
    all_to_all x3 -> x2, blocking collectives: 53.7 us -> 33.8 us  [swap(): return lax.all_to_all(slots, axes, 0, 0, tiled=True)]
    all_to_all x3 -> x4, waiting for transfers between devices: 15.1 us -> 22.7 us  [swap(): return lax.all_to_all(slots, axes, 0, 0, tiled=True)]
    all_to_all x3 -> x4, starting transfers between devices: 11.9 us -> 19 us  [swap(): return lax.all_to_all(slots, axes, 0, 0, tiled=True)]
    reduce_scatter x1, waiting for transfers between devices: 0.01 us -> 4.08 us  [local(): lax.psum_scatter(mix_grad, 'fsdp', scatter_dimension=0, tiled=False)]
    unnamed x58 -> x60, local copies, waits for them, and re-layouts: 5.31 us -> 5.29 us
  transfers between devices with their start and end apart: 28 -> 29, of which waited for: 11 -> 13; matrix products, arithmetic and copies ran while one was open for 7% -> 6% of each run, Pallas kernels for 18% -> 18%
where the time goes in v5:
time: 225 us; the launch traced here: 224 us
  Pallas kernels  62.5 us (28%)
  starting transfers between devices  53 us (24%)
  waiting for transfers between devices  41 us (18%)
  blocking collectives  33.8 us (15%)
  local copies, waits for them, and re-layouts  14.5 us (6%)
  between operations  14.4 us (6%)
  other arithmetic  4.68 us (2%)
    all_to_all x2, blocking collectives, swap(): return lax.all_to_all(slots, axes, 0, 0, tiled=True)  33.8 us
    ppermute x22, starting transfers between devices, shift_by(): return lax.ppermute(value, ('ctx', 'fsdp'), pairs)  33.6 us
    all_to_all x4, waiting for transfers between devices, swap(): return lax.all_to_all(slots, axes, 0, 0, tiled=True)  22.7 us
    all_to_all x4, starting transfers between devices, swap(): return lax.all_to_all(slots, axes, 0, 0, tiled=True)  19 us
    ppermute x22, waiting for transfers between devices, shift_by(): return lax.ppermute(value, ('ctx', 'fsdp'), pairs)  14.2 us
    pallas_call x1, Pallas kernels, feed_forward(): pl.pallas_call(kernel, out_shape=outs, in_specs=[pl.BlockSpec(memory_spac...  14.1 us
    pallas_call x1, Pallas kernels, head_backward(): vmem_call(kernel, [shape((CTX, HALF, 6 * DEPTH), BF), shape((SEQ, 3 * DEP...  13.5 us
    pallas_call x1, Pallas kernels, head_forward(): vmem_call(kernel, [shape((CTX, HALF, 2 * DEPTH), BF), shape((SEQ, WIDTH),...  11.6 us
  transfers between devices with their start and end apart: 29, of which 13 were waited for; matrix products, arithmetic and copies ran while one was open for 6% of the time, Pallas kernels for 18%

profile of v5, /device:TPU:0, one launch (start us, length us, event | category | flops | bytes accessed | tf_op | source)
XLA Modules:
  0.0 223.9 jit_solution(16163978883135817606)
XLA Ops:
  7.2 1.8 gather_tokens.1
  9.1 2.5 %gather_weights.1 = bf16[864,768]{1,0:T(8,128)(2,1)} custom-call(bf16[96,768]{1,0:T(8,128)(2,1)} %out_weight, bf16[96,3072]{1,0:T(8,128)(2,1)} %up_weight, bf16[384,768]{1,0:T(8,128)(2,1)} %down_weight), custom_call_target="tpu_custom_call" | custom-call | flops 1000000 | bytes 8388608 | tf_op jit(solution)/shard_map/gather_weights/pallas_call | solution.py:122
  11.7 0.9 constant_dynamic-slice_fusion.4
  13.5 3.2 %collective-permute-start.14 = (bf16[112,192]{0,1:T(8,128)(2,1)S(1)}, bf16[112,192]{0,1:T(8,128)(2,1)S(1)}, u32[]{:S(2)}, u32[]{:S(2)}) collective-permute-start(bf16[112,192]{0,1:T(8,128)(2,1)S(1)} %maximum_maximum_fusion), channel_id=1, source_target_pairs={{0,6},{1,7},{2,0},{3,1},{4,2},{5,3},{6,4},{7,5},{8,14},{9,15},{10,... | collective-permute-start | bytes 129032 | tf_op jit(solution)/shard_map/gather_small/ppermute | solution.py:675
  16.7 0.6 collective-permute-start.15
  17.3 1.0 collective-permute-start.16
  18.3 4.0 %collective-permute-start.9 = (bf16[64,768]{1,0:T(8,128)(2,1)S(1)}, bf16[64,768]{1,0:T(8,128)(2,1)S(1)}, u32[]{:S(2)}, u32[]{:S(2)}) collective-permute-start(bf16[64,768]{1,0:T(8,128)(2,1)S(1)} %get-tuple-element.107), channel_id=1, source_target_pairs={{0,64},{1,65},{2,66},{3,67},{4,68},{5,69},{6,70},{7,71},{8,72},{9,... | collective-permute-start | bytes 294920 | tf_op jit(solution)/shard_map/gather_tokens/ppermute | solution.py:675
  22.3 1.0 collective-permute-start.7
  23.5 2.2 collective-permute-start.8
  25.8 1.5 collective-permute-start
  27.3 1.7 collective-permute-start.1
  29.1 1.9 collective-permute-start.2
  31.1 0.7 collective-permute-start.10
  31.7 0.9 collective-permute-done
  32.7 1.7 collective-permute-start.11
  34.4 1.5 collective-permute-done.2
  36.0 3.2 %collective-permute-start.4 = (bf16[4,64,768]{2,1,0:T(8,128)(2,1)S(1)}, bf16[4,64,768]{2,1,0:T(8,128)(2,1)S(1)}, u32[]{:S(2)}, u32[]{:S(2)}) collective-permute-start(bf16[4,64,768]{2,1,0:T(8,128)(2,1)S(1)} %pad_maximum_fusion.refs_0_), channel_id=1, source_target_pairs={{0,96},{1,97},{2,98},{3,99},{4,100},{5,101},{6,102},{7,103},{8,104... | collective-permute-start | bytes 1179656 | tf_op jit(solution)/shard_map/gather_tokens/ppermute | solution.py:675
  40.3 0.7 reshape.105.refs_12_.gain
  40.9 0.7 reshape.106.refs_13_.shift
  41.6 1.0 copy.53
  42.6 1.4 collective-permute-done.10.refs_6_
  44.2 3.3 %collective-permute-start.13 = (bf16[2,64,768]{2,1,0:T(8,128)(2,1)S(1)}, bf16[2,64,768]{2,1,0:T(8,128)(2,1)S(1)}, u32[]{:S(2)}, u32[]{:S(2)}) collective-permute-start(bf16[2,64,768]{2,1,0:T(8,128)(2,1)S(1)} %slice.79), channel_id=1, source_target_pairs={{0,24},{1,25},{2,26},{3,27},{4,28},{5,29},{6,30},{7,31},{8,0},{9,1... | collective-permute-start | bytes 589832 | tf_op jit(solution)/shard_map/gather_tokens/ppermute | solution.py:675
  47.6 3.5 %collective-permute-start.6 = (bf16[2,64,768]{2,1,0:T(8,128)(2,1)S(1)}, bf16[2,64,768]{2,1,0:T(8,128)(2,1)S(1)}, u32[]{:S(2)}, u32[]{:S(2)}) collective-permute-start(bf16[2,64,768]{2,1,0:T(8,128)(2,1)S(1)} %slice.76), channel_id=1, source_target_pairs={{0,96},{1,97},{2,98},{3,99},{4,100},{5,101},{6,102},{7,103},{8,104... | collective-permute-start | bytes 589832 | tf_op jit(solution)/shard_map/gather_tokens/ppermute | solution.py:675
  52.1 2.9 %collective-permute-done.5.refs_3_ = bf16[2,64,768]{2,1,0:T(8,128)(2,1)S(1)} collective-permute-done((bf16[2,64,768]{2,1,0:T(8,128)(2,1)S(1)}, bf16[2,64,768]{2,1,0:T(8,128)(2,1)S(1)}, u32[]{:S(2)}, u32[]{:S(2)}) %collective-permute-start.5) | collective-permute-done | bytes 196640 | tf_op jit(solution)/shard_map/gather_tokens/ppermute | solution.py:675
  55.0 0.6 copy-done.25
  55.7 11.6 %attention.1 = (bf16[16,64,128]{2,1,0:T(8,128)(2,1)}, bf16[2048,768]{1,0:T(8,128)(2,1)}, bf16[2048,64]{1,0:T(8,128)(2,1)}, bf16[2048,64]{1,0:T(8,128)(2,1)}, bf1...) custom-call(s32[16]{0:T(128)} %order.3, ...), custom_call_target="tpu_custom_call" | custom-call | flops 2000000000 | bytes 8388608 | tf_op jit(solution)/shard_map/attention/pallas_call | solution.py:246
  67.3 4.5 %all-to-all-start = ((bf16[16,64,128]{2,1,0:T(8,128)(2,1)}), bf16[16,64,128]{2,1,0:T(8,128)(2,1)S(1)}, u32[]{:S(2)}, u32[]{:S(2)}) async-start(bf16[16,64,128]{2,1,0:T(8,128)(2,1)} %get-tuple-element.58), calls=%async_computation | async-start | bytes 524288 | tf_op jit(solution)/shard_map/attention/all_to_all | solution.py:662
  72.1 0.7 reshape.107.out_bias
  72.8 0.7 reshape.108.gain
  73.5 0.7 reshape.109.shift
  74.1 0.7 reshape.111.down_bias
  74.9 0.6 copy.64
  75.5 5.1 %all-to-all-done.heads_out = bf16[16,64,128]{2,1,0:T(8,128)(2,1)S(1)} async-done(((bf16[16,64,128]{2,1,0:T(8,128)(2,1)}), bf16[16,64,128]{2,1,0:T(8,128)(2,1)S(1)}, u32[]{:S(2)}, u32[]{:S(2)}) %all-to-all-start) | async-done | bytes 262176 | tf_op jit(solution)/shard_map/attention/all_to_all | solution.py:662
  80.6 0.7 copy-done.6
  81.3 14.1 %feed_forward.1 = (bf16[128,768]{1,0:T(8,128)(2,1)}, bf16[8,864,768]{2,1,0:T(8,128)(2,1)}, bf16[16,64,128]{2,1,0:T(8,128)(2,1)}, f32[128,768]{1,0:T(8,128)}, f32[4,768]{1,0:T(4,128)}, /*index=5*/f32[1,3072]{1,0:T(1,128)}) custom-call(bf16[8,864,768]{2,1,0:T(8,128)(2,1)} %bitcast.92, bf16[128,768]{1,0:T(8,128)(2,1)} %bitcast.75, ...), custom_call_target="tpu_custom_call" | custom-call | flops 4000000000 | bytes 25165824 | tf_op jit(solution)/shard_map/feed_forward/pallas_call | solution.py:496
  95.4 0.9 copy-done.7
  96.3 12.0 %all_to_all.30.upstream = bf16[16,64,128]{2,1,0:T(8,128)(2,1)} all-to-all(bf16[16,64,128]{2,1,0:T(8,128)(2,1)S(1)} %copy-done.7), channel_id=1, replica_groups=mesh['ctx'=16,'fsdp'=8] {'ctx'}, dimensions={0} | all-to-all | bytes 524288 | tf_op jit(solution)/shard_map/feed_forward/all_to_all | solution.py:662
  108.3 13.5 %attention_back.1 = (bf16[16,64,384]{2,1,0:T(8,128)(2,1)}, bf16[2048,192]{1,0:T(8,128)(2,1)}, f32[1,192]{1,0:T(1,128)}) custom-call(s32[16]{0:T(128)} %order.3, bf16[16,64,128]{2,1,0:T(8,128)(2,1)} %all_to_all.30.upstream, bf16[2048,64]{1,0:T(8,128)(2,1)} %get-tuple-element.62.query, bf16[2048,64]{1,0:T(8,128)(2,1)} %get-tuple-element.63.key, ...), custom_call_target="tpu_custom_call" | custom-call | flops 4000000000 | bytes 8388608 | tf_op jit(solution)/shard_map/attention_back/pallas_call | solution.py:358
  121.8 3.6 %all-to-all-start.2 = ((bf16[16,64,384]{2,1,0:T(8,128)(2,1)}), bf16[16,64,384]{2,1,0:T(8,128)(2,1)S(1)}, u32[]{:S(2)}, u32[]{:S(2)}) async-start(bf16[16,64,384]{2,1,0:T(8,128)(2,1)} %get-tuple-element.73), calls=%async_computation.2 | async-start | bytes 1572864 | tf_op jit(solution)/shard_map/attention_back/all_to_all | solution.py:662
  125.5 4.5 %early_grads.2 = bf16[8,104,192]{2,1,0:T(8,128)(2,1)} custom-call(s32[1]{0:T(128)} %bitcast.2.where, bf16[2048,768]{1,0:T(8,128)(2,1)} %get-tuple-element.60.hats, bf16[2048,192]{1,0:T(8,128)(2,1)} %get-tuple-element.69.rows, bf16[768,192]{1,0:T(8,128)(2,1)} %bitcast.73, f32[1,768]{1,0:T(1,128)} %reshape.105.refs_12_.gain, ...), custom_call_target="tpu_custom_call" | custom-call | flops 603979776 | bytes 8388608 | tf_op jit(solution)/shard_map/early_grads/pallas_call | solution.py:571
  130.0 1.1 select_bitcast_fusion
  131.2 1.4 collective-permute-done.18
  132.6 1.1 fusion
  133.7 0.7 dynamic-slice_bitcast_fusion
  134.4 1.7 collective-permute-start.19
  136.1 1.5 collective-permute-start.20
  137.6 0.6 collective-permute-start.21
  138.3 2.2 collective-permute-done.19.left
  140.5 0.9 collective-permute-done.20.right
  141.4 2.6 %collective-permute-done.21.far = bf16[104,192]{1,0:T(8,128)(2,1)S(1)} collective-permute-done((bf16[104,192]{1,0:T(8,128)(2,1)S(1)}, bf16[104,192]{1,0:T(8,128)(2,1)S(1)}, u32[]{:S(2)}, u32[]{:S(2)}) %collective-permute-start.21) | collective-permute-done | bytes 39968 | tf_op jit(solution)/shard_map/early_grads/ppermute | solution.py:675
  144.5 1.9 early_grads.3
  146.5 7.2 %all-to-all-start.3 = ((bf16[16,32,768]{2,1,0:T(8,128)(2,1)}), bf16[16,32,768]{2,1,0:T(8,128)(2,1)S(1)}, u32[]{:S(2)}, u32[]{:S(2)}) async-start(bf16[16,32,768]{2,1,0:T(8,128)(2,1)} %early_grads.3), calls=%async_computation.4 | async-start | bytes 1572864 | tf_op jit(solution)/shard_map/early_grads/all_to_all | solution.py:662
  153.6 4.1 %reduce-scatter.2.cloned.1.call-done = bf16[1,864,768]{2,1,0:T(8,128)(2,1)} async-done(((bf16[8,864,768]{2,1,0:T(8,128)(2,1)}), bf16[1,864,768]{2,1,0:T(8,128)(2,1)}) %reduce-scatter.2.cloned.1.call-update) | async-done | bytes 1327120 | tf_op jit(solution)/shard_map/feed_forward/reduce_scatter | solution.py:792
  157.7 1.5 reduce_scatter.11
  159.2 7.5 %all-to-all-done.3.pieces = bf16[16,32,768]{2,1,0:T(8,128)(2,1)S(1)} async-done(((bf16[16,32,768]{2,1,0:T(8,128)(2,1)}), bf16[16,32,768]{2,1,0:T(8,128)(2,1)S(1)}, u32[]{:S(2)}, u32[]{:S(2)}) %all-to-all-start.3) | async-done | bytes 786464 | tf_op jit(solution)/shard_map/early_grads/all_to_all | solution.py:662
  166.7 21.8 %all_to_all.31.parts = bf16[16,54,768]{2,1,0:T(8,128)(2,1)} all-to-all(bf16[16,54,768]{2,1,0:T(8,128)(2,1)S(1)} %reduce_scatter.11), channel_id=1, replica_groups=mesh['ctx'=16,'fsdp'=8] {'ctx'}, dimensions={0} | all-to-all | bytes 2654208 | tf_op jit(solution)/shard_map/sum_over_ctx/all_to_all | solution.py:662
  188.5 2.7 %sum_over_ctx.3 = bf16[16,54,768]{2,1,0:T(8,128)(2,1)} custom-call(bf16[16,54,768]{2,1,0:T(8,128)(2,1)} %all_to_all.31.parts), custom_call_target="tpu_custom_call" | custom-call | flops 1000000 | bytes 8388608 | tf_op jit(solution)/shard_map/sum_over_ctx/pallas_call | solution.py:638
  191.2 3.7 %all-to-all-start.5 = ((bf16[16,54,768]{2,1,0:T(8,128)(2,1)}), bf16[16,54,768]{2,1,0:T(8,128)(2,1)S(1)}, u32[]{:S(2)}, u32[]{:S(2)}) async-start(bf16[16,54,768]{2,1,0:T(8,128)(2,1)} %sum_over_ctx.3), calls=%async_computation.6 | async-start | bytes 2752512 | tf_op jit(solution)/shard_map/sum_over_ctx/all_to_all | solution.py:662
  194.9 4.6 %token_gradient.1 = f32[128,768]{1,0:T(8,128)} custom-call(bf16[768,2304]{1,0:T(8,128)(2,1)} %all-gather.4.cloned.1.call-done.weight, bf16[128,768]{1,0:T(8,128)(2,1)} %bitcast.76, bf16[16,64,384]{2,1,0:T(8,128)(2,1)} %copy-done.2, f32[1,768]{1,0:T(1,128)} %reshape.105.refs_12_.gain, f32[128,768]{1,0:T(8,128)} %get-tuple-element.77.grad_residual), custom_call_target="tpu_custom_call" | custom-call | flops 452984832 | bytes 8388608 | tf_op jit(solution)/shard_map/token_gradient/pallas_call | solution.py:527
  199.5 2.4 %sum_over_ctx.4 = (f32[96,2304]{1,0:T(8,128)}, f32[1,96]{1,0:T(1,128)}, f32[1,96]{1,0:T(1,128)}, f32[1,192]{1,0:T(1,128)}, f32[1,96]{1,0:T(1,128)}, /*index=5*/f...) custom-call(bf16[16,32,768]{2,1,0:T(8,128)(2,1)} %copy-done.1), custom_call_target="tpu_custom_call" | custom-call | flops 1000000 | bytes 8388608 | tf_op jit(solution)/shard_map/sum_over_ctx/pallas_call | solution.py:620
  201.9 1.3 reduce
  203.2 10.1 %all-to-all-done.5.pieces = bf16[16,54,768]{2,1,0:T(8,128)(2,1)S(1)} async-done(((bf16[16,54,768]{2,1,0:T(8,128)(2,1)}), bf16[16,54,768]{2,1,0:T(8,128)(2,1)S(1)}, u32[]{:S(2)}, u32[]{:S(2)}) %all-to-all-start.5) | async-done | bytes 1327136 | tf_op jit(solution)/shard_map/sum_over_ctx/all_to_all | solution.py:662
  213.3 1.1 copy-done
  214.4 2.9 %sum_over_ctx.5 = (f32[96,768]{1,0:T(8,128)}, f32[96,3072]{1,0:T(8,128)}, f32[384,768]{1,0:T(8,128)}) custom-call(bf16[16,54,768]{2,1,0:T(8,128)(2,1)} %copy-done), custom_call_target="tpu_custom_call" | custom-call | flops 1000000 | bytes 8388608 | tf_op jit(solution)/shard_map/sum_over_ctx/pallas_call | solution.py:652
  (110 shorter events, 4.9 us)
Async XLA Ops:
  7.2 73.4 %all-gather.6.cloned.1.call-start = ((), (), s32[]{:S(2)}) async-start(), calls=%async_computation.9 | async-start | bytes 11943936 | tf_op jit(solution)/shard_map/gather_weights/all_gather | solution.py:752
  11.6 1.4 copy-start.15
  11.6 1.4 copy-start.16
  11.6 1.4 copy-start.17
  11.6 1.4 copy-start.18
  11.6 1.4 copy-start.19
  11.6 1.4 copy-start.20
  11.6 1.4 copy-start.21
  11.6 1.4 copy-start.22
  11.6 6.7 %copy-start.3 = (bf16[128,768]{1,0:T(8,128)(2,1)S(1)}, bf16[128,768]{1,0:T(8,128)(2,1)}, u32[]{:S(2)}) copy-start(bf16[128,768]{1,0:T(8,128)(2,1)} %gather_tokens.1) | copy-start | bytes 589828
  13.5 10.0 %collective-permute-start.14 = (bf16[112,192]{0,1:T(8,128)(2,1)S(1)}, bf16[112,192]{0,1:T(8,128)(2,1)S(1)}, u32[]{:S(2)}, u32[]{:S(2)}) collective-permute-start(bf16[112,192]{0,1:T(8,128)(2,1)S(1)} %maximum_maximum_fusion), channel_id=1, source_target_pairs={{0,6},{1,7},{2,0},{3,1},{4,2},{5,3},{6,4},{7,5},{8,14},{9,15},{10,... | collective-permute-start | bytes 129032 | tf_op jit(solution)/shard_map/gather_small/ppermute | solution.py:675
  16.7 9.1 %collective-permute-start.15 = (bf16[112,192]{0,1:T(8,128)(2,1)S(1)}, bf16[112,192]{0,1:T(8,128)(2,1)S(1)}, u32[]{:S(2)}, u32[]{:S(2)}) collective-permute-start(bf16[112,192]{0,1:T(8,128)(2,1)S(1)} %maximum_maximum_fusion), channel_id=1, source_target_pairs={{0,4},{1,5},{2,6},{3,7},{4,0},{5,1},{6,2},{7,3},{8,12},{9,13},{10,... | collective-permute-start | bytes 129032 | tf_op jit(solution)/shard_map/gather_small/ppermute | solution.py:675
  17.3 9.9 %collective-permute-start.16 = (bf16[112,192]{0,1:T(8,128)(2,1)S(1)}, bf16[112,192]{0,1:T(8,128)(2,1)S(1)}, u32[]{:S(2)}, u32[]{:S(2)}) collective-permute-start(bf16[112,192]{0,1:T(8,128)(2,1)S(1)} %maximum_maximum_fusion), channel_id=1, source_target_pairs={{0,2},{1,3},{2,4},{3,5},{4,6},{5,7},{6,0},{7,1},{8,10},{9,11},{10,... | collective-permute-start | bytes 129032 | tf_op jit(solution)/shard_map/gather_small/ppermute | solution.py:675
  18.3 10.7 %collective-permute-start.9 = (bf16[64,768]{1,0:T(8,128)(2,1)S(1)}, bf16[64,768]{1,0:T(8,128)(2,1)S(1)}, u32[]{:S(2)}, u32[]{:S(2)}) collective-permute-start(bf16[64,768]{1,0:T(8,128)(2,1)S(1)} %get-tuple-element.107), channel_id=1, source_target_pairs={{0,64},{1,65},{2,66},{3,67},{4,68},{5,69},{6,70},{7,71},{8,72},{9,... | collective-permute-start | bytes 294920 | tf_op jit(solution)/shard_map/gather_tokens/ppermute | solution.py:675
  22.3 8.7 %collective-permute-start.7 = (bf16[64,768]{1,0:T(8,128)(2,1)S(1)}, bf16[64,768]{1,0:T(8,128)(2,1)S(1)}, u32[]{:S(2)}, u32[]{:S(2)}) collective-permute-start(bf16[64,768]{1,0:T(8,128)(2,1)S(1)} %get-tuple-element.107), channel_id=1, source_target_pairs={{0,32},{1,33},{2,34},{3,35},{4,36},{5,37},{6,38},{7,39},{8,40},{9,... | collective-permute-start | bytes 294920 | tf_op jit(solution)/shard_map/gather_tokens/ppermute | solution.py:675
  23.5 7.4 %collective-permute-start.8 = (bf16[64,768]{1,0:T(8,128)(2,1)S(1)}, bf16[64,768]{1,0:T(8,128)(2,1)S(1)}, u32[]{:S(2)}, u32[]{:S(2)}) collective-permute-start(bf16[64,768]{1,0:T(8,128)(2,1)S(1)} %get-tuple-element.107), channel_id=1, source_target_pairs={{0,96},{1,97},{2,98},{3,99},{4,100},{5,101},{6,102},{7,103},{8,104... | collective-permute-start | bytes 294920 | tf_op jit(solution)/shard_map/gather_tokens/ppermute | solution.py:675
  25.8 6.9 %collective-permute-start = (bf16[64,768]{1,0:T(8,128)(2,1)S(1)}, bf16[64,768]{1,0:T(8,128)(2,1)S(1)}, u32[]{:S(2)}, u32[]{:S(2)}) collective-permute-start(bf16[64,768]{1,0:T(8,128)(2,1)S(1)} %get-tuple-element.108), channel_id=1, source_target_pairs={{0,8},{1,9},{2,10},{3,11},{4,12},{5,13},{6,14},{7,15},{8,16},{9,17... | collective-permute-start | bytes 294920 | tf_op jit(solution)/shard_map/gather_tokens/ppermute | solution.py:675
  27.3 7.1 %collective-permute-start.1 = (bf16[64,768]{1,0:T(8,128)(2,1)S(1)}, bf16[64,768]{1,0:T(8,128)(2,1)S(1)}, u32[]{:S(2)}, u32[]{:S(2)}) collective-permute-start(bf16[64,768]{1,0:T(8,128)(2,1)S(1)} %get-tuple-element.108), channel_id=1, source_target_pairs={{0,24},{1,25},{2,26},{3,27},{4,28},{5,29},{6,30},{7,31},{8,0},{9,1... | collective-permute-start | bytes 294920 | tf_op jit(solution)/shard_map/gather_tokens/ppermute | solution.py:675
  29.1 6.7 %collective-permute-start.2 = (bf16[64,768]{1,0:T(8,128)(2,1)S(1)}, bf16[64,768]{1,0:T(8,128)(2,1)S(1)}, u32[]{:S(2)}, u32[]{:S(2)}) collective-permute-start(bf16[64,768]{1,0:T(8,128)(2,1)S(1)} %get-tuple-element.108), channel_id=1, source_target_pairs={{0,16},{1,17},{2,18},{3,19},{4,20},{5,21},{6,22},{7,23},{8,24},{9,... | collective-permute-start | bytes 294920 | tf_op jit(solution)/shard_map/gather_tokens/ppermute | solution.py:675
  31.0 8.2 %collective-permute-start.17 = (bf16[4,112,192]{1,2,0:T(8,128)(2,1)S(1)}, bf16[4,112,192]{1,2,0:T(8,128)(2,1)S(1)}, u32[]{:S(2)}, u32[]{:S(2)}) collective-permute-start(bf16[4,112,192]{1,2,0:T(8,128)(2,1)S(1)} %pad_maximum_fusion.2), channel_id=1, source_target_pairs={{0,1},{1,0},{2,3},{3,2},{4,5},{5,4},{6,7},{7,6},{8,9},{9,8},{10,11... | collective-permute-start | bytes 516104 | tf_op jit(solution)/shard_map/gather_small/ppermute | solution.py:675
  31.1 8.6 %copy-start.4 = (bf16[4,64,768]{2,1,0:T(8,128)(2,1)}, bf16[4,64,768]{2,1,0:T(8,128)(2,1)S(1)}, u32[]{:S(2)}) copy-start(bf16[4,64,768]{2,1,0:T(8,128)(2,1)S(1)} %pad_maximum_fusion.1.refs_5_) | copy-start | bytes 1179652
  31.1 13.0 %collective-permute-start.10 = (bf16[4,64,768]{2,1,0:T(8,128)(2,1)S(1)}, bf16[4,64,768]{2,1,0:T(8,128)(2,1)S(1)}, u32[]{:S(2)}, u32[]{:S(2)}) collective-permute-start(bf16[4,64,768]{2,1,0:T(8,128)(2,1)S(1)} %pad_maximum_fusion.1.refs_5_), channel_id=1, source_target_pairs={{0,8},{1,9},{2,10},{3,11},{4,12},{5,13},{6,14},{7,15},{8,16},{9,17... | collective-permute-start | bytes 1179656 | tf_op jit(solution)/shard_map/gather_tokens/ppermute | solution.py:675
  32.7 11.5 %collective-permute-start.11 = (bf16[4,64,768]{2,1,0:T(8,128)(2,1)S(1)}, bf16[4,64,768]{2,1,0:T(8,128)(2,1)S(1)}, u32[]{:S(2)}, u32[]{:S(2)}) collective-permute-start(bf16[4,64,768]{2,1,0:T(8,128)(2,1)S(1)} %pad_maximum_fusion.1.refs_5_), channel_id=1, source_target_pairs={{0,24},{1,25},{2,26},{3,27},{4,28},{5,29},{6,30},{7,31},{8,0},{9,1... | collective-permute-start | bytes 1179656 | tf_op jit(solution)/shard_map/gather_tokens/ppermute | solution.py:675
  35.9 4.0 %copy-start.5 = (bf16[4,64,768]{2,1,0:T(8,128)(2,1)}, bf16[4,64,768]{2,1,0:T(8,128)(2,1)S(1)}, u32[]{:S(2)}) copy-start(bf16[4,64,768]{2,1,0:T(8,128)(2,1)S(1)} %pad_maximum_fusion.refs_0_) | copy-start | bytes 1179652
  35.9 11.6 %collective-permute-start.3 = (bf16[4,64,768]{2,1,0:T(8,128)(2,1)S(1)}, bf16[4,64,768]{2,1,0:T(8,128)(2,1)S(1)}, u32[]{:S(2)}, u32[]{:S(2)}) collective-permute-start(bf16[4,64,768]{2,1,0:T(8,128)(2,1)S(1)} %pad_maximum_fusion.refs_0_), channel_id=1, source_target_pairs={{0,32},{1,33},{2,34},{3,35},{4,36},{5,37},{6,38},{7,39},{8,40},{9,... | collective-permute-start | bytes 1179656 | tf_op jit(solution)/shard_map/gather_tokens/ppermute | solution.py:675
  36.0 11.6 %collective-permute-start.4 = (bf16[4,64,768]{2,1,0:T(8,128)(2,1)S(1)}, bf16[4,64,768]{2,1,0:T(8,128)(2,1)S(1)}, u32[]{:S(2)}, u32[]{:S(2)}) collective-permute-start(bf16[4,64,768]{2,1,0:T(8,128)(2,1)S(1)} %pad_maximum_fusion.refs_0_), channel_id=1, source_target_pairs={{0,96},{1,97},{2,98},{3,99},{4,100},{5,101},{6,102},{7,103},{8,104... | collective-permute-start | bytes 1179656 | tf_op jit(solution)/shard_map/gather_tokens/ppermute | solution.py:675
  44.1 10.9 %copy-start.8 = (bf16[4,64,768]{2,1,0:T(8,128)(2,1)}, bf16[4,64,768]{2,1,0:T(8,128)(2,1)S(1)}, u32[]{:S(2)}) copy-start(bf16[4,64,768]{2,1,0:T(8,128)(2,1)S(1)} %collective-permute-done.10.refs_6_) | copy-start | bytes 1179652
  44.1 8.0 %collective-permute-start.12 = (bf16[2,64,768]{2,1,0:T(8,128)(2,1)S(1)}, bf16[2,64,768]{2,1,0:T(8,128)(2,1)S(1)}, u32[]{:S(2)}, u32[]{:S(2)}) collective-permute-start(bf16[2,64,768]{2,1,0:T(8,128)(2,1)S(1)} %slice.78), channel_id=1, source_target_pairs={{0,8},{1,9},{2,10},{3,11},{4,12},{5,13},{6,14},{7,15},{8,16},{9,17... | collective-permute-start | bytes 589832 | tf_op jit(solution)/shard_map/gather_tokens/ppermute | solution.py:675
  44.2 10.8 %copy-start.9 = (bf16[4,64,768]{2,1,0:T(8,128)(2,1)}, bf16[4,64,768]{2,1,0:T(8,128)(2,1)S(1)}, u32[]{:S(2)}) copy-start(bf16[4,64,768]{2,1,0:T(8,128)(2,1)S(1)} %collective-permute-done.11.refs_7_) | copy-start | bytes 1179652
  44.2 7.9 %collective-permute-start.13 = (bf16[2,64,768]{2,1,0:T(8,128)(2,1)S(1)}, bf16[2,64,768]{2,1,0:T(8,128)(2,1)S(1)}, u32[]{:S(2)}, u32[]{:S(2)}) collective-permute-start(bf16[2,64,768]{2,1,0:T(8,128)(2,1)S(1)} %slice.79), channel_id=1, source_target_pairs={{0,24},{1,25},{2,26},{3,27},{4,28},{5,29},{6,30},{7,31},{8,0},{9,1... | collective-permute-start | bytes 589832 | tf_op jit(solution)/shard_map/gather_tokens/ppermute | solution.py:675
  47.5 7.5 %copy-start.10 = (bf16[4,64,768]{2,1,0:T(8,128)(2,1)}, bf16[4,64,768]{2,1,0:T(8,128)(2,1)S(1)}, u32[]{:S(2)}) copy-start(bf16[4,64,768]{2,1,0:T(8,128)(2,1)S(1)} %collective-permute-done.3.refs_1_) | copy-start | bytes 1179652
  47.5 7.5 %collective-permute-start.5 = (bf16[2,64,768]{2,1,0:T(8,128)(2,1)S(1)}, bf16[2,64,768]{2,1,0:T(8,128)(2,1)S(1)}, u32[]{:S(2)}, u32[]{:S(2)}) collective-permute-start(bf16[2,64,768]{2,1,0:T(8,128)(2,1)S(1)} %slice.75), channel_id=1, source_target_pairs={{0,32},{1,33},{2,34},{3,35},{4,36},{5,37},{6,38},{7,39},{8,40},{9,... | collective-permute-start | bytes 589832 | tf_op jit(solution)/shard_map/gather_tokens/ppermute | solution.py:675
  47.6 7.4 %copy-start.11 = (bf16[4,64,768]{2,1,0:T(8,128)(2,1)}, bf16[4,64,768]{2,1,0:T(8,128)(2,1)S(1)}, u32[]{:S(2)}) copy-start(bf16[4,64,768]{2,1,0:T(8,128)(2,1)S(1)} %collective-permute-done.4.refs_2_) | copy-start | bytes 1179652
  47.6 7.3 %collective-permute-start.6 = (bf16[2,64,768]{2,1,0:T(8,128)(2,1)S(1)}, bf16[2,64,768]{2,1,0:T(8,128)(2,1)S(1)}, u32[]{:S(2)}, u32[]{:S(2)}) collective-permute-start(bf16[2,64,768]{2,1,0:T(8,128)(2,1)S(1)} %slice.76), channel_id=1, source_target_pairs={{0,96},{1,97},{2,98},{3,99},{4,100},{5,101},{6,102},{7,103},{8,104... | collective-permute-start | bytes 589832 | tf_op jit(solution)/shard_map/gather_tokens/ppermute | solution.py:675
  52.1 2.9 %copy-start.23 = (bf16[2,64,768]{2,1,0:T(8,128)(2,1)}, bf16[2,64,768]{2,1,0:T(8,128)(2,1)S(1)}, u32[]{:S(2)}) copy-start(bf16[2,64,768]{2,1,0:T(8,128)(2,1)S(1)} %collective-permute-done.12.refs_8_) | copy-start | bytes 589828
  52.1 2.9 %copy-start.24 = (bf16[2,64,768]{2,1,0:T(8,128)(2,1)}, bf16[2,64,768]{2,1,0:T(8,128)(2,1)S(1)}, u32[]{:S(2)}) copy-start(bf16[2,64,768]{2,1,0:T(8,128)(2,1)S(1)} %collective-permute-done.13.refs_9_) | copy-start | bytes 589828
  55.0 0.7 copy-start.25
  55.0 0.7 copy-start.26
  67.3 13.2 %all-to-all-start = ((bf16[16,64,128]{2,1,0:T(8,128)(2,1)}), bf16[16,64,128]{2,1,0:T(8,128)(2,1)S(1)}, u32[]{:S(2)}, u32[]{:S(2)}) async-start(bf16[16,64,128]{2,1,0:T(8,128)(2,1)} %get-tuple-element.58), calls=%async_computation | async-start | bytes 524288 | tf_op jit(solution)/shard_map/attention/all_to_all | solution.py:662
  71.9 85.9 %reduce-scatter.2.cloned.1.call-start = ((), (), s32[]{:S(2)}) async-start(), calls=%async_computation.8 | async-start | bytes 11943936 | tf_op jit(solution)/shard_map/feed_forward/reduce_scatter | solution.py:792
  80.5 0.7 copy-start.6
  95.4 1.0 copy-start.7
  121.8 24.6 %all-to-all-start.2 = ((bf16[16,64,384]{2,1,0:T(8,128)(2,1)}), bf16[16,64,384]{2,1,0:T(8,128)(2,1)S(1)}, u32[]{:S(2)}, u32[]{:S(2)}) async-start(bf16[16,64,384]{2,1,0:T(8,128)(2,1)} %get-tuple-element.73), calls=%async_computation.2 | async-start | bytes 1572864 | tf_op jit(solution)/shard_map/attention_back/all_to_all | solution.py:662
  125.5 69.4 %all-gather.4.cloned.1.call-start = ((), (), s32[]{:S(2)}) async-start(), calls=%async_computation.7 | async-start | bytes 3981312 | tf_op jit(solution)/shard_map/token_gradient/all_gather | solution.py:826
  131.1 1.5 collective-permute-start.18
  134.4 6.1 %collective-permute-start.19 = (bf16[104,192]{1,0:T(8,128)(2,1)S(1)}, bf16[104,192]{1,0:T(8,128)(2,1)S(1)}, u32[]{:S(2)}, u32[]{:S(2)}) collective-permute-start(bf16[104,192]{1,0:T(8,128)(2,1)S(1)} %get-tuple-element.103), channel_id=1, source_target_pairs={{0,2},{1,3},{2,4},{3,5},{4,6},{5,7},{6,0},{7,1},{8,10},{9,11},{10,... | collective-permute-start | bytes 119816 | tf_op jit(solution)/shard_map/early_grads/ppermute | solution.py:675
  136.1 5.3 %collective-permute-start.20 = (bf16[104,192]{1,0:T(8,128)(2,1)S(1)}, bf16[104,192]{1,0:T(8,128)(2,1)S(1)}, u32[]{:S(2)}, u32[]{:S(2)}) collective-permute-start(bf16[104,192]{1,0:T(8,128)(2,1)S(1)} %get-tuple-element.102), channel_id=1, source_target_pairs={{0,6},{1,7},{2,0},{3,1},{4,2},{5,3},{6,4},{7,5},{8,14},{9,15},{10,... | collective-permute-start | bytes 119816 | tf_op jit(solution)/shard_map/early_grads/ppermute | solution.py:675
  137.6 6.3 %collective-permute-start.21 = (bf16[104,192]{1,0:T(8,128)(2,1)S(1)}, bf16[104,192]{1,0:T(8,128)(2,1)S(1)}, u32[]{:S(2)}, u32[]{:S(2)}) collective-permute-start(bf16[104,192]{1,0:T(8,128)(2,1)S(1)} %get-tuple-element.101), channel_id=1, source_target_pairs={{0,4},{1,5},{2,6},{3,7},{4,0},{5,1},{6,2},{7,3},{8,12},{9,13},{10,... | collective-permute-start | bytes 119816 | tf_op jit(solution)/shard_map/early_grads/ppermute | solution.py:675
  140.5 3.4 %copy-start.12 = (bf16[104,192]{1,0:T(8,128)(2,1)}, bf16[104,192]{1,0:T(8,128)(2,1)S(1)}, u32[]{:S(2)}) copy-start(bf16[104,192]{1,0:T(8,128)(2,1)S(1)} %collective-permute-done.19.left) | copy-start | bytes 119812
  141.3 2.6 %copy-start.13 = (bf16[104,192]{1,0:T(8,128)(2,1)}, bf16[104,192]{1,0:T(8,128)(2,1)S(1)}, u32[]{:S(2)}) copy-start(bf16[104,192]{1,0:T(8,128)(2,1)S(1)} %collective-permute-done.20.right) | copy-start | bytes 119812
  143.9 0.6 copy-start.14
  146.4 12.8 %copy-start.2 = (bf16[16,64,384]{2,1,0:T(8,128)(2,1)}, bf16[16,64,384]{2,1,0:T(8,128)(2,1)S(1)}, u32[]{:S(2)}) copy-start(bf16[16,64,384]{2,1,0:T(8,128)(2,1)S(1)} %all-to-all-done.2.heads_grad) | copy-start | bytes 2359300
  146.5 20.2 %all-to-all-start.3 = ((bf16[16,32,768]{2,1,0:T(8,128)(2,1)}), bf16[16,32,768]{2,1,0:T(8,128)(2,1)S(1)}, u32[]{:S(2)}, u32[]{:S(2)}) async-start(bf16[16,32,768]{2,1,0:T(8,128)(2,1)} %early_grads.3), calls=%async_computation.4 | async-start | bytes 1572864 | tf_op jit(solution)/shard_map/early_grads/all_to_all | solution.py:662
  166.7 21.8 %copy-start.1 = (bf16[16,32,768]{2,1,0:T(8,128)(2,1)}, bf16[16,32,768]{2,1,0:T(8,128)(2,1)S(1)}, u32[]{:S(2)}) copy-start(bf16[16,32,768]{2,1,0:T(8,128)(2,1)S(1)} %all-to-all-done.3.pieces) | copy-start | bytes 2359300
  191.2 22.1 %all-to-all-start.5 = ((bf16[16,54,768]{2,1,0:T(8,128)(2,1)}), bf16[16,54,768]{2,1,0:T(8,128)(2,1)S(1)}, u32[]{:S(2)}, u32[]{:S(2)}) async-start(bf16[16,54,768]{2,1,0:T(8,128)(2,1)} %sum_over_ctx.3), calls=%async_computation.6 | async-start | bytes 2752512 | tf_op jit(solution)/shard_map/sum_over_ctx/all_to_all | solution.py:662
  213.3 1.1 copy-start
Sparse Core Ops, SparseCore 0:
  11.8 61.5 all-gather.5
  95.5 62.1 reduce-scatter.1
  159.5 29.1 all-gather.3

commit v6 on v5

--- a/solution.py
+++ b/solution.py
@@ -20,7 +20,7 @@
 EPSILON = 1e-05
 SCALE_LOG2 = DEPTH ** -0.5 * 1.4426950408889634
 NEGATIVE = -1e30
-VMEM_LIMIT = 56 * 1024 * 1024
+MIB = 1024 * 1024
 
 BF = jnp.bfloat16
 F32 = jnp.float32
@@ -90,7 +90,8 @@
 
 
 def vmem_call(
-    kernel, out_shape, scratch, flops, in_vmem, smem=0, transcendentals=0, far_outs=()
+    kernel, out_shape, scratch, flops, in_vmem, smem=0, transcendentals=0, far_outs=(),
+    limit=16,
 ):
     specs = [pl.BlockSpec(memory_space=pltpu.VMEM)] * in_vmem
     specs = [pl.BlockSpec(memory_space=pltpu.SMEM)] * smem + specs
@@ -103,7 +104,7 @@
             for index in range(len(out_shape))
         ],
         scratch_shapes=scratch,
-        compiler_params=pltpu.CompilerParams(vmem_limit_bytes=VMEM_LIMIT),
+        compiler_params=pltpu.CompilerParams(vmem_limit_bytes=limit * MIB),
         cost_estimate=pl.CostEstimate(
             flops=flops, bytes_accessed=8 * 2**20, transcendentals=transcendentals
         ),
@@ -120,7 +121,7 @@
         pack[DOWN_AT:PACK_ROWS, :] = down_weight[...]
 
     return vmem_call(
-        kernel, [jax.ShapeDtypeStruct((PACK_ROWS, WIDTH), BF)], [], 10**6, 3
+        kernel, [jax.ShapeDtypeStruct((PACK_ROWS, WIDTH), BF)], [], 10**6, 3, limit=56
     )(out_weight, up_weight, down_weight)[0]
 
 
@@ -129,7 +130,7 @@
         hat[...] = normalise(tokens[...].astype(F32))[0].astype(BF)
 
     return vmem_call(
-        kernel, [jax.ShapeDtypeStruct((ROWS, WIDTH), BF)], [], 10**6, 1
+        kernel, [jax.ShapeDtypeStruct((ROWS, WIDTH), BF)], [], 10**6, 1, limit=56
     )(tokens)[0]
 
 
@@ -267,6 +268,7 @@
         smem=2,
         transcendentals=3 * 10**6,
         far_outs=(1,),
+        limit=56,
     )(order, where, *[block for _, _, block in blocks], weight, bias, gain, shift)
 
 
@@ -375,6 +377,7 @@
         8,
         smem=1,
         transcendentals=3 * 10**6,
+        limit=56,
     )(order, upstream, query, key, value, query_t, key_t, out_t, lse)
 
 
@@ -508,7 +511,7 @@
             pltpu.VMEM((FSDP, PACK_ROWS, WIDTH), BF),
             pltpu.SemaphoreType.DMA((9,)),
         ],
-        compiler_params=pltpu.CompilerParams(vmem_limit_bytes=VMEM_LIMIT),
+        compiler_params=pltpu.CompilerParams(vmem_limit_bytes=56 * MIB),
         cost_estimate=pl.CostEstimate(
             flops=4 * 10**9, bytes_accessed=24 * 2**20, transcendentals=4 * 10**5
         ),

time: 225 us -> 224 us (level); the launches traced: 224 us -> 219 us
  Pallas kernels: 62.5 us -> 52.2 us
  waiting for transfers between devices: 41 us -> 44.3 us
  other arithmetic: 4.68 us -> 1.91 us
  blocking collectives: 33.8 us -> 36.5 us
    reduce_scatter x1, waiting for transfers between devices: 4.08 us -> 9.11 us  [local(): lax.psum_scatter(mix_grad, 'fsdp', scatter_dimension=0, tiled=False)]
    pallas_call x1, Pallas kernels: 4.46 us -> 1.31 us  [early_slots(): vmem_call(kernel, [jax.ShapeDtypeStruct((FSDP, 104, 3 * DEPTH), BF)], [],...]
    all_to_all x2, blocking collectives: 33.8 us -> 36.5 us  [swap(): return lax.all_to_all(slots, axes, 0, 0, tiled=True)]
    pallas_call x1, Pallas kernels: 4.62 us -> 2.22 us  [token_gradient(): vmem_call(kernel, [jax.ShapeDtypeStruct((ROWS, WIDTH), F32)], [], 2 * ROW...]
    unnamed x60 -> x70, local copies, waits for them, and re-layouts: 5.29 us -> 7.56 us
  transfers between devices with their start and end apart: 29 -> 29, of which waited for: 13 -> 13; matrix products, arithmetic and copies ran while one was open for 6% -> 5% of each run, Pallas kernels for 18% -> 15%
where the time goes in v6:
time: 224 us; the launch traced here: 219 us
  starting transfers between devices  53.5 us (24%)
  Pallas kernels  52.2 us (23%)
  waiting for transfers between devices  44.3 us (20%)
  blocking collectives  36.5 us (16%)
  local copies, waits for them, and re-layouts  16.2 us (7%)
  between operations  14.6 us (7%)
    all_to_all x2, blocking collectives, swap(): return lax.all_to_all(slots, axes, 0, 0, tiled=True)  36.5 us
    ppermute x22, starting transfers between devices, shift_by(): return lax.ppermute(value, ('ctx', 'fsdp'), pairs)  33.8 us
    all_to_all x4, waiting for transfers between devices, swap(): return lax.all_to_all(slots, axes, 0, 0, tiled=True)  21.1 us
    all_to_all x4, starting transfers between devices, swap(): return lax.all_to_all(slots, axes, 0, 0, tiled=True)  19.3 us
    pallas_call x1, Pallas kernels, feed_forward(): pl.pallas_call(kernel, out_shape=outs, in_specs=[pl.BlockSpec(memory_spac...  14.1 us
    ppermute x22, waiting for transfers between devices, shift_by(): return lax.ppermute(value, ('ctx', 'fsdp'), pairs)  14 us
    pallas_call x1, Pallas kernels, head_backward(): vmem_call(kernel, [shape((CTX, HALF, 6 * DEPTH), BF), shape((SEQ, 3 * DEP...  13.5 us
    pallas_call x1, Pallas kernels, head_forward(): vmem_call(kernel, [shape((CTX, HALF, 2 * DEPTH), BF), shape((SEQ, WIDTH),...  11.6 us
  transfers between devices with their start and end apart: 29, of which 13 were waited for; matrix products, arithmetic and copies ran while one was open for 5% of the time, Pallas kernels for 15%

profile of v6, /device:TPU:0, one launch (start us, length us, event | category | flops | bytes accessed | tf_op | source)
XLA Modules:
  0.0 219.1 jit_solution(12816175888709340311)
XLA Ops:
  7.2 1.8 gather_tokens.1
  9.1 2.5 %gather_weights.1 = bf16[864,768]{1,0:T(8,128)(2,1)} custom-call(bf16[96,768]{1,0:T(8,128)(2,1)} %out_weight, bf16[96,3072]{1,0:T(8,128)(2,1)} %up_weight, bf16[384,768]{1,0:T(8,128)(2,1)} %down_weight), custom_call_target="tpu_custom_call" | custom-call | flops 1000000 | bytes 8388608 | tf_op jit(solution)/shard_map/gather_weights/pallas_call | solution.py:123
  11.7 0.9 constant_dynamic-slice_fusion.4
  13.5 3.2 %collective-permute-start.14 = (bf16[112,192]{0,1:T(8,128)(2,1)S(1)}, bf16[112,192]{0,1:T(8,128)(2,1)S(1)}, u32[]{:S(2)}, u32[]{:S(2)}) collective-permute-start(bf16[112,192]{0,1:T(8,128)(2,1)S(1)} %maximum_maximum_fusion), channel_id=1, source_target_pairs={{0,6},{1,7},{2,0},{3,1},{4,2},{5,3},{6,4},{7,5},{8,14},{9,15},{10,... | collective-permute-start | bytes 129032 | tf_op jit(solution)/shard_map/gather_small/ppermute | solution.py:678
  16.7 0.6 collective-permute-start.15
  17.3 1.0 collective-permute-start.16
  18.3 4.0 %collective-permute-start.9 = (bf16[64,768]{1,0:T(8,128)(2,1)S(1)}, bf16[64,768]{1,0:T(8,128)(2,1)S(1)}, u32[]{:S(2)}, u32[]{:S(2)}) collective-permute-start(bf16[64,768]{1,0:T(8,128)(2,1)S(1)} %get-tuple-element.107), channel_id=1, source_target_pairs={{0,64},{1,65},{2,66},{3,67},{4,68},{5,69},{6,70},{7,71},{8,72},{9,... | collective-permute-start | bytes 294920 | tf_op jit(solution)/shard_map/gather_tokens/ppermute | solution.py:678
  22.3 1.0 collective-permute-start.7
  23.5 2.2 %collective-permute-start.8 = (bf16[64,768]{1,0:T(8,128)(2,1)S(1)}, bf16[64,768]{1,0:T(8,128)(2,1)S(1)}, u32[]{:S(2)}, u32[]{:S(2)}) collective-permute-start(bf16[64,768]{1,0:T(8,128)(2,1)S(1)} %get-tuple-element.107), channel_id=1, source_target_pairs={{0,96},{1,97},{2,98},{3,99},{4,100},{5,101},{6,102},{7,103},{8,104... | collective-permute-start | bytes 294920 | tf_op jit(solution)/shard_map/gather_tokens/ppermute | solution.py:678
  25.8 1.5 collective-permute-start
  27.3 1.7 collective-permute-start.1
  29.1 1.9 collective-permute-start.2
  31.0 0.7 collective-permute-start.10
  31.7 0.9 collective-permute-done
  32.6 1.7 collective-permute-start.11
  34.4 1.5 collective-permute-done.2
  36.0 3.2 %collective-permute-start.4 = (bf16[4,64,768]{2,1,0:T(8,128)(2,1)S(1)}, bf16[4,64,768]{2,1,0:T(8,128)(2,1)S(1)}, u32[]{:S(2)}, u32[]{:S(2)}) collective-permute-start(bf16[4,64,768]{2,1,0:T(8,128)(2,1)S(1)} %pad_maximum_fusion.refs_0_), channel_id=1, source_target_pairs={{0,96},{1,97},{2,98},{3,99},{4,100},{5,101},{6,102},{7,103},{8,104... | collective-permute-start | bytes 1179656 | tf_op jit(solution)/shard_map/gather_tokens/ppermute | solution.py:678
  40.3 0.7 reshape.105.refs_12_.gain
  40.9 0.7 reshape.106.refs_13_.shift
  41.6 1.0 copy.53
  42.7 1.4 collective-permute-done.10.refs_6_
  44.2 3.3 %collective-permute-start.13 = (bf16[2,64,768]{2,1,0:T(8,128)(2,1)S(1)}, bf16[2,64,768]{2,1,0:T(8,128)(2,1)S(1)}, u32[]{:S(2)}, u32[]{:S(2)}) collective-permute-start(bf16[2,64,768]{2,1,0:T(8,128)(2,1)S(1)} %slice.79), channel_id=1, source_target_pairs={{0,24},{1,25},{2,26},{3,27},{4,28},{5,29},{6,30},{7,31},{8,0},{9,1... | collective-permute-start | bytes 589832 | tf_op jit(solution)/shard_map/gather_tokens/ppermute | solution.py:678
  47.6 3.5 %collective-permute-start.6 = (bf16[2,64,768]{2,1,0:T(8,128)(2,1)S(1)}, bf16[2,64,768]{2,1,0:T(8,128)(2,1)S(1)}, u32[]{:S(2)}, u32[]{:S(2)}) collective-permute-start(bf16[2,64,768]{2,1,0:T(8,128)(2,1)S(1)} %slice.76), channel_id=1, source_target_pairs={{0,96},{1,97},{2,98},{3,99},{4,100},{5,101},{6,102},{7,103},{8,104... | collective-permute-start | bytes 589832 | tf_op jit(solution)/shard_map/gather_tokens/ppermute | solution.py:678
  51.1 0.6 pad_maximum_fusion.3.refs_11_
  51.6 0.5 collective-permute-done.12.refs_8_
  52.1 2.9 %collective-permute-done.5.refs_3_ = bf16[2,64,768]{2,1,0:T(8,128)(2,1)S(1)} collective-permute-done((bf16[2,64,768]{2,1,0:T(8,128)(2,1)S(1)}, bf16[2,64,768]{2,1,0:T(8,128)(2,1)S(1)}, u32[]{:S(2)}, u32[]{:S(2)}) %collective-permute-start.5) | collective-permute-done | bytes 196640 | tf_op jit(solution)/shard_map/gather_tokens/ppermute | solution.py:678
  55.0 0.6 copy-done.30
  55.7 11.6 %attention.1 = (bf16[16,64,128]{2,1,0:T(8,128)(2,1)}, bf16[2048,768]{1,0:T(8,128)(2,1)}, bf16[2048,64]{1,0:T(8,128)(2,1)}, bf16[2048,64]{1,0:T(8,128)(2,1)}, bf1...) custom-call(s32[16]{0:T(128)} %order.3, ...), custom_call_target="tpu_custom_call" | custom-call | flops 2000000000 | bytes 8388608 | tf_op jit(solution)/shard_map/attention/pallas_call | solution.py:247
  67.3 4.5 %all-to-all-start = ((bf16[16,64,128]{2,1,0:T(8,128)(2,1)}), bf16[16,64,128]{2,1,0:T(8,128)(2,1)S(1)}, u32[]{:S(2)}, u32[]{:S(2)}) async-start(bf16[16,64,128]{2,1,0:T(8,128)(2,1)} %get-tuple-element.58), calls=%async_computation | async-start | bytes 524288 | tf_op jit(solution)/shard_map/attention/all_to_all | solution.py:665
  72.1 0.7 reshape.107.out_bias
  72.8 0.7 reshape.108.gain
  73.4 0.7 reshape.109.shift
  74.1 0.7 reshape.111.down_bias
  74.8 0.6 copy.64
  75.5 5.1 %all-to-all-done.heads_out = bf16[16,64,128]{2,1,0:T(8,128)(2,1)S(1)} async-done(((bf16[16,64,128]{2,1,0:T(8,128)(2,1)}), bf16[16,64,128]{2,1,0:T(8,128)(2,1)S(1)}, u32[]{:S(2)}, u32[]{:S(2)}) %all-to-all-start) | async-done | bytes 262176 | tf_op jit(solution)/shard_map/attention/all_to_all | solution.py:665
  80.5 0.7 copy-done.14
  81.2 14.1 %feed_forward.1 = (bf16[128,768]{1,0:T(8,128)(2,1)}, bf16[8,864,768]{2,1,0:T(8,128)(2,1)}, bf16[16,64,128]{2,1,0:T(8,128)(2,1)}, f32[128,768]{1,0:T(8,128)}, f32[4,768]{1,0:T(4,128)}, /*index=5*/f32[1,3072]{1,0:T(1,128)}) custom-call(bf16[8,864,768]{2,1,0:T(8,128)(2,1)} %bitcast.92, bf16[128,768]{1,0:T(8,128)(2,1)} %bitcast.73, ...), custom_call_target="tpu_custom_call" | custom-call | flops 4000000000 | bytes 25165824 | tf_op jit(solution)/shard_map/feed_forward/pallas_call | solution.py:499
  95.3 0.9 copy-done.15
  96.3 11.9 %all_to_all.30.upstream = bf16[16,64,128]{2,1,0:T(8,128)(2,1)} all-to-all(bf16[16,64,128]{2,1,0:T(8,128)(2,1)S(1)} %copy-done.15), channel_id=1, replica_groups=mesh['ctx'=16,'fsdp'=8] {'ctx'}, dimensions={0} | all-to-all | bytes 524288 | tf_op jit(solution)/shard_map/feed_forward/all_to_all | solution.py:665
  108.2 13.5 %attention_back.1 = (bf16[16,64,384]{2,1,0:T(8,128)(2,1)}, bf16[2048,192]{1,0:T(8,128)(2,1)}, f32[1,192]{1,0:T(1,128)}) custom-call(s32[16]{0:T(128)} %order.3, bf16[16,64,128]{2,1,0:T(8,128)(2,1)} %all_to_all.30.upstream, bf16[2048,64]{1,0:T(8,128)(2,1)} %get-tuple-element.62.query, bf16[2048,64]{1,0:T(8,128)(2,1)} %get-tuple-element.63.key, ...), custom_call_target="tpu_custom_call" | custom-call | flops 4000000000 | bytes 8388608 | tf_op jit(solution)/shard_map/attention_back/pallas_call | solution.py:360
  121.8 3.8 %all-to-all-start.2 = ((bf16[16,64,384]{2,1,0:T(8,128)(2,1)}), bf16[16,64,384]{2,1,0:T(8,128)(2,1)S(1)}, u32[]{:S(2)}, u32[]{:S(2)}) async-start(bf16[16,64,384]{2,1,0:T(8,128)(2,1)} %get-tuple-element.73), calls=%async_computation.2 | async-start | bytes 1572864 | tf_op jit(solution)/shard_map/attention_back/all_to_all | solution.py:665
  125.7 2.0 copy-done.1
  127.7 1.3 early_grads.2
  129.2 1.4 collective-permute-done.18
  130.7 1.8 collective-permute-start.19
  132.5 1.5 collective-permute-start.20
  134.0 0.8 collective-permute-start.21
  134.8 2.0 collective-permute-done.19.left
  136.8 0.9 collective-permute-done.20.right
  137.7 2.6 %collective-permute-done.21.far = bf16[104,192]{1,0:T(8,128)(2,1)S(1)} collective-permute-done((bf16[104,192]{1,0:T(8,128)(2,1)S(1)}, bf16[104,192]{1,0:T(8,128)(2,1)S(1)}, u32[]{:S(2)}, u32[]{:S(2)}) %collective-permute-start.21) | collective-permute-done | bytes 39968 | tf_op jit(solution)/shard_map/early_grads/ppermute | solution.py:678
  140.3 1.0 early_grads.3
  141.3 7.2 %all-to-all-start.3 = ((bf16[16,32,768]{2,1,0:T(8,128)(2,1)}), bf16[16,32,768]{2,1,0:T(8,128)(2,1)S(1)}, u32[]{:S(2)}, u32[]{:S(2)}) async-start(bf16[16,32,768]{2,1,0:T(8,128)(2,1)} %early_grads.3), calls=%async_computation.4 | async-start | bytes 1572864 | tf_op jit(solution)/shard_map/early_grads/all_to_all | solution.py:665
  148.5 9.1 %reduce-scatter.2.cloned.1.call-done = bf16[1,864,768]{2,1,0:T(8,128)(2,1)} async-done(((bf16[8,864,768]{2,1,0:T(8,128)(2,1)}), bf16[1,864,768]{2,1,0:T(8,128)(2,1)}) %reduce-scatter.2.cloned.1.call-update) | async-done | bytes 1327120 | tf_op jit(solution)/shard_map/feed_forward/reduce_scatter | solution.py:795
  157.6 1.5 reduce_scatter.11
  159.1 2.4 %all-to-all-done.3.pieces = bf16[16,32,768]{2,1,0:T(8,128)(2,1)S(1)} async-done(((bf16[16,32,768]{2,1,0:T(8,128)(2,1)}), bf16[16,32,768]{2,1,0:T(8,128)(2,1)S(1)}, u32[]{:S(2)}, u32[]{:S(2)}) %all-to-all-start.3) | async-done | bytes 786464 | tf_op jit(solution)/shard_map/early_grads/all_to_all | solution.py:665
  161.5 24.5 %all_to_all.31.parts = bf16[16,54,768]{2,1,0:T(8,128)(2,1)S(1)} all-to-all(bf16[16,54,768]{2,1,0:T(8,128)(2,1)S(1)} %reduce_scatter.11), channel_id=1, replica_groups=mesh['ctx'=16,'fsdp'=8] {'ctx'}, dimensions={0} | all-to-all | bytes 2654208 | tf_op jit(solution)/shard_map/sum_over_ctx/all_to_all | solution.py:665
  186.1 1.3 sum_over_ctx.3
  187.4 3.8 %all-to-all-start.5 = ((bf16[16,54,768]{2,1,0:T(8,128)(2,1)}), bf16[16,54,768]{2,1,0:T(8,128)(2,1)S(1)}, u32[]{:S(2)}, u32[]{:S(2)}) async-start(bf16[16,54,768]{2,1,0:T(8,128)(2,1)} %sum_over_ctx.3), calls=%async_computation.6 | async-start | bytes 2752512 | tf_op jit(solution)/shard_map/sum_over_ctx/all_to_all | solution.py:665
  191.3 2.0 copy-done
  193.3 2.2 %token_gradient.1 = f32[128,768]{1,0:T(8,128)} custom-call(bf16[768,2304]{1,0:T(8,128)(2,1)S(1)} %copy-done, bf16[128,768]{1,0:T(8,128)(2,1)S(1)} %bitcast.74, bf16[16,64,384]{2,1,0:T(8,128)(2,1)S(1)} %all-to-all-done.2.heads_grad, f32[1,768]{1,0:T(1,128)S(1)} %copy-done.6, f32[128,768]{1,0:T(8,128)S(1)} %copy-done.5), custom_call_target="tpu_custom_call" | custom-call | flops 452984832 | bytes 8388608 | tf_op jit(solution)/shard_map/token_gradient/pallas_call | solution.py:530
  195.5 1.2 sum_over_ctx.4
  196.8 0.6 reduce
  197.3 13.6 %all-to-all-done.5.pieces = bf16[16,54,768]{2,1,0:T(8,128)(2,1)S(1)} async-done(((bf16[16,54,768]{2,1,0:T(8,128)(2,1)}), bf16[16,54,768]{2,1,0:T(8,128)(2,1)S(1)}, u32[]{:S(2)}, u32[]{:S(2)}) %all-to-all-start.5) | async-done | bytes 1327136 | tf_op jit(solution)/shard_map/sum_over_ctx/all_to_all | solution.py:665
  211.0 1.6 sum_over_ctx.5
  (120 shorter events, 3.4 us)
Async XLA Ops:
  7.2 73.3 %all-gather.6.cloned.1.call-start = ((), (), s32[]{:S(2)}) async-start(), calls=%async_computation.9 | async-start | bytes 11943936 | tf_op jit(solution)/shard_map/gather_weights/all_gather | solution.py:755
  11.5 1.4 copy-start.20
  11.5 1.4 copy-start.21
  11.5 1.4 copy-start.22
  11.5 1.4 copy-start.23
  11.6 1.4 copy-start.24
  11.6 1.4 copy-start.25
  11.6 1.4 copy-start.26
  11.6 1.4 copy-start.27
  11.6 6.7 %copy-start.11 = (bf16[128,768]{1,0:T(8,128)(2,1)S(1)}, bf16[128,768]{1,0:T(8,128)(2,1)}, u32[]{:S(2)}) copy-start(bf16[128,768]{1,0:T(8,128)(2,1)} %gather_tokens.1) | copy-start | bytes 589828
  13.5 10.0 %collective-permute-start.14 = (bf16[112,192]{0,1:T(8,128)(2,1)S(1)}, bf16[112,192]{0,1:T(8,128)(2,1)S(1)}, u32[]{:S(2)}, u32[]{:S(2)}) collective-permute-start(bf16[112,192]{0,1:T(8,128)(2,1)S(1)} %maximum_maximum_fusion), channel_id=1, source_target_pairs={{0,6},{1,7},{2,0},{3,1},{4,2},{5,3},{6,4},{7,5},{8,14},{9,15},{10,... | collective-permute-start | bytes 129032 | tf_op jit(solution)/shard_map/gather_small/ppermute | solution.py:678
  16.7 9.1 %collective-permute-start.15 = (bf16[112,192]{0,1:T(8,128)(2,1)S(1)}, bf16[112,192]{0,1:T(8,128)(2,1)S(1)}, u32[]{:S(2)}, u32[]{:S(2)}) collective-permute-start(bf16[112,192]{0,1:T(8,128)(2,1)S(1)} %maximum_maximum_fusion), channel_id=1, source_target_pairs={{0,4},{1,5},{2,6},{3,7},{4,0},{5,1},{6,2},{7,3},{8,12},{9,13},{10,... | collective-permute-start | bytes 129032 | tf_op jit(solution)/shard_map/gather_small/ppermute | solution.py:678
  17.3 9.9 %collective-permute-start.16 = (bf16[112,192]{0,1:T(8,128)(2,1)S(1)}, bf16[112,192]{0,1:T(8,128)(2,1)S(1)}, u32[]{:S(2)}, u32[]{:S(2)}) collective-permute-start(bf16[112,192]{0,1:T(8,128)(2,1)S(1)} %maximum_maximum_fusion), channel_id=1, source_target_pairs={{0,2},{1,3},{2,4},{3,5},{4,6},{5,7},{6,0},{7,1},{8,10},{9,11},{10,... | collective-permute-start | bytes 129032 | tf_op jit(solution)/shard_map/gather_small/ppermute | solution.py:678
  18.3 10.7 %collective-permute-start.9 = (bf16[64,768]{1,0:T(8,128)(2,1)S(1)}, bf16[64,768]{1,0:T(8,128)(2,1)S(1)}, u32[]{:S(2)}, u32[]{:S(2)}) collective-permute-start(bf16[64,768]{1,0:T(8,128)(2,1)S(1)} %get-tuple-element.107), channel_id=1, source_target_pairs={{0,64},{1,65},{2,66},{3,67},{4,68},{5,69},{6,70},{7,71},{8,72},{9,... | collective-permute-start | bytes 294920 | tf_op jit(solution)/shard_map/gather_tokens/ppermute | solution.py:678
  22.3 8.7 %collective-permute-start.7 = (bf16[64,768]{1,0:T(8,128)(2,1)S(1)}, bf16[64,768]{1,0:T(8,128)(2,1)S(1)}, u32[]{:S(2)}, u32[]{:S(2)}) collective-permute-start(bf16[64,768]{1,0:T(8,128)(2,1)S(1)} %get-tuple-element.107), channel_id=1, source_target_pairs={{0,32},{1,33},{2,34},{3,35},{4,36},{5,37},{6,38},{7,39},{8,40},{9,... | collective-permute-start | bytes 294920 | tf_op jit(solution)/shard_map/gather_tokens/ppermute | solution.py:678
  23.5 7.4 %collective-permute-start.8 = (bf16[64,768]{1,0:T(8,128)(2,1)S(1)}, bf16[64,768]{1,0:T(8,128)(2,1)S(1)}, u32[]{:S(2)}, u32[]{:S(2)}) collective-permute-start(bf16[64,768]{1,0:T(8,128)(2,1)S(1)} %get-tuple-element.107), channel_id=1, source_target_pairs={{0,96},{1,97},{2,98},{3,99},{4,100},{5,101},{6,102},{7,103},{8,104... | collective-permute-start | bytes 294920 | tf_op jit(solution)/shard_map/gather_tokens/ppermute | solution.py:678
  25.8 6.9 %collective-permute-start = (bf16[64,768]{1,0:T(8,128)(2,1)S(1)}, bf16[64,768]{1,0:T(8,128)(2,1)S(1)}, u32[]{:S(2)}, u32[]{:S(2)}) collective-permute-start(bf16[64,768]{1,0:T(8,128)(2,1)S(1)} %get-tuple-element.108), channel_id=1, source_target_pairs={{0,8},{1,9},{2,10},{3,11},{4,12},{5,13},{6,14},{7,15},{8,16},{9,17... | collective-permute-start | bytes 294920 | tf_op jit(solution)/shard_map/gather_tokens/ppermute | solution.py:678
  27.3 7.1 %collective-permute-start.1 = (bf16[64,768]{1,0:T(8,128)(2,1)S(1)}, bf16[64,768]{1,0:T(8,128)(2,1)S(1)}, u32[]{:S(2)}, u32[]{:S(2)}) collective-permute-start(bf16[64,768]{1,0:T(8,128)(2,1)S(1)} %get-tuple-element.108), channel_id=1, source_target_pairs={{0,24},{1,25},{2,26},{3,27},{4,28},{5,29},{6,30},{7,31},{8,0},{9,1... | collective-permute-start | bytes 294920 | tf_op jit(solution)/shard_map/gather_tokens/ppermute | solution.py:678
  29.1 6.7 %collective-permute-start.2 = (bf16[64,768]{1,0:T(8,128)(2,1)S(1)}, bf16[64,768]{1,0:T(8,128)(2,1)S(1)}, u32[]{:S(2)}, u32[]{:S(2)}) collective-permute-start(bf16[64,768]{1,0:T(8,128)(2,1)S(1)} %get-tuple-element.108), channel_id=1, source_target_pairs={{0,16},{1,17},{2,18},{3,19},{4,20},{5,21},{6,22},{7,23},{8,24},{9,... | collective-permute-start | bytes 294920 | tf_op jit(solution)/shard_map/gather_tokens/ppermute | solution.py:678
  31.0 8.2 %collective-permute-start.17 = (bf16[4,112,192]{1,2,0:T(8,128)(2,1)S(1)}, bf16[4,112,192]{1,2,0:T(8,128)(2,1)S(1)}, u32[]{:S(2)}, u32[]{:S(2)}) collective-permute-start(bf16[4,112,192]{1,2,0:T(8,128)(2,1)S(1)} %pad_maximum_fusion.2), channel_id=1, source_target_pairs={{0,1},{1,0},{2,3},{3,2},{4,5},{5,4},{6,7},{7,6},{8,9},{9,8},{10,11... | collective-permute-start | bytes 516104 | tf_op jit(solution)/shard_map/gather_small/ppermute | solution.py:678
  31.0 8.6 %copy-start.12 = (bf16[4,64,768]{2,1,0:T(8,128)(2,1)}, bf16[4,64,768]{2,1,0:T(8,128)(2,1)S(1)}, u32[]{:S(2)}) copy-start(bf16[4,64,768]{2,1,0:T(8,128)(2,1)S(1)} %pad_maximum_fusion.1.refs_5_) | copy-start | bytes 1179652
  31.0 13.0 %collective-permute-start.10 = (bf16[4,64,768]{2,1,0:T(8,128)(2,1)S(1)}, bf16[4,64,768]{2,1,0:T(8,128)(2,1)S(1)}, u32[]{:S(2)}, u32[]{:S(2)}) collective-permute-start(bf16[4,64,768]{2,1,0:T(8,128)(2,1)S(1)} %pad_maximum_fusion.1.refs_5_), channel_id=1, source_target_pairs={{0,8},{1,9},{2,10},{3,11},{4,12},{5,13},{6,14},{7,15},{8,16},{9,17... | collective-permute-start | bytes 1179656 | tf_op jit(solution)/shard_map/gather_tokens/ppermute | solution.py:678
  32.6 11.5 %collective-permute-start.11 = (bf16[4,64,768]{2,1,0:T(8,128)(2,1)S(1)}, bf16[4,64,768]{2,1,0:T(8,128)(2,1)S(1)}, u32[]{:S(2)}, u32[]{:S(2)}) collective-permute-start(bf16[4,64,768]{2,1,0:T(8,128)(2,1)S(1)} %pad_maximum_fusion.1.refs_5_), channel_id=1, source_target_pairs={{0,24},{1,25},{2,26},{3,27},{4,28},{5,29},{6,30},{7,31},{8,0},{9,1... | collective-permute-start | bytes 1179656 | tf_op jit(solution)/shard_map/gather_tokens/ppermute | solution.py:678
  35.9 4.0 %copy-start.13 = (bf16[4,64,768]{2,1,0:T(8,128)(2,1)}, bf16[4,64,768]{2,1,0:T(8,128)(2,1)S(1)}, u32[]{:S(2)}) copy-start(bf16[4,64,768]{2,1,0:T(8,128)(2,1)S(1)} %pad_maximum_fusion.refs_0_) | copy-start | bytes 1179652
  35.9 11.6 %collective-permute-start.3 = (bf16[4,64,768]{2,1,0:T(8,128)(2,1)S(1)}, bf16[4,64,768]{2,1,0:T(8,128)(2,1)S(1)}, u32[]{:S(2)}, u32[]{:S(2)}) collective-permute-start(bf16[4,64,768]{2,1,0:T(8,128)(2,1)S(1)} %pad_maximum_fusion.refs_0_), channel_id=1, source_target_pairs={{0,32},{1,33},{2,34},{3,35},{4,36},{5,37},{6,38},{7,39},{8,40},{9,... | collective-permute-start | bytes 1179656 | tf_op jit(solution)/shard_map/gather_tokens/ppermute | solution.py:678
  36.0 11.6 %collective-permute-start.4 = (bf16[4,64,768]{2,1,0:T(8,128)(2,1)S(1)}, bf16[4,64,768]{2,1,0:T(8,128)(2,1)S(1)}, u32[]{:S(2)}, u32[]{:S(2)}) collective-permute-start(bf16[4,64,768]{2,1,0:T(8,128)(2,1)S(1)} %pad_maximum_fusion.refs_0_), channel_id=1, source_target_pairs={{0,96},{1,97},{2,98},{3,99},{4,100},{5,101},{6,102},{7,103},{8,104... | collective-permute-start | bytes 1179656 | tf_op jit(solution)/shard_map/gather_tokens/ppermute | solution.py:678
  44.0 10.9 %copy-start.16 = (bf16[4,64,768]{2,1,0:T(8,128)(2,1)}, bf16[4,64,768]{2,1,0:T(8,128)(2,1)S(1)}, u32[]{:S(2)}) copy-start(bf16[4,64,768]{2,1,0:T(8,128)(2,1)S(1)} %collective-permute-done.10.refs_6_) | copy-start | bytes 1179652
  44.1 8.0 %collective-permute-start.12 = (bf16[2,64,768]{2,1,0:T(8,128)(2,1)S(1)}, bf16[2,64,768]{2,1,0:T(8,128)(2,1)S(1)}, u32[]{:S(2)}, u32[]{:S(2)}) collective-permute-start(bf16[2,64,768]{2,1,0:T(8,128)(2,1)S(1)} %slice.78), channel_id=1, source_target_pairs={{0,8},{1,9},{2,10},{3,11},{4,12},{5,13},{6,14},{7,15},{8,16},{9,17... | collective-permute-start | bytes 589832 | tf_op jit(solution)/shard_map/gather_tokens/ppermute | solution.py:678
  44.2 10.8 %copy-start.17 = (bf16[4,64,768]{2,1,0:T(8,128)(2,1)}, bf16[4,64,768]{2,1,0:T(8,128)(2,1)S(1)}, u32[]{:S(2)}) copy-start(bf16[4,64,768]{2,1,0:T(8,128)(2,1)S(1)} %collective-permute-done.11.refs_7_) | copy-start | bytes 1179652
  44.2 7.9 %collective-permute-start.13 = (bf16[2,64,768]{2,1,0:T(8,128)(2,1)S(1)}, bf16[2,64,768]{2,1,0:T(8,128)(2,1)S(1)}, u32[]{:S(2)}, u32[]{:S(2)}) collective-permute-start(bf16[2,64,768]{2,1,0:T(8,128)(2,1)S(1)} %slice.79), channel_id=1, source_target_pairs={{0,24},{1,25},{2,26},{3,27},{4,28},{5,29},{6,30},{7,31},{8,0},{9,1... | collective-permute-start | bytes 589832 | tf_op jit(solution)/shard_map/gather_tokens/ppermute | solution.py:678
  47.5 7.5 %copy-start.18 = (bf16[4,64,768]{2,1,0:T(8,128)(2,1)}, bf16[4,64,768]{2,1,0:T(8,128)(2,1)S(1)}, u32[]{:S(2)}) copy-start(bf16[4,64,768]{2,1,0:T(8,128)(2,1)S(1)} %collective-permute-done.3.refs_1_) | copy-start | bytes 1179652
  47.5 7.5 %collective-permute-start.5 = (bf16[2,64,768]{2,1,0:T(8,128)(2,1)S(1)}, bf16[2,64,768]{2,1,0:T(8,128)(2,1)S(1)}, u32[]{:S(2)}, u32[]{:S(2)}) collective-permute-start(bf16[2,64,768]{2,1,0:T(8,128)(2,1)S(1)} %slice.75), channel_id=1, source_target_pairs={{0,32},{1,33},{2,34},{3,35},{4,36},{5,37},{6,38},{7,39},{8,40},{9,... | collective-permute-start | bytes 589832 | tf_op jit(solution)/shard_map/gather_tokens/ppermute | solution.py:678
  47.6 7.4 %copy-start.19 = (bf16[4,64,768]{2,1,0:T(8,128)(2,1)}, bf16[4,64,768]{2,1,0:T(8,128)(2,1)S(1)}, u32[]{:S(2)}) copy-start(bf16[4,64,768]{2,1,0:T(8,128)(2,1)S(1)} %collective-permute-done.4.refs_2_) | copy-start | bytes 1179652
  47.6 7.3 %collective-permute-start.6 = (bf16[2,64,768]{2,1,0:T(8,128)(2,1)S(1)}, bf16[2,64,768]{2,1,0:T(8,128)(2,1)S(1)}, u32[]{:S(2)}, u32[]{:S(2)}) collective-permute-start(bf16[2,64,768]{2,1,0:T(8,128)(2,1)S(1)} %slice.76), channel_id=1, source_target_pairs={{0,96},{1,97},{2,98},{3,99},{4,100},{5,101},{6,102},{7,103},{8,104... | collective-permute-start | bytes 589832 | tf_op jit(solution)/shard_map/gather_tokens/ppermute | solution.py:678
  52.1 2.9 %copy-start.28 = (bf16[2,64,768]{2,1,0:T(8,128)(2,1)}, bf16[2,64,768]{2,1,0:T(8,128)(2,1)S(1)}, u32[]{:S(2)}) copy-start(bf16[2,64,768]{2,1,0:T(8,128)(2,1)S(1)} %collective-permute-done.12.refs_8_) | copy-start | bytes 589828
  52.1 2.9 %copy-start.29 = (bf16[2,64,768]{2,1,0:T(8,128)(2,1)}, bf16[2,64,768]{2,1,0:T(8,128)(2,1)S(1)}, u32[]{:S(2)}) copy-start(bf16[2,64,768]{2,1,0:T(8,128)(2,1)S(1)} %collective-permute-done.13.refs_9_) | copy-start | bytes 589828
  55.0 0.7 copy-start.30
  55.0 0.7 copy-start.31
  67.3 13.2 %all-to-all-start = ((bf16[16,64,128]{2,1,0:T(8,128)(2,1)}), bf16[16,64,128]{2,1,0:T(8,128)(2,1)S(1)}, u32[]{:S(2)}, u32[]{:S(2)}) async-start(bf16[16,64,128]{2,1,0:T(8,128)(2,1)} %get-tuple-element.58), calls=%async_computation | async-start | bytes 524288 | tf_op jit(solution)/shard_map/attention/all_to_all | solution.py:665
  71.8 85.8 %reduce-scatter.2.cloned.1.call-start = ((), (), s32[]{:S(2)}) async-start(), calls=%async_computation.8 | async-start | bytes 11943936 | tf_op jit(solution)/shard_map/feed_forward/reduce_scatter | solution.py:795
  80.5 0.7 copy-start.14
  95.3 1.0 copy-start.15
  121.8 3.9 %copy-start.2 = (bf16[8,96,192]{2,1,0:T(8,128)(2,1)S(1)}, bf16[8,96,192]{2,1,0:T(8,128)(2,1)}, u32[]{:S(2)}) copy-start(bf16[8,96,192]{2,1,0:T(8,128)(2,1)} %copy.53) | copy-start | bytes 884740
  121.8 3.9 %copy-start.3 = (bf16[2048,192]{1,0:T(8,128)(2,1)S(1)}, bf16[2048,192]{1,0:T(8,128)(2,1)}, u32[]{:S(2)}) copy-start(bf16[2048,192]{1,0:T(8,128)(2,1)} %get-tuple-element.69.rows) | copy-start | bytes 2359300
  121.8 3.9 %copy-start.6 = (f32[1,768]{1,0:T(1,128)S(1)}, f32[1,768]{1,0:T(1,128)}, u32[]{:S(2)}) copy-start(f32[1,768]{1,0:T(1,128)} %reshape.105.refs_12_.gain) | copy-start | bytes 9220
  121.8 3.9 %copy-start.7 = (f32[4,768]{1,0:T(4,128)S(1)}, f32[4,768]{1,0:T(4,128)}, u32[]{:S(2)}) copy-start(f32[4,768]{1,0:T(4,128)} %get-tuple-element.71.vector_sums) | copy-start | bytes 36868
  121.8 3.9 %copy-start.8 = (f32[1,3072]{1,0:T(1,128)S(1)}, f32[1,3072]{1,0:T(1,128)}, u32[]{:S(2)}) copy-start(f32[1,3072]{1,0:T(1,128)} %get-tuple-element.72.up_sums) | copy-start | bytes 36868
  121.8 3.9 %copy-start.9 = (f32[1,768]{1,0:T(1,128)S(1)}, f32[1,768]{1,0:T(1,128)}, u32[]{:S(2)}) copy-start(f32[1,768]{1,0:T(1,128)} %reshape.106.refs_13_.shift) | copy-start | bytes 9220
  121.8 3.9 %copy-start.10 = (f32[1,192]{1,0:T(1,128)S(1)}, f32[1,192]{1,0:T(1,128)}, u32[]{:S(2)}) copy-start(f32[1,192]{1,0:T(1,128)} %get-tuple-element.70.bias_sums) | copy-start | bytes 2308
  121.8 19.5 %all-to-all-start.2 = ((bf16[16,64,384]{2,1,0:T(8,128)(2,1)}), bf16[16,64,384]{2,1,0:T(8,128)(2,1)S(1)}, u32[]{:S(2)}, u32[]{:S(2)}) async-start(bf16[16,64,384]{2,1,0:T(8,128)(2,1)} %get-tuple-element.73), calls=%async_computation.2 | async-start | bytes 1572864 | tf_op jit(solution)/shard_map/attention_back/all_to_all | solution.py:665
  125.6 65.7 %all-gather.4.cloned.1.call-start = ((), (), s32[]{:S(2)}) async-start(), calls=%async_computation.7 | async-start | bytes 3981312 | tf_op jit(solution)/shard_map/token_gradient/all_gather | solution.py:829
  125.7 2.0 copy-start.1
  129.0 1.5 collective-permute-start.18
  130.7 6.1 %collective-permute-start.19 = (bf16[104,192]{1,0:T(8,128)(2,1)S(1)}, bf16[104,192]{1,0:T(8,128)(2,1)S(1)}, u32[]{:S(2)}, u32[]{:S(2)}) collective-permute-start(bf16[104,192]{1,0:T(8,128)(2,1)S(1)} %get-tuple-element.103), channel_id=1, source_target_pairs={{0,2},{1,3},{2,4},{3,5},{4,6},{5,7},{6,0},{7,1},{8,10},{9,11},{10,... | collective-permute-start | bytes 119816 | tf_op jit(solution)/shard_map/early_grads/ppermute | solution.py:678
  132.5 5.2 %collective-permute-start.20 = (bf16[104,192]{1,0:T(8,128)(2,1)S(1)}, bf16[104,192]{1,0:T(8,128)(2,1)S(1)}, u32[]{:S(2)}, u32[]{:S(2)}) collective-permute-start(bf16[104,192]{1,0:T(8,128)(2,1)S(1)} %get-tuple-element.102), channel_id=1, source_target_pairs={{0,6},{1,7},{2,0},{3,1},{4,2},{5,3},{6,4},{7,5},{8,14},{9,15},{10,... | collective-permute-start | bytes 119816 | tf_op jit(solution)/shard_map/early_grads/ppermute | solution.py:678
  134.0 6.3 %collective-permute-start.21 = (bf16[104,192]{1,0:T(8,128)(2,1)S(1)}, bf16[104,192]{1,0:T(8,128)(2,1)S(1)}, u32[]{:S(2)}, u32[]{:S(2)}) collective-permute-start(bf16[104,192]{1,0:T(8,128)(2,1)S(1)} %get-tuple-element.101), channel_id=1, source_target_pairs={{0,4},{1,5},{2,6},{3,7},{4,0},{5,1},{6,2},{7,3},{8,12},{9,13},{10,... | collective-permute-start | bytes 119816 | tf_op jit(solution)/shard_map/early_grads/ppermute | solution.py:678
  141.3 20.2 %all-to-all-start.3 = ((bf16[16,32,768]{2,1,0:T(8,128)(2,1)}), bf16[16,32,768]{2,1,0:T(8,128)(2,1)S(1)}, u32[]{:S(2)}, u32[]{:S(2)}) async-start(bf16[16,32,768]{2,1,0:T(8,128)(2,1)} %early_grads.3), calls=%async_computation.4 | async-start | bytes 1572864 | tf_op jit(solution)/shard_map/early_grads/all_to_all | solution.py:665
  187.4 3.9 %copy-start.4 = (bf16[1,128,768]{2,1,0:T(8,128)(2,1)S(1)}, bf16[1,128,768]{2,1,0:T(8,128)(2,1)}, u32[]{:S(2)}) copy-start(bf16[1,128,768]{2,1,0:T(8,128)(2,1)} %param.15) | copy-start | bytes 589828
  187.4 3.9 %copy-start.5 = (f32[128,768]{1,0:T(8,128)S(1)}, f32[128,768]{1,0:T(8,128)}, u32[]{:S(2)}) copy-start(f32[128,768]{1,0:T(8,128)} %get-tuple-element.77.grad_residual) | copy-start | bytes 1179652
  187.4 23.6 %all-to-all-start.5 = ((bf16[16,54,768]{2,1,0:T(8,128)(2,1)}), bf16[16,54,768]{2,1,0:T(8,128)(2,1)S(1)}, u32[]{:S(2)}, u32[]{:S(2)}) async-start(bf16[16,54,768]{2,1,0:T(8,128)(2,1)} %sum_over_ctx.3), calls=%async_computation.6 | async-start | bytes 2752512 | tf_op jit(solution)/shard_map/sum_over_ctx/all_to_all | solution.py:665
  191.3 2.0 copy-start
Sparse Core Ops, SparseCore 0:
  11.8 61.5 all-gather.5
  95.5 62.1 reduce-scatter.1
  159.4 29.1 all-gather.3
